TPU v7x, 32 devices: a whole 2x2x4 slice. The times are simulated.
32 devices in a mesh: req: 8 (over z, y), tensor: 4 (over x, core).
Axes of the slice: x: 2, y: 2, z: 4, core: 2. Of those that a mesh axis runs over, the one named last changes fastest.
Arguments:
- span_in: bfloat16 [16, 512, 2048], P('req'), may hold values from -6 to 6
- w_qkv: bfloat16 [3, 2048, 2048], P(None, None, 'tensor'), may hold values from -1 to 1
- qk_gain: bfloat16 [2, 2048], P(None, 'tensor'), may hold values from 0.099609375 to 1.8984375
- w_out: bfloat16 [2048, 2048], P('tensor'), may hold values from -1 to 1
- post_gain: bfloat16 [2048], P('tensor'), may hold values from 0.099609375 to 1.8984375
- kv_pool: bfloat16 [4, 512, 16, 2048], P(None, 'req', None, 'tensor'), may hold values from -66 to 66
- block_table: int32 [16, 32], replicated, may hold values from 0 to 63, as said below
- request_order: int32 [16], replicated, may hold values from 0 to 15, each once
- lengths: int32 [16], replicated, may hold values from 1 to 512, as said below
Outputs:
- span_out: bfloat16 [16, 512, 2048], P('req', None, 'tensor')
- relaid_cache: bfloat16 [4, 16, 512, 2048], P(None, 'req', None, 'tensor')
Inputs may be any that keep to these rules, and one draw needn't show every extreme that they name: `block_table`: entry (r, j) is the slot, among the 64 slots of the req index j modulo the number of req devices, that holds block j of request r; each slot of each req index is named once. `lengths`: some request has exactly 512 cached tokens.
All inputs are finite; a program needn't handle non-finite values.
Results may differ from a plain program's by a relative error of at most 0.0095.
Values may be sent and summed in bfloat16 or wider, within the bound.
No kernel may reach another device: no remote copies, remote signals or barrier semaphores. Data moves between devices by JAX's collectives and lax.ppermute only.
A program may use at most 192 MiB of HBM per device.

v0:
```python
import jax
import jax.numpy as jnp
from jax import lax
from jax.sharding import PartitionSpec as P

HD = 128


norm_eps = 1e-06
rope_base = 500000.0


def rotate(values, positions):
    half_dim = values.shape[-1] // 2
    frequency = rope_base ** (-jnp.arange(half_dim, dtype=jnp.float32) * (2.0 / values.shape[-1]))
    angles = positions[:, None] * frequency[None, :]
    cosine = jnp.cos(angles)[:, None, :]
    sine_part = jnp.sin(angles)[:, None, :]
    first_half = values[..., :half_dim]
    second_half = values[..., half_dim:]
    return jnp.concatenate(
        [
            first_half * cosine - second_half * sine_part,
            second_half * cosine + first_half * sine_part,
        ],
        axis=-1,
    )


def on_device(
    span_in, w_qkv, qk_gain, w_out, post_gain, kv_pool, block_table, request_order, lengths
):
    req_count = lax.axis_size("req")
    req_index = lax.axis_index("req")
    per_device = span_in.shape[0]
    span_len = span_in.shape[1]
    full_width = span_in.shape[2]
    part_width = w_qkv.shape[2]
    block_len = kv_pool.shape[2]
    blocks_each = block_table.shape[1] // req_count
    wanted = jnp.transpose(request_order.reshape(req_count, per_device))
    table_rows = jnp.take(block_table, wanted, axis=0)
    local_blocks = req_index + req_count * jnp.arange(blocks_each, dtype=jnp.int32)
    picked = jnp.take(table_rows, local_blocks, axis=2)
    picked = jnp.transpose(picked, (0, 2, 1)).reshape(-1)
    gathered = jnp.take(kv_pool, picked, axis=1)
    received = lax.all_to_all(
        gathered.reshape(
            kv_pool.shape[0], per_device, blocks_each, req_count * block_len, part_width
        ),
        "req",
        split_axis=3,
        concat_axis=3,
        tiled=True,
    )
    relaid = received.reshape(kv_pool.shape[0], per_device, -1, part_width)
    my_order = lax.dynamic_slice_in_dim(request_order, req_index * per_device, per_device)
    my_lengths = jnp.take(lengths, my_order)
    flat_in = span_in.reshape(-1, full_width)
    projected = jnp.einsum("rd,mdw->mrw", flat_in, w_qkv, preferred_element_type=jnp.float32)
    queries = projected[0]
    keys_new = projected[1]
    values_new = projected[2].astype(jnp.bfloat16)
    query_sq, key_sq = lax.psum(
        (jnp.sum(queries * queries, axis=-1), jnp.sum(keys_new * keys_new, axis=-1)), "tensor"
    )
    norm_gains = qk_gain.astype(jnp.float32)
    queries = queries * lax.rsqrt(query_sq / full_width + norm_eps)[:, None] * norm_gains[0]
    keys_new = keys_new * lax.rsqrt(key_sq / full_width + norm_eps)[:, None] * norm_gains[1]
    positions = (
        my_lengths.astype(jnp.float32)[:, None] + jnp.arange(span_len, dtype=jnp.float32)[None, :]
    ).reshape(-1)
    local_heads = part_width // HD
    query_rot = rotate(queries.reshape(-1, local_heads, HD), positions).astype(jnp.bfloat16)
    query_rot = query_rot.reshape(per_device, span_len, local_heads, HD)
    key_rot = rotate(keys_new.reshape(-1, local_heads, HD), positions).astype(jnp.bfloat16)
    key_rot = key_rot.reshape(per_device, span_len, local_heads, HD)
    context = relaid.shape[2]
    all_keys = jnp.concatenate(
        [relaid[0].reshape(per_device, context, local_heads, HD), key_rot], axis=1
    )
    all_values = jnp.concatenate(
        [
            relaid[1].reshape(per_device, context, local_heads, HD),
            values_new.reshape(per_device, span_len, local_heads, HD),
        ],
        axis=1,
    )
    scores = jnp.einsum(
        "bqhd,bkhd->bhqk", query_rot, all_keys, preferred_element_type=jnp.float32
    ) * HD ** (-0.5)
    cache_live = jnp.arange(context, dtype=jnp.int32)[None, :] < my_lengths[:, None]
    causal = jnp.arange(span_len)[None, :] <= jnp.arange(span_len)[:, None]
    live_mask = jnp.concatenate(
        [
            jnp.broadcast_to(cache_live[:, None, :], (per_device, span_len, context)),
            jnp.broadcast_to(causal[None], (per_device, span_len, span_len)),
        ],
        axis=2,
    )
    scores = jnp.where(live_mask[:, None], scores, -1e30)
    maxima = jnp.max(scores, axis=-1, keepdims=True)
    exponent = jnp.exp(scores - maxima)
    weights = (exponent / jnp.sum(exponent, axis=-1, keepdims=True)).astype(jnp.bfloat16)
    attended = jnp.einsum(
        "bhqk,bkhd->bqhd", weights, all_values, preferred_element_type=jnp.float32
    )
    attended = attended.astype(jnp.bfloat16).reshape(-1, part_width)
    partial_value = jnp.dot(attended, w_out, preferred_element_type=jnp.float32)
    tensor_index = lax.axis_index("tensor")
    residual_part = lax.dynamic_slice_in_dim(
        flat_in, tensor_index * part_width, part_width, 1
    ).astype(jnp.float32)
    gain_part = post_gain.astype(jnp.float32)
    summed = lax.psum(partial_value.astype(jnp.bfloat16), "tensor").astype(jnp.float32)
    scale_rows = lax.rsqrt(jnp.mean(summed * summed, axis=-1, keepdims=True) + norm_eps)
    own_share = lax.dynamic_slice_in_dim(summed, tensor_index * part_width, part_width, 1)
    layer_out = (residual_part + own_share * scale_rows * gain_part).astype(jnp.bfloat16)
    return (layer_out.reshape(per_device, span_len, part_width), relaid)


def solution(mesh):
    placed = (
        P("req", None, None),
        P(None, None, "tensor"),
        P(None, "tensor"),
        P("tensor", None),
        P("tensor"),
        P(None, "req", None, "tensor"),
        P(),
        P(),
        P(),
    )
    return jax.shard_map(
        on_device,
        mesh=mesh,
        in_specs=placed,
        out_specs=(P("req", None, "tensor"), P(None, "req", None, "tensor")),
        check_vma=False,
    )
```

profile of v0, /device:TPU:0, one launch (start us, length us, event | category | flops | bytes accessed | tf_op | source)
XLA Modules:
  0.0 282.2 jit_solution(17379610644233913870)
XLA Ops:
  7.2 0.9 reshape.255
  8.4 1.3 gather_fusion
  9.8 0.6 gather_fusion.1
  10.7 5.0 %gather_fusion.2 = bf16[64,4,16,512]{3,2,1,0:T(8,128)(2,1)} fusion(bf16[4,64,16,512]{3,2,1,0:T(8,128)(2,1)} %param.14, s32[1024]{0:T(1024)S(1)} %pad_clamp_fusion.1), kind=kCustom, calls=%fused_computation.2 | custom fusion | bytes 8388864 | tf_op jit(solution)/shard_map/jit(_take)/gather | solution.py:46
  15.7 2.6 copy.67
  18.4 0.5 broadcast_select_fusion
  18.9 5.3 %copy.68 = bf16[4,2,4,128,512]{4,2,1,0,3:T(4,128)(2,1)} copy(bf16[4,2,4,128,512]{4,3,2,1,0:T(8,128)(2,1)S(1)} %broadcast_select_fusion) | data formatting | bytes 8388608 | tf_op jit(solution)/shard_map/jit(_take)/select_n | solution.py:46
  24.1 7.4 %all-to-all-start = ((bf16[4,2,4,128,512]{4,2,1,0,3:T(4,128)(2,1)}), bf16[4,2,4,128,512]{4,2,1,0,3:T(4,128)(2,1)}, u32[]{:S(2)}, u32[]{:S(2)}) async-start(bf16[4,2,4,128,512]{4,2,1,0,3:T(4,128)(2,1)} %copy.68), calls=%async_computation | async-start | bytes 8388608 | tf_op jit(solution)/shard_map/all_to_all | solution.py:47
  31.7 0.6 gather_fusion.3
  32.5 10.1 %convolution_bitcast_fusion = f32[3,1024,512]{1,2,0:T(8,128)S(1)} fusion(bf16[3,2048,512]{2,1,0:T(8,128)(2,1)} %param.10, bf16[1024,2048,1]{1,0,2:T(8,128)(2,1)} %bitcast.61), kind=kOutput, calls=%fused_computation.17 | convolution fusion | flops 6442450944 | bytes 16777216 | tf_op jit(solution)/shard_map/rd,mdw->mrw/dot_general | solution.py:60
  42.6 2.6 copy-done.4
  45.2 1.1 slice.77
  46.3 1.8 convert_element_type.42
  48.2 1.1 copy.71
  49.3 5.0 %multiply_reduce_fusion.2 = (f32[1024]{0:T(1024)S(1)}, f32[1024]{0:T(1024)S(1)}, f32[1,1024,512]{1,2,0:T(8,128)}, f32[1,1024,512]{1,2,0:T(8,128)}) fusion(f32[3,1024,512]{1,2,0:T(8,128)} %copy-done.4), kind=kLoop, calls=%fused_computation.32 | loop fusion | flops 2095104 | bytes 8396800 | tf_op jit(solution)/shard_map/reduce_sum | solution.py:65
  54.3 7.0 %all-reduce = (f32[1024]{0:T(1024)S(1)}, f32[1024]{0:T(1024)S(1)}) all-reduce(f32[1024]{0:T(1024)S(1)} %get-tuple-element.3, f32[1024]{0:T(1024)S(1)} %get-tuple-element.2), channel_id=1, replica_groups=mesh['req'=8,'tensor'=4] {'tensor'}, use_global_device_ids=true, to_apply=%region_3.4 | all-reduce | flops 2048 | bytes 16384 | tf_op jit(solution)/shard_map/psum | solution.py:64
  61.4 1.0 multiply_cosine_fusion
  62.4 1.8 multiply_multiply_fusion.1
  64.2 0.2 multiply_multiply_fusion
  64.5 1.9 subtract_convert_fusion.1
  66.4 1.4 concatenate.29
  67.8 1.3 copy.72
  69.2 1.4 concatenate.30
  70.6 1.3 copy.73
  71.9 1.4 concatenate.33
  73.4 1.3 copy.76
  74.7 0.4 concatenate.32
  75.1 1.3 copy.75
  76.9 1.1 pad_add_fusion
  77.9 46.9 %all-to-all-done = bf16[4,2,4,128,512]{4,2,1,0,3:T(4,128)(2,1)} async-done(((bf16[4,2,4,128,512]{4,2,1,0,3:T(4,128)(2,1)}), bf16[4,2,4,128,512]{4,2,1,0,3:T(4,128)(2,1)}, u32[]{:S(2)}, u32[]{:S(2)}) %all-to-all-start) | async-done | bytes 4194336 | tf_op jit(solution)/shard_map/all_to_all | solution.py:47
  124.8 3.6 %fusion.33 = (bf16[1,2,4,128,512]{4,2,1,0,3:T(4,128)(2,1)}, bf16[1,2,4,128,512]{4,2,1,0,3:T(4,128)(2,1)}) fusion(bf16[4,2,4,128,512]{4,2,1,0,3:T(4,128)(2,1)} %all-to-all-done), kind=kLoop, calls=%fused_computation.76 | loop fusion | bytes 4194304 | tf_op jit(solution)/shard_map/slice | solution.py:84
  128.4 2.7 copy.69
  131.2 1.2 reshape_squeeze.6
  132.4 1.5 copy.74
  133.9 1.1 reshape_squeeze.7
  135.0 1.4 copy.77
  136.4 10.3 %fusion.9 = f32[2,4,512,1024]{3,2,1,0:T(8,128)} fusion(bf16[2,512,4,64]{3,1,2,0:T(8,128)(2,1)} %copy.76, bf16[2,512,4,64]{3,1,2,0:T(8,128)(2,1)} %copy.75, bf16[2,512,4,128]{3,1,2,0:T(8,128)(2,1)S(1)} %copy.77, bf16[2,512,4,64]{3,1,2,0:T(8,128)(2,1)} %copy.73, bf16[2,512,4,64]{3,1,2,0:T(8,128)(2,1)} %copy.72), kind=kOutput, calls=%fused_computation.22 | convolution fusion | flops 1082130432 | bytes 19922944 | tf_op jit(solution)/shard_map/bqhd,bkhd->bhqk/dot_general | solution.py:89
  146.7 22.0 %fusion.35 = (f32[2,4,512]{2,1,0:T(4,128)S(1)}, f32[2,4,512,1024]{3,2,1,0:T(8,128)}) fusion(f32[2,4,512,1024]{3,2,1,0:T(8,128)} %fusion.9, pred[2,512,1024]{2,1,0:T(8,128)(4,1)} %pad_add_fusion), kind=kOutput, calls=%fused_computation.78 | output fusion | flops 25166848 | bytes 34619392 | tf_op jit(solution)/shard_map/sub | solution.py:103
  168.8 8.7 %fusion.18 = bf16[2,512,4,128]{1,3,2,0:T(8,128)(2,1)} fusion(f32[2,4,512,1024]{3,2,1,0:T(8,128)} %get-tuple-element.25, f32[2,4,512]{2,1,0:T(4,128)S(1)} %get-tuple-element.24, bf16[2,512,4,128]{1,3,2,0:T(8,128)(2,1)S(1)} %copy-done.5, bf16[2,512,4,128]{1,3,2,0:T(8,128)(2,1)} %reshape_squeeze.6), kind=kOutput, calls=%fused_computation.34 | convolution fusion | flops 1086849024 | bytes 19939328 | tf_op jit(solution)/shard_map/bhqk,bkhd->bqhd/dot_general | solution.py:105
  177.5 1.7 copy.78
  179.2 4.3 %convolution_convert_fusion = bf16[1024,2048]{1,0:T(8,128)(2,1)} fusion(bf16[512,2048]{1,0:T(8,128)(2,1)S(1)} %copy-done, bf16[128,8,4,128]{3,2,1,0:T(4,128)(2,1)S(1)} %bitcast.60), kind=kOutput, calls=%fused_computation.16 | convolution fusion | flops 2149580800 | bytes 7340032 | tf_op jit(solution)/shard_map/dot_general | solution.py:109
  183.6 0.6 copy-done.8
  184.2 6.5 %copy.79 = bf16[4,2,4,128,512]{4,3,2,1,0:T(8,128)(2,1)} copy(bf16[4,2,4,128,512]{4,2,1,0,3:T(4,128)(2,1)} %all-to-all-done) | data formatting | bytes 8388608 | tf_op jit(solution)/shard_map/all_to_all | solution.py:47
  190.8 77.5 %all-reduce.3.cloned.1.call-done = bf16[1024,2048]{1,0:T(8,128)(2,1)} async-done(((bf16[1024,2048]{1,0:T(8,128)(2,1)}), bf16[1024,2048]{1,0:T(8,128)(2,1)}) %all-reduce.3.cloned.1.call-update) | async-done | bytes 4194320 | tf_op jit(solution)/shard_map/psum | solution.py:115
  268.2 3.2 %multiply_reduce_fusion = f32[1024]{0:T(1024)S(1)} fusion(bf16[1024,2048]{1,0:T(8,128)(2,1)} %all-reduce.3.cloned.1.call-done), kind=kLoop, calls=%fused_computation.9 | loop fusion | flops 6290432 | bytes 4198400 | tf_op jit(solution)/shard_map/reduce_sum | solution.py:116
  271.5 0.2 copy-done.2
  271.7 1.1 convert_element_type.49
  272.8 2.6 add_convert_fusion
  (50 shorter events, 1.6 us)
Async XLA Ops:
  7.2 172.1 %copy-start = (bf16[512,2048]{1,0:T(8,128)(2,1)S(1)}, bf16[512,2048]{1,0:T(8,128)(2,1)}, u32[]{:S(2)}) copy-start(bf16[512,2048]{1,0:T(8,128)(2,1)} %param.12) | copy-start | bytes 6291460
  24.1 7.5 %copy-start.7 = (s32[16]{0:T(128)S(1)}, s32[16]{0:T(128)}, u32[]{:S(2)}) copy-start(s32[16]{0:T(128)} %param.16) | copy-start | bytes 196
  24.1 7.6 %copy-start.1 = (s32[16]{0:T(128)S(1)}, s32[16]{0:T(128)}, u32[]{:S(2)}) copy-start(s32[16]{0:T(128)} %param.17) | copy-start | bytes 196
  24.1 100.7 %all-to-all-start = ((bf16[4,2,4,128,512]{4,2,1,0,3:T(4,128)(2,1)}), bf16[4,2,4,128,512]{4,2,1,0,3:T(4,128)(2,1)}, u32[]{:S(2)}, u32[]{:S(2)}) async-start(bf16[4,2,4,128,512]{4,2,1,0,3:T(4,128)(2,1)} %copy.68), calls=%async_computation | async-start | bytes 8388608 | tf_op jit(solution)/shard_map/all_to_all | solution.py:47
  31.5 236.7 %all-reduce.3.cloned.1.call-start = ((), (), s32[]{:S(2)}) async-start(), calls=%async_computation.1 | async-start | bytes 8388608 | tf_op jit(solution)/shard_map/psum | solution.py:115
  42.6 2.6 copy-start.4
  49.3 12.0 %copy-start.6 = (bf16[2,512]{1,0:T(2,128)(2,1)S(1)}, bf16[2,512]{1,0:T(2,128)(2,1)}, u32[]{:S(2)}) copy-start(bf16[2,512]{1,0:T(2,128)(2,1)} %param.11) | copy-start | bytes 6148
  61.3 2.9 %copy-start.3 = (f32[1,1024,512]{1,2,0:T(8,128)S(1)}, f32[1,1024,512]{1,2,0:T(8,128)}, u32[]{:S(2)}) copy-start(f32[1,1024,512]{1,2,0:T(8,128)} %get-tuple-element.11) | copy-start | bytes 6291460
  146.7 22.1 %copy-start.5 = (bf16[2,512,4,128]{1,3,2,0:T(8,128)(2,1)S(1)}, bf16[2,512,4,128]{1,3,2,0:T(8,128)(2,1)}, u32[]{:S(2)}) copy-start(bf16[2,512,4,128]{1,3,2,0:T(8,128)(2,1)} %copy.71) | copy-start | bytes 3145732
  183.5 0.7 copy-start.8
  268.2 3.4 %copy-start.2 = (bf16[1024,2048]{1,0:T(8,128)(2,1)S(1)}, bf16[1024,2048]{1,0:T(8,128)(2,1)}, u32[]{:S(2)}) copy-start(bf16[1024,2048]{1,0:T(8,128)(2,1)} %all-reduce.3.cloned.1.call-done) | copy-start | bytes 12582916
Sparse Core Ops, SparseCore 0:
  183.7 84.5 all-reduce.2
where the time goes:
time: 283 us; the launch traced here: 282 us
  waiting for transfers between devices  124 us (44%)
  local copies, waits for them, and re-layouts  54.6 us (19%)
  other arithmetic  41.1 us (15%)
  matrix products  33.4 us (12%)
  between operations  14.3 us (5%)
  starting transfers between devices  7.45 us (3%)
  blocking collectives  6.97 us (2%)
    psum x1, waiting for transfers between devices, on_device(): lax.psum(partial_value.astype(jnp.bfloat16), 'tensor').astype(jnp.float32)  77.5 us
    all_to_all x1, waiting for transfers between devices, on_device(): lax.all_to_all(gathered.reshape(kv_pool.shape[0], per_device, blocks_each...  46.9 us
    sub x1, other arithmetic, on_device(): exponent = jnp.exp(scores - maxima)  22 us
    dot_general x1, matrix products, on_device(): jnp.einsum('bqhd,bkhd->bhqk', query_rot, all_keys, preferred_element_type...  10.3 us
    dot_general x1, matrix products, on_device(): jnp.einsum('rd,mdw->mrw', flat_in, w_qkv, preferred_element_type=jnp.floa...  10.1 us
    concatenate x8, local copies, waits for them, and re-layouts, rotate(): jnp.concatenate([first_half * cosine - second_half * sine_part, second_ha...  10 us
    dot_general x1, matrix products, on_device(): jnp.einsum('bhqk,bkhd->bqhd', weights, all_values, preferred_element_type...  8.74 us
    gather x2, local copies, waits for them, and re-layouts, on_device(): gathered = jnp.take(kv_pool, picked, axis=1)  7.65 us
  transfers between devices with their start and end apart: 2, of which 2 were waited for; matrix products, arithmetic and copies ran while one was open for 15% of the time, Pallas kernels for 0%

commit v1 on v0

v1 whole, which is shorter than its diff:
```python
import functools
import math

import jax
import jax.numpy as jnp
from jax import lax
from jax.experimental import pallas as pl
from jax.experimental.pallas import tpu as pltpu
from jax.sharding import PartitionSpec as P

HD = 128
norm_eps = 1e-06
rope_base = 500000.0

ANY = pl.BlockSpec(memory_space=pl.ANY)
SMEM = pl.BlockSpec(memory_space=pltpu.SMEM)
VMEM_LIMIT = 48 * 1024 * 1024


def cost(flops, moved, exps=0):
    return pl.CostEstimate(flops=flops, bytes_accessed=moved, transcendentals=exps)


def params():
    return pltpu.CompilerParams(vmem_limit_bytes=VMEM_LIMIT)


def gather_body(offsets, first, planes, count, per_device, blocks, together, table, order, pool, *rest):
    outs, sems = rest[:-1], rest[-1]
    if together:
        outs = outs[-1:]
    else:
        outs = outs[-len(offsets) :]
    me = lax.axis_index("req")
    for at, offset in enumerate(offsets):
        target = offset if together else me ^ offset
        for p in range(per_device):
            request = order[target * per_device + p]
            for b in range(blocks):
                slot = table[request, b * count + me]
                place = outs[0].at[at, :, p, b] if together else outs[at].at[:, p, b]
                pltpu.make_async_copy(
                    pool.at[pl.ds(first, planes), slot], place, sems.at[0 if together else at]
                ).start()
    for at, out in enumerate(outs):
        pltpu.make_async_copy(out, out, sems.at[at]).wait()


def gather(pool, table, order, count, offsets, first, planes, together, after=()):
    per_device = order.shape[0] // count
    blocks = table.shape[1] // count
    piece = (planes, per_device, blocks) + pool.shape[2:]
    if together:
        shapes = [jax.ShapeDtypeStruct((len(offsets),) + piece, pool.dtype)]
    else:
        shapes = [jax.ShapeDtypeStruct(piece, pool.dtype) for _ in offsets]
    moved = 4 * len(offsets) * math.prod(piece)
    return pl.pallas_call(
        functools.partial(gather_body, offsets, first, planes, count, per_device, blocks, together),
        in_specs=[SMEM, SMEM, ANY] + [ANY] * len(after),
        out_specs=[ANY] * len(shapes),
        out_shape=shapes,
        scratch_shapes=[pltpu.SemaphoreType.DMA((len(shapes),))],
        cost_estimate=cost(0, moved),
        compiler_params=params(),
        name="gather_blocks",
    )(table, order, pool, *after)


def place_body(offsets, first, planes, count, per_device, blocks, together, filled, table, order, pool, *rest):
    sems, out = rest[-1], rest[-2]
    received = rest[1:] if filled else rest
    me = lax.axis_index("req")
    for p in range(per_device):
        request = order[me * per_device + p]
        for b in range(blocks):
            slot = table[request, b * count + me]
            pltpu.make_async_copy(
                pool.at[pl.ds(first, planes), slot],
                out.at[pl.ds(first, planes), p, b, me],
                sems.at[0],
            ).start()
    copies = []
    for at, offset in enumerate(offsets):
        source = me ^ offset
        piece = received[0].at[source] if together else received[at]
        copy = pltpu.make_async_copy(
            piece, out.at[pl.ds(first, planes), :, :, source], sems.at[1 + at]
        )
        copy.start()
        copies.append(copy)
    own = out.at[pl.ds(first, planes), :, :, me]
    pltpu.make_async_copy(own, own, sems.at[0]).wait()
    for copy in copies:
        copy.wait()


def place(pool, table, order, count, offsets, first, planes, together, received, filled=None):
    per_device = order.shape[0] // count
    blocks = table.shape[1] // count
    shape = (pool.shape[0], per_device, blocks, count) + pool.shape[2:]
    start = [] if filled is None else [filled]
    return pl.pallas_call(
        functools.partial(
            place_body, offsets, first, planes, count, per_device, blocks, together, filled is not None
        ),
        in_specs=[SMEM, SMEM, ANY] + [ANY] * (len(start) + len(received)),
        out_specs=ANY,
        out_shape=jax.ShapeDtypeStruct(shape, pool.dtype),
        scratch_shapes=[pltpu.SemaphoreType.DMA((1 + len(offsets),))],
        input_output_aliases={} if filled is None else {3: 0},
        cost_estimate=cost(0, 4 * math.prod(shape) * planes // pool.shape[0]),
        compiler_params=params(),
        name="place_blocks",
    )(table, order, pool, *start, *received)


def turned(values, cosine, sine):
    heads = []
    for head in range(values.shape[1] // HD):
        part = values[:, head * HD : (head + 1) * HD]
        swapped = jnp.concatenate([part[:, HD // 2 :], part[:, : HD // 2]], axis=1)
        heads.append(part * cosine + swapped * sine)
    return jnp.concatenate(heads, axis=1)


def project_body(x, w, gain, cosine, sine, q_out, k_out, v_out, squares):
    rows = x[...]
    for which, out in ((0, q_out), (1, k_out)):
        raw = jnp.dot(rows, w[which], preferred_element_type=jnp.float32)
        squares[:, which : which + 1] = jnp.sum(raw * raw, axis=1, keepdims=True)
        out[...] = turned(raw * gain[which : which + 1].astype(jnp.float32), cosine[...], sine[...])
    v_out[...] = jnp.dot(rows, w[2], preferred_element_type=jnp.float32).astype(v_out.dtype)


def project(x, w, gain, cosine, sine, block=256):
    rows, depth = x.shape
    width = w.shape[2]
    by_row = lambda i: (i, 0)
    return pl.pallas_call(
        project_body,
        grid=(rows // block,),
        in_specs=[
            pl.BlockSpec((block, depth), by_row),
            pl.BlockSpec((3, depth, width), lambda i: (0, 0, 0)),
            pl.BlockSpec((2, width), lambda i: (0, 0)),
            pl.BlockSpec((block, HD), by_row),
            pl.BlockSpec((block, HD), by_row),
        ],
        out_specs=[
            pl.BlockSpec((block, width), by_row),
            pl.BlockSpec((block, width), by_row),
            pl.BlockSpec((block, width), by_row),
            pl.BlockSpec((block, 2), by_row),
        ],
        out_shape=[
            jax.ShapeDtypeStruct((rows, width), jnp.float32),
            jax.ShapeDtypeStruct((rows, width), jnp.float32),
            jax.ShapeDtypeStruct((rows, width), jnp.bfloat16),
            jax.ShapeDtypeStruct((rows, 2), jnp.float32),
        ],
        cost_estimate=cost(6 * rows * depth * width, 2 * (rows * depth + 3 * depth * width + 5 * rows * width)),
        compiler_params=params(),
        name="project_qkv",
    )(x, w, gain, cosine, sine)


def attend_body(which, full_width, q_block, lengths, q, k, v, squares, cache_k, cache_v, out):
    span = q.shape[0]
    context = cache_k.shape[0]
    scales = lax.rsqrt(squares[...] / full_width + norm_eps)
    queries = (q[...] * (scales[:, 0:1] * (HD**-0.5 * math.log2(math.e)))).astype(jnp.bfloat16)
    keys = (k[...] * scales[:, 1:2]).astype(jnp.bfloat16)
    contract = (((1,), (1,)), ((), ()))
    live = lax.broadcasted_iota(jnp.int32, (1, context), 1) < lengths[which]
    for low in range(0, span, q_block):
        high = low + q_block
        part = queries[low:high]
        old = lax.dot_general(part, cache_k[...], contract, preferred_element_type=jnp.float32)
        new = lax.dot_general(part, keys[:high], contract, preferred_element_type=jnp.float32)
        old = jnp.where(live, old, -1e30)
        row = lax.broadcasted_iota(jnp.int32, (q_block, high), 0) + low
        column = lax.broadcasted_iota(jnp.int32, (q_block, high), 1)
        new = jnp.where(column <= row, new, -1e30)
        top = jnp.maximum(
            jnp.max(old, axis=1, keepdims=True), jnp.max(new, axis=1, keepdims=True)
        )
        old = jnp.exp2(old - top)
        new = jnp.exp2(new - top)
        total = jnp.sum(old, axis=1, keepdims=True) + jnp.sum(new, axis=1, keepdims=True)
        mixed = jnp.dot(old.astype(jnp.bfloat16), cache_v[...], preferred_element_type=jnp.float32)
        mixed += jnp.dot(new.astype(jnp.bfloat16), v[:high], preferred_element_type=jnp.float32)
        out[low:high] = (mixed / total).astype(out.dtype)


def attend(which, full_width, span, lengths, q, k, v, squares, cache, q_block=256):
    width = q.shape[1]
    context = cache.shape[2]
    q_block = min(q_block, span)
    head_rows = lambda h: (which, h)
    return pl.pallas_call(
        functools.partial(attend_body, which, full_width, q_block),
        grid=(width // HD,),
        in_specs=[
            SMEM,
            pl.BlockSpec((span, HD), head_rows),
            pl.BlockSpec((span, HD), head_rows),
            pl.BlockSpec((span, HD), head_rows),
            pl.BlockSpec((span, 2), lambda h: (which, 0)),
            pl.BlockSpec((None, None, context, HD), lambda h: (0, which, 0, h)),
            pl.BlockSpec((None, None, context, HD), lambda h: (1, which, 0, h)),
        ],
        out_specs=pl.BlockSpec((span, HD), lambda h: (0, h)),
        out_shape=jax.ShapeDtypeStruct((span, width), jnp.bfloat16),
        cost_estimate=cost(
            4 * span * (span + context) * width,
            span * width * 12 + context * width * 4,
            span * (span + context) * width // HD,
        ),
        compiler_params=params(),
        name="attend",
    )(lengths, q, k, v, squares, cache, cache)


def mix_body(count, *refs):
    parts, w, out, squares = refs[:count], refs[count], refs[count + 1], refs[count + 2]
    me = lax.axis_index("tensor")
    total = jnp.dot(parts[0][...], w[me], preferred_element_type=jnp.float32)
    for at in range(1, count):
        total += jnp.dot(parts[at][...], w[me ^ at], preferred_element_type=jnp.float32)
    out[...] = total
    squares[...] = jnp.sum(total * total, axis=1, keepdims=True)


def mix(parts, w, block=256):
    rows, depth = parts[0].shape
    width = w.shape[2]
    count = len(parts)
    block = min(block, rows)
    return pl.pallas_call(
        functools.partial(mix_body, count),
        grid=(rows // block,),
        in_specs=[pl.BlockSpec((block, depth), lambda i: (i, 0))] * count
        + [pl.BlockSpec((count, depth, width), lambda i: (0, 0, 0))],
        out_specs=[
            pl.BlockSpec((block, width), lambda i: (i, 0)),
            pl.BlockSpec((block, 1), lambda i: (i, 0)),
        ],
        out_shape=[
            jax.ShapeDtypeStruct((rows, width), jnp.float32),
            jax.ShapeDtypeStruct((rows, 1), jnp.float32),
        ],
        cost_estimate=cost(
            2 * rows * depth * width * count,
            2 * count * (rows * depth + depth * width) + 4 * rows * width,
        ),
        compiler_params=params(),
        name="mix_heads",
    )(*parts, w)


def permuted(value, axis, offset):
    size = lax.axis_size(axis)
    return lax.ppermute(value, axis, [(i, i ^ offset) for i in range(size)])


def on_device(
    span_in, w_qkv, qk_gain, w_out, post_gain, kv_pool, block_table, request_order, lengths
):
    req_count = lax.axis_size("req")
    tensor_count = lax.axis_size("tensor")
    req_index = lax.axis_index("req")
    tensor_index = lax.axis_index("tensor")
    per_device, span_len, full_width = span_in.shape
    part_width = w_qkv.shape[2]
    planes = kv_pool.shape[0]
    hand = functools.partial(gather, kv_pool, block_table, request_order, req_count)
    put = functools.partial(place, kv_pool, block_table, request_order, req_count)

    offsets = sorted(range(1, req_count), key=lambda s: (s & (req_count // 2 - 1), -s))
    sent = hand(offsets, 0, 2, False)
    received = [permuted(piece, "req", s) for piece, s in zip(sent, offsets)]

    w_split = jnp.transpose(w_out.reshape(part_width, tensor_count, -1), (1, 0, 2))
    w_mix = lax.all_to_all(w_split, "tensor", 0, 0)

    my_order = lax.dynamic_slice_in_dim(request_order, req_index * per_device, per_device)
    my_lengths = jnp.take(lengths, my_order, mode="clip")
    positions = (
        my_lengths.astype(jnp.float32)[:, None] + jnp.arange(span_len, dtype=jnp.float32)[None, :]
    ).reshape(-1)
    frequency = rope_base ** (-jnp.arange(HD // 2, dtype=jnp.float32) * (2.0 / HD))
    angles = positions[:, None] * frequency[None, :]
    cosine, sine = jnp.cos(angles), jnp.sin(angles)
    cosine = jnp.concatenate([cosine, cosine], axis=1)
    sine = jnp.concatenate([-sine, sine], axis=1)
    flat_in = span_in.reshape(-1, full_width)
    q_raw, k_raw, values, squares = project(flat_in, w_qkv, qk_gain, cosine, sine)
    squares = lax.psum(squares, "tensor")

    rest = planes - 2
    everyone = list(range(req_count))
    (sent_rest,) = hand(everyone, 2, rest, True, after=(q_raw,))
    received_rest = lax.all_to_all(sent_rest, "req", 0, 0)

    relaid = put(offsets, 0, 2, False, received)
    cache = relaid.reshape(planes, per_device, -1, part_width)
    outs, sums = [], []
    for p in range(per_device):
        attended = attend(
            p, full_width, span_len, my_lengths, q_raw, k_raw, values, squares, cache
        )
        parts = {0: attended}
        bit = tensor_count // 2
        while bit:
            for at in list(parts):
                parts[at ^ bit] = permuted(parts[at], "tensor", bit)
            bit //= 2
        out, total = mix([parts[at] for at in range(tensor_count)], w_mix)
        outs.append(out)
        sums.append(total)
    projected = jnp.concatenate(outs, axis=0)
    total = jnp.concatenate(sums, axis=0)
    row_sums = total
    for at in range(1, tensor_count):
        row_sums = row_sums + permuted(total, "tensor", at)
    scale_rows = lax.rsqrt(row_sums / full_width + norm_eps)
    residual = lax.dynamic_slice_in_dim(flat_in, tensor_index * part_width, part_width, 1)
    layer_out = (
        residual.astype(jnp.float32) + projected * scale_rows * post_gain.astype(jnp.float32)
    ).astype(jnp.bfloat16)

    relaid = put(offsets, 2, rest, True, [received_rest], filled=relaid)
    return (
        layer_out.reshape(per_device, span_len, part_width),
        relaid.reshape(planes, per_device, -1, part_width),
    )


def solution(mesh):
    placed = (
        P("req", None, None),
        P(None, None, "tensor"),
        P(None, "tensor"),
        P("tensor", None),
        P("tensor"),
        P(None, "req", None, "tensor"),
        P(),
        P(),
        P(),
    )
    return jax.shard_map(
        on_device,
        mesh=mesh,
        in_specs=placed,
        out_specs=(P("req", None, "tensor"), P(None, "req", None, "tensor")),
        check_vma=False,
    )
```

time: 283 us -> 299 us (1.057)
  Pallas kernels: 0 us -> 139 us
  local copies, waits for them, and re-layouts: 54.6 us -> 17.9 us
  other arithmetic: 41.1 us -> 5.58 us
  matrix products: 33.4 us -> 0 us
  waiting for transfers between devices: 124 us -> 94.2 us
  starting transfers between devices: 7.45 us -> 25.1 us
  between operations: 14.3 us -> 0.9 us
  blocking collectives: 6.97 us -> 16.1 us
    pallas_call x0 -> x9, Pallas kernels: none -> 139 us  [the longest x2 107 us: place(): pl.pallas_call(functools.partial(place_body, offsets, first, planes, coun...]
    ppermute x0 -> x16, waiting for transfers between devices: none -> 88.9 us  [permuted(): return lax.ppermute(value, axis, [(i, i ^ offset) for i in range(size)])]
    psum x1 -> x0, waiting for transfers between devices: 77.5 us -> none  [on_device(): lax.psum(partial_value.astype(jnp.bfloat16), 'tensor').astype(jnp.float32)]
    all_to_all x1 -> x2, waiting for transfers between devices: 46.9 us -> 5.29 us  [the longest x1 5.29 us: on_device(): w_mix = lax.all_to_all(w_split, 'tensor', 0, 0)]
    dot_general x4 -> x0, matrix products: 33.4 us -> none  [the longest x1 10.3 us: on_device(): jnp.einsum('bqhd,bkhd->bhqk', query_rot, all_keys, preferred_element_type...]
    sub x1 -> x0, other arithmetic: 22 us -> none  [on_device(): exponent = jnp.exp(scores - maxima)]
    ppermute x0 -> x16, starting transfers between devices: none -> 14.1 us  [permuted(): return lax.ppermute(value, axis, [(i, i ^ offset) for i in range(size)])]
    unnamed x19 -> x34, local copies, waits for them, and re-layouts: 3.53 us -> 14.6 us
  transfers between devices with their start and end apart: 2 -> 18, of which waited for: 2 -> 7; matrix products, arithmetic and copies ran while one was open for 15% -> 2% of each run, Pallas kernels for 0% -> 25%
where the time goes in v1:
time: 299 us
  Pallas kernels  139 us (46%)
  waiting for transfers between devices  94.2 us (32%)
  starting transfers between devices  25.1 us (8%)
  local copies, waits for them, and re-layouts  17.9 us (6%)
  blocking collectives  16.1 us (5%)
  other arithmetic  5.58 us (2%)
    pallas_call x2, Pallas kernels, place(): pl.pallas_call(functools.partial(place_body, offsets, first, planes, coun...  107 us
    ppermute x16, waiting for transfers between devices, permuted(): return lax.ppermute(value, axis, [(i, i ^ offset) for i in range(size)])  88.9 us
    psum x1, blocking collectives, on_device(): squares = lax.psum(squares, 'tensor')  16.1 us
    unnamed x34, local copies, waits for them, and re-layouts  14.6 us
    ppermute x16, starting transfers between devices, permuted(): return lax.ppermute(value, axis, [(i, i ^ offset) for i in range(size)])  14.1 us
    pallas_call x2, Pallas kernels, attend(): pl.pallas_call(functools.partial(attend_body, which, full_width, q_block)...  11.9 us
    pallas_call x1, Pallas kernels, project(): pl.pallas_call(project_body, grid=(rows // block,), in_specs=[pl.BlockSpe...  11.4 us
    all_to_all x1, starting transfers between devices, on_device(): received_rest = lax.all_to_all(sent_rest, 'req', 0, 0)  6.65 us
  transfers between devices with their start and end apart: 18, of which 7 were waited for; matrix products, arithmetic and copies ran while one was open for 2% of the time, Pallas kernels for 25%

profile of v1, /device:TPU:0, one launch (start us, length us, event | category | flops | bytes accessed | tf_op | source)
XLA Modules:
  0.0 298.7 jit_solution(17368810467799961197)
XLA Ops:
  0.6 2.9 copy.14
  3.5 2.4 copy.15
  5.9 4.3 %all-to-all-start = ((bf16[4,512,512]{2,1,0:T(8,128)(2,1)}), bf16[4,512,512]{2,1,0:T(8,128)(2,1)S(1)}, u32[]{:S(2)}, u32[]{:S(2)}) async-start(bf16[4,512,512]{2,1,0:T(8,128)(2,1)} %bitcast.15), calls=%async_computation | async-start | bytes 4194304 | tf_op jit(solution)/shard_map/all_to_all | solution.py:285
  10.2 0.1 dynamic_slice.7
  10.3 0.6 gather_fusion
  11.0 0.1 add_bitcast_fusion
  11.1 1.9 fusion.3
  13.0 0.3 pad_maximum_fusion
  13.3 11.4 %project_qkv.1 = (f32[1024,512]{1,0:T(8,128)S(1)}, f32[1024,512]{1,0:T(8,128)}, bf16[1024,512]{1,0:T(8,128)(2,1)S(1)}, f32[1024,2]{1,0:T(8,128)S(1)}) custom-call(bf16[1024,2048]{1,0:T(8,128)(2,1)} %bitcast.18, bf16[3,2048,512]{2,1,0:T(8,128)(2,1)} %w.1, bf16[2,512]{1,0:T(2,128)(2,1)S(1)} %copy-done.14, f32[1024,128]{1,0:T(8,128)S(1)} %get-tuple-element.35.cosine, ...), custom_call_target="tpu_custom_call" | custom-call | flops 6442450944 | bytes 15728640 | tf_op jit(solution)/shard_map/project_qkv/pallas_call | solution.py:140
  24.7 1.0 copy-done.6
  25.7 2.2 gather_blocks.3
  27.9 1.4 copy-done.3
  29.3 1.3 copy-done.5
  30.6 5.3 %all-to-all-done.refs_4_ = bf16[4,512,512]{2,1,0:T(8,128)(2,1)S(1)} async-done(((bf16[4,512,512]{2,1,0:T(8,128)(2,1)}), bf16[4,512,512]{2,1,0:T(8,128)(2,1)S(1)}, u32[]{:S(2)}, u32[]{:S(2)}) %all-to-all-start) | async-done | bytes 2097184 | tf_op jit(solution)/shard_map/all_to_all | solution.py:285
  35.9 6.7 %all-to-all-start.1 = ((bf16[8,2,2,4,16,512]{5,4,3,2,1,0:T(8,128)(2,1)}), bf16[8,2,2,4,16,512]{5,4,3,2,1,0:T(8,128)(2,1)}, u32[]{:S(2)}, u32[]{:S(2)}) async-start(bf16[8,2,2,4,16,512]{5,4,3,2,1,0:T(8,128)(2,1)} %copy-done.5), calls=%async_computation.1 | async-start | bytes 4194304 | tf_op jit(solution)/shard_map/all_to_all | solution.py:304
  42.6 2.2 copy-done.1
  44.8 2.2 gather_blocks.2
  47.0 3.0 collective-permute-start
  50.0 1.5 collective-permute-start.1
  51.4 0.1 collective-permute-start.2
  51.5 3.7 %collective-permute-start.3 = (bf16[2,2,4,16,512]{4,3,2,1,0:T(8,128)(2,1)}, bf16[2,2,4,16,512]{4,3,2,1,0:T(8,128)(2,1)}, u32[]{:S(2)}, u32[]{:S(2)}) collective-permute-start(bf16[2,2,4,16,512]{4,3,2,1,0:T(8,128)(2,1)} %get-tuple-element.24), channel_id=1, source_target_pairs={{0,24},{4,28},{8,16},{12,20},{16,8},{20,12},{24,0},{28,4},{1,25},{... | collective-permute-start | bytes 786440 | tf_op jit(solution)/shard_map/ppermute | solution.py:264
  55.3 59.4 %collective-permute-done.rest_0_ = bf16[2,2,4,16,512]{4,3,2,1,0:T(8,128)(2,1)S(1)} collective-permute-done((bf16[2,2,4,16,512]{4,3,2,1,0:T(8,128)(2,1)S(1)}, bf16[2,2,4,16,512]{4,3,2,1,0:T(8,128)(2,1)S(1)}, u32[]{:S(2)}, u32[]{:S(2)}) %collective-permute-start) | collective-permute-done | bytes 262176 | tf_op jit(solution)/shard_map/ppermute | solution.py:264
  114.7 0.9 collective-permute-start.5
  115.6 10.7 %collective-permute-done.1.rest_1_ = bf16[2,2,4,16,512]{4,3,2,1,0:T(8,128)(2,1)S(1)} collective-permute-done((bf16[2,2,4,16,512]{4,3,2,1,0:T(8,128)(2,1)S(1)}, bf16[2,2,4,16,512]{4,3,2,1,0:T(8,128)(2,1)S(1)}, u32[]{:S(2)}, u32[]{:S(2)}) %collective-permute-start.1) | collective-permute-done | bytes 262176 | tf_op jit(solution)/shard_map/ppermute | solution.py:264
  126.3 0.7 copy-done.10
  127.0 16.1 %psum.7.squares = f32[1024,2]{1,0:T(8,128)S(1)} all-reduce(f32[1024,2]{1,0:T(8,128)S(1)} %get-tuple-element.20), channel_id=1, replica_groups=mesh['req'=8,'tensor'=4] {'tensor'}, use_global_device_ids=true, to_apply=%region_0.1 | all-reduce | flops 2048 | bytes 16384 | tf_op jit(solution)/shard_map/psum | solution.py:299
  143.2 2.2 copy-done.2
  145.4 0.9 copy-done.11
  146.3 41.6 %place_blocks.2.rest_0_ = bf16[4,2,4,8,16,512]{5,4,3,2,1,0:T(8,128)(2,1)} custom-call(s32[16,32]{1,0:T(8,128)S(1)} %copy-done.12, s32[16]{0:T(128)S(1)} %copy-done.13, bf16[4,64,16,512]{3,2,1,0:T(8,128)(2,1)S(1)} %copy-done.2, bf16[2,2,4,16,512]{4,3,2,1,0:T(8,128)(2,1)S(1)} %collective-permute-done.rest_0_, bf16[2,2,4,16,512]{4,3,2,1,0:T(8,128)(2,1)S(1)} %copy-done.11, ...), custom_call_target="tpu_custom_call" | custom-call | bytes 4194304 | tf_op jit(solution)/shard_map/place_blocks/pallas_call | solution.py:103
  187.9 5.9 %attend.2.refs_0_ = bf16[512,512]{1,0:T(8,128)(2,1)S(1)} custom-call(s32[2]{0:T(128)S(1)} %gather_fusion, f32[1024,512]{1,0:T(8,128)S(1)} %copy-done.4, f32[1024,512]{1,0:T(8,128)} %get-tuple-element.18.k, bf16[1024,512]{1,0:T(8,128)(2,1)S(1)} %copy-done.7, f32[1024,2]{1,0:T(8,128)S(1)} %psum.7.squares, bf16[4,2,512,512]{3,2,1,0:T(8,128)(2,1)} %bitcast.10, ...), custom_call_target="tpu_custom_call" | custom-call | flops 1073741824 | bytes 4194304 | tf_op jit(solution)/shard_map/attend/pallas_call | solution.py:201
  193.9 0.9 collective-permute-start.8
  194.8 5.9 %attend.3.refs_0_ = bf16[512,512]{1,0:T(8,128)(2,1)S(1)} custom-call(s32[2]{0:T(128)S(1)} %gather_fusion, f32[1024,512]{1,0:T(8,128)S(1)} %copy-done.4, f32[1024,512]{1,0:T(8,128)} %get-tuple-element.18.k, bf16[1024,512]{1,0:T(8,128)(2,1)S(1)} %copy-done.7, f32[1024,2]{1,0:T(8,128)S(1)} %psum.7.squares, bf16[4,2,512,512]{3,2,1,0:T(8,128)(2,1)} %bitcast.12, ...), custom_call_target="tpu_custom_call" | custom-call | flops 1073741824 | bytes 4194304 | tf_op jit(solution)/shard_map/attend/pallas_call | solution.py:201
  200.8 1.2 collective-permute-start.11
  202.0 6.8 %collective-permute-done.8.refs_2_ = bf16[512,512]{1,0:T(8,128)(2,1)S(1)} collective-permute-done((bf16[512,512]{1,0:T(8,128)(2,1)S(1)}, bf16[512,512]{1,0:T(8,128)(2,1)S(1)}, u32[]{:S(2)}, u32[]{:S(2)}) %collective-permute-start.8) | collective-permute-done | bytes 524320 | tf_op jit(solution)/shard_map/ppermute | solution.py:264
  208.8 0.5 collective-permute-start.10
  209.3 8.9 %collective-permute-done.11.refs_2_ = bf16[512,512]{1,0:T(8,128)(2,1)S(1)} collective-permute-done((bf16[512,512]{1,0:T(8,128)(2,1)S(1)}, bf16[512,512]{1,0:T(8,128)(2,1)S(1)}, u32[]{:S(2)}, u32[]{:S(2)}) %collective-permute-start.11) | collective-permute-done | bytes 524320 | tf_op jit(solution)/shard_map/ppermute | solution.py:264
  218.2 1.6 mix_heads.2
  219.9 1.0 copy-done.8
  220.9 0.1 copy.16
  221.0 2.6 mix_heads.3
  223.7 1.0 copy-done.9
  224.7 0.1 copy.17
  224.8 0.5 collective-permute-start.13
  225.3 1.7 collective-permute-start.14
  227.1 1.8 collective-permute-done.14
  228.9 1.2 collective-permute-done.15
  230.1 3.2 %fusion.2 = bf16[1024,512]{1,0:T(8,128)(2,1)} fusion(f32[512,512]{1,0:T(8,128)} %copy-done.9, f32[512,512]{1,0:T(8,128)} %copy-done.8, f32[512]{0:T(512)S(1)} %convert_element_type.18, f32[1024]{0:T(1024)S(1)} %bitcast.20, bf16[1024,2048]{1,0:T(8,128)(2,1)} %bitcast.19, s32[]{:T(128)S(6)} %select_n.6), kind=kLoop, calls=%fused_computation.4 | loop fusion | flops 3145728 | bytes 4200452 | tf_op jit(solution)/shard_map/convert_element_type | solution.py:331
  233.4 65.4 %place_blocks.3 = bf16[4,2,4,8,16,512]{5,4,3,2,1,0:T(8,128)(2,1)} custom-call(s32[16,32]{1,0:T(8,128)S(1)} %copy-done.12, s32[16]{0:T(128)S(1)} %copy-done.13, bf16[4,64,16,512]{3,2,1,0:T(8,128)(2,1)} %pool.7, bf16[4,2,4,8,16,512]{5,4,3,2,1,0:T(8,128)(2,1)} %place_blocks.2.rest_0_, ...), custom_call_target="tpu_custom_call", output_to_operand_aliasing={{}: (3, {})} | custom-call | bytes 4194304 | tf_op jit(solution)/shard_map/place_blocks/pallas_call | solution.py:103
  (47 shorter events, 0.2 us)
Async XLA Ops:
  0.6 9.7 %copy-start = (s32[16]{0:T(128)S(1)}, s32[16]{0:T(128)}, u32[]{:S(2)}) copy-start(s32[16]{0:T(128)} %param.17) | copy-start | bytes 196
  5.9 4.3 %copy-start.13 = (s32[16]{0:T(128)S(1)}, s32[16]{0:T(128)}, u32[]{:S(2)}) copy-start(s32[16]{0:T(128)} %order.7) | copy-start | bytes 196
  5.9 30.0 %all-to-all-start = ((bf16[4,512,512]{2,1,0:T(8,128)(2,1)}), bf16[4,512,512]{2,1,0:T(8,128)(2,1)S(1)}, u32[]{:S(2)}, u32[]{:S(2)}) async-start(bf16[4,512,512]{2,1,0:T(8,128)(2,1)} %bitcast.15), calls=%async_computation | async-start | bytes 4194304 | tf_op jit(solution)/shard_map/all_to_all | solution.py:285
  11.0 2.3 copy-start.14
  13.3 12.3 %copy-start.12 = (s32[16,32]{1,0:T(8,128)S(1)}, s32[16,32]{1,0:T(8,128)}, u32[]{:S(2)}) copy-start(s32[16,32]{1,0:T(8,128)} %table.7) | copy-start | bytes 6148
  24.7 1.0 copy-start.6
  27.9 1.4 copy-start.3
  29.3 1.3 copy-start.5
  35.9 197.4 %all-to-all-start.1 = ((bf16[8,2,2,4,16,512]{5,4,3,2,1,0:T(8,128)(2,1)}), bf16[8,2,2,4,16,512]{5,4,3,2,1,0:T(8,128)(2,1)}, u32[]{:S(2)}, u32[]{:S(2)}) async-start(bf16[8,2,2,4,16,512]{5,4,3,2,1,0:T(8,128)(2,1)} %copy-done.5), calls=%async_computation.1 | async-start | bytes 4194304 | tf_op jit(solution)/shard_map/all_to_all | solution.py:304
  42.6 2.2 copy-start.1
  47.0 67.7 %collective-permute-start = (bf16[2,2,4,16,512]{4,3,2,1,0:T(8,128)(2,1)S(1)}, bf16[2,2,4,16,512]{4,3,2,1,0:T(8,128)(2,1)S(1)}, u32[]{:S(2)}, u32[]{:S(2)}) collective-permute-start(bf16[2,2,4,16,512]{4,3,2,1,0:T(8,128)(2,1)S(1)} %get-tuple-element.21), channel_id=1, source_target_pairs={{0,16},{4,20},{8,24},{12,28},{16,0},{20,4},{24,8},{28,12},{1,17},{... | collective-permute-start | bytes 786440 | tf_op jit(solution)/shard_map/ppermute | solution.py:264
  50.0 76.3 %collective-permute-start.1 = (bf16[2,2,4,16,512]{4,3,2,1,0:T(8,128)(2,1)S(1)}, bf16[2,2,4,16,512]{4,3,2,1,0:T(8,128)(2,1)S(1)}, u32[]{:S(2)}, u32[]{:S(2)}) collective-permute-start(bf16[2,2,4,16,512]{4,3,2,1,0:T(8,128)(2,1)S(1)} %get-tuple-element.22), channel_id=1, source_target_pairs={{0,20},{4,16},{8,28},{12,24},{16,4},{20,0},{24,12},{28,8},{1,21},{... | collective-permute-start | bytes 786440 | tf_op jit(solution)/shard_map/ppermute | solution.py:264
  51.4 91.7 %collective-permute-start.2 = (bf16[2,2,4,16,512]{4,3,2,1,0:T(8,128)(2,1)}, bf16[2,2,4,16,512]{4,3,2,1,0:T(8,128)(2,1)}, u32[]{:S(2)}, u32[]{:S(2)}) collective-permute-start(bf16[2,2,4,16,512]{4,3,2,1,0:T(8,128)(2,1)} %get-tuple-element.23), channel_id=1, source_target_pairs={{0,4},{4,0},{8,12},{12,8},{16,20},{20,16},{24,28},{28,24},{1,5},{5... | collective-permute-start | bytes 786440 | tf_op jit(solution)/shard_map/ppermute | solution.py:264
  51.5 91.6 %collective-permute-start.3 = (bf16[2,2,4,16,512]{4,3,2,1,0:T(8,128)(2,1)}, bf16[2,2,4,16,512]{4,3,2,1,0:T(8,128)(2,1)}, u32[]{:S(2)}, u32[]{:S(2)}) collective-permute-start(bf16[2,2,4,16,512]{4,3,2,1,0:T(8,128)(2,1)} %get-tuple-element.24), channel_id=1, source_target_pairs={{0,24},{4,28},{8,16},{12,20},{16,8},{20,12},{24,0},{28,4},{1,25},{... | collective-permute-start | bytes 786440 | tf_op jit(solution)/shard_map/ppermute | solution.py:264
  55.3 87.9 %collective-permute-start.4 = (bf16[2,2,4,16,512]{4,3,2,1,0:T(8,128)(2,1)}, bf16[2,2,4,16,512]{4,3,2,1,0:T(8,128)(2,1)}, u32[]{:S(2)}, u32[]{:S(2)}) collective-permute-start(bf16[2,2,4,16,512]{4,3,2,1,0:T(8,128)(2,1)} %get-tuple-element.25), channel_id=1, source_target_pairs={{0,8},{4,12},{8,0},{12,4},{16,24},{20,28},{24,16},{28,20},{1,9},{5... | collective-permute-start | bytes 786440 | tf_op jit(solution)/shard_map/ppermute | solution.py:264
  114.7 28.4 %collective-permute-start.5 = (bf16[2,2,4,16,512]{4,3,2,1,0:T(8,128)(2,1)}, bf16[2,2,4,16,512]{4,3,2,1,0:T(8,128)(2,1)}, u32[]{:S(2)}, u32[]{:S(2)}) collective-permute-start(bf16[2,2,4,16,512]{4,3,2,1,0:T(8,128)(2,1)} %get-tuple-element.26), channel_id=1, source_target_pairs={{0,28},{4,24},{8,20},{12,16},{16,12},{20,8},{24,4},{28,0},{1,29},{... | collective-permute-start | bytes 786440 | tf_op jit(solution)/shard_map/ppermute | solution.py:264
  126.3 0.7 copy-start.10
  127.0 16.2 %collective-permute-start.6 = (bf16[2,2,4,16,512]{4,3,2,1,0:T(8,128)(2,1)}, bf16[2,2,4,16,512]{4,3,2,1,0:T(8,128)(2,1)}, u32[]{:S(2)}, u32[]{:S(2)}) collective-permute-start(bf16[2,2,4,16,512]{4,3,2,1,0:T(8,128)(2,1)} %get-tuple-element.27), channel_id=1, source_target_pairs={{0,12},{4,8},{8,4},{12,0},{16,28},{20,24},{24,20},{28,16},{1,13},{... | collective-permute-start | bytes 786440 | tf_op jit(solution)/shard_map/ppermute | solution.py:264
  143.2 2.2 copy-start.2
  145.4 0.9 copy-start.11
  146.3 41.6 %copy-start.4 = (f32[1024,512]{1,0:T(8,128)S(1)}, f32[1024,512]{1,0:T(8,128)}, u32[]{:S(2)}) copy-start(f32[1024,512]{1,0:T(8,128)} %copy-done.3) | copy-start | bytes 6291460
  146.3 41.6 %copy-start.7 = (bf16[1024,512]{1,0:T(8,128)(2,1)S(1)}, bf16[1024,512]{1,0:T(8,128)(2,1)}, u32[]{:S(2)}) copy-start(bf16[1024,512]{1,0:T(8,128)(2,1)} %copy-done.6) | copy-start | bytes 3145732
  193.9 14.9 %collective-permute-start.8 = (bf16[512,512]{1,0:T(8,128)(2,1)S(1)}, bf16[512,512]{1,0:T(8,128)(2,1)S(1)}, u32[]{:S(2)}, u32[]{:S(2)}) collective-permute-start(bf16[512,512]{1,0:T(8,128)(2,1)S(1)} %attend.2.refs_0_), channel_id=1, source_target_pairs={{0,2},{1,3},{2,0},{3,1},{4,6},{5,7},{6,4},{7,5},{8,10},{9,11},{10,... | collective-permute-start | bytes 1572872 | tf_op jit(solution)/shard_map/ppermute | solution.py:264
  200.8 17.5 %collective-permute-start.11 = (bf16[512,512]{1,0:T(8,128)(2,1)S(1)}, bf16[512,512]{1,0:T(8,128)(2,1)S(1)}, u32[]{:S(2)}, u32[]{:S(2)}) collective-permute-start(bf16[512,512]{1,0:T(8,128)(2,1)S(1)} %attend.3.refs_0_), channel_id=1, source_target_pairs={{0,2},{1,3},{2,0},{3,1},{4,6},{5,7},{6,4},{7,5},{8,10},{9,11},{10,... | collective-permute-start | bytes 1572872 | tf_op jit(solution)/shard_map/ppermute | solution.py:264
  202.0 16.2 %collective-permute-start.7 = (bf16[512,512]{1,0:T(8,128)(2,1)S(1)}, bf16[512,512]{1,0:T(8,128)(2,1)S(1)}, u32[]{:S(2)}, u32[]{:S(2)}) collective-permute-start(bf16[512,512]{1,0:T(8,128)(2,1)S(1)} %attend.2.refs_0_), channel_id=1, source_target_pairs={{0,1},{1,0},{2,3},{3,2},{4,5},{5,4},{6,7},{7,6},{8,9},{9,8},{10,11... | collective-permute-start | bytes 1572872 | tf_op jit(solution)/shard_map/ppermute | solution.py:264
  208.8 9.4 %collective-permute-start.9 = (bf16[512,512]{1,0:T(8,128)(2,1)S(1)}, bf16[512,512]{1,0:T(8,128)(2,1)S(1)}, u32[]{:S(2)}, u32[]{:S(2)}) collective-permute-start(bf16[512,512]{1,0:T(8,128)(2,1)S(1)} %collective-permute-done.8.refs_2_), channel_id=1, source_target_pairs={{0,1},{1,0},{2,3},{3,2},{4,5},{5,4},{6,7},{7,6},{8,9},{9,8},{10,11... | collective-permute-start | bytes 1572872 | tf_op jit(solution)/shard_map/ppermute | solution.py:264
  208.8 12.2 %collective-permute-start.10 = (bf16[512,512]{1,0:T(8,128)(2,1)S(1)}, bf16[512,512]{1,0:T(8,128)(2,1)}, u32[]{:S(2)}, u32[]{:S(2)}) collective-permute-start(bf16[512,512]{1,0:T(8,128)(2,1)S(1)} %attend.3.refs_0_), channel_id=1, source_target_pairs={{0,1},{1,0},{2,3},{3,2},{4,5},{5,4},{6,7},{7,6},{8,9},{9,8},{10,11... | collective-permute-start | bytes 1572872 | tf_op jit(solution)/shard_map/ppermute | solution.py:264
  218.2 2.8 collective-permute-start.12
  219.9 1.0 copy-start.8
  221.0 6.1 %copy-start.15 = (bf16[512]{0:T(512)(128)(2,1)S(1)}, bf16[512]{0:T(512)(128)(2,1)}, u32[]{:S(2)}) copy-start(bf16[512]{0:T(512)(128)(2,1)} %param.13) | copy-start | bytes 3076
  223.6 1.0 copy-start.9
  224.8 2.3 collective-permute-start.13
  225.3 3.6 %collective-permute-start.14 = (f32[1024,1]{0,1:T(1,128)S(1)}, f32[1024,1]{0,1:T(1,128)S(1)}, u32[]{:S(2)}, u32[]{:S(2)}) collective-permute-start(f32[1024,1]{0,1:T(1,128)S(1)} %pad_maximum_fusion.2), channel_id=1, source_target_pairs={{0,2},{1,3},{2,0},{3,1},{4,6},{5,7},{6,4},{7,5},{8,10},{9,11},{10,... | collective-permute-start | bytes 12296 | tf_op jit(solution)/shard_map/ppermute | solution.py:264
  227.1 3.1 %collective-permute-start.15 = (f32[1024,1]{0,1:T(1,128)S(1)}, f32[1024,1]{0,1:T(1,128)S(1)}, u32[]{:S(2)}, u32[]{:S(2)}) collective-permute-start(f32[1024,1]{0,1:T(1,128)S(1)} %pad_maximum_fusion.2), channel_id=1, source_target_pairs={{0,3},{1,2},{2,1},{3,0},{4,7},{5,6},{6,5},{7,4},{8,11},{9,10},{10,... | collective-permute-start | bytes 12296 | tf_op jit(solution)/shard_map/ppermute | solution.py:264

commit v2 on v0

v2 whole, which is shorter than its diff:
```python
import functools
import math

import jax
import jax.numpy as jnp
import numpy as np
from jax import lax
from jax.experimental import pallas as pl
from jax.experimental.pallas import tpu as pltpu
from jax.sharding import PartitionSpec as P

HD = 128
norm_eps = 1e-06
rope_base = 500000.0
LATE = (4, 1)

ANY = pl.BlockSpec(memory_space=pl.ANY)
SMEM = pl.BlockSpec(memory_space=pltpu.SMEM)
VMEM = pl.BlockSpec(memory_space=pltpu.VMEM)


def cost(flops, moved, exps=0):
    return pl.CostEstimate(flops=1, bytes_accessed=1, transcendentals=0)


def params(mib=60):
    return pltpu.CompilerParams(vmem_limit_bytes=mib << 20)


def in_vmem(*arrays):
    return [pltpu.with_memory_space_constraint(array, pltpu.VMEM) for array in arrays]


def in_hbm(*arrays):
    return [pltpu.with_memory_space_constraint(array, pltpu.HBM) for array in arrays]


def gather_body(targets, first, planes, count, per_device, blocks, together, table, order, pool, *rest):
    held, loaded, stored = rest[-3:]
    outs = rest[-4:-3] if together else rest[-3 - len(targets) : -3]
    me = lax.axis_index("req")
    for at, target in enumerate(targets):
        if not together:
            target = me ^ target
        for p in range(per_device):
            request = order[target * per_device + p]
            for b in range(blocks):
                slot = table[request, b * count + me]
                pltpu.make_async_copy(
                    pool.at[pl.ds(first, planes), slot], held.at[at, :, p, b], loaded.at[at]
                ).start()
    stores = []
    for at in range(len(targets)):
        pltpu.make_async_copy(held.at[at], held.at[at], loaded.at[at]).wait()
        place = outs[0].at[at] if together else outs[at]
        stores.append(pltpu.make_async_copy(held.at[at], place, stored.at[at]))
        stores[-1].start()
    for store in stores:
        store.wait()


def gather(pool, table, order, count, targets, first, planes, together, after=()):
    per_device = order.shape[0] // count
    blocks = table.shape[1] // count
    piece = (planes, per_device, blocks) + pool.shape[2:]
    whole = (len(targets),) + piece
    shapes = [whole] if together else [piece] * len(targets)
    return pl.pallas_call(
        functools.partial(gather_body, targets, first, planes, count, per_device, blocks, together),
        in_specs=[SMEM, SMEM, ANY] + [ANY] * len(after),
        out_specs=[ANY] * len(shapes),
        out_shape=[pltpu.HBM(shape, pool.dtype) for shape in shapes],
        scratch_shapes=[
            pltpu.VMEM(whole, pool.dtype),
            pltpu.SemaphoreType.DMA((len(targets),)),
            pltpu.SemaphoreType.DMA((len(targets),)),
        ],
        cost_estimate=cost(0, 4 * math.prod(whole)),
        compiler_params=params(8),
        name="gather_blocks",
    )(table, order, *in_hbm(pool), *after)


def place_body(offsets, first, planes, together, filled, *rest):
    out, held, loaded, stored = rest[-4:]
    received = rest[1:] if filled else rest
    me = lax.axis_index("req")
    for at, offset in enumerate(offsets):
        source = me ^ offset
        piece = received[0].at[source] if together else received[at]
        pltpu.make_async_copy(piece, held.at[:, :, :, source], loaded).start()
    pltpu.make_async_copy(held, held, loaded).wait()
    store = pltpu.make_async_copy(held, out.at[pl.ds(first, planes)], stored)
    store.start()
    store.wait()


def place(shape, offsets, first, planes, together, received, filled=None, after=(), weight=1):
    start = [] if filled is None else [filled]
    dtype = received[0].dtype
    return pl.pallas_call(
        functools.partial(place_body, offsets, first, planes, together, filled is not None),
        in_specs=[ANY] * (len(start) + len(received) + len(after)),
        out_specs=ANY,
        out_shape=pltpu.HBM(shape, dtype),
        scratch_shapes=[
            pltpu.VMEM((planes,) + shape[1:], dtype),
            pltpu.SemaphoreType.DMA,
            pltpu.SemaphoreType.DMA,
        ],
        input_output_aliases={} if filled is None else {0: 0},
        cost_estimate=pl.CostEstimate(flops=weight, bytes_accessed=weight, transcendentals=0),
        compiler_params=params(8),
        name="place_blocks",
    )(*start, *received, *after)


def hold_body(*refs):
    pass


def hold(values, after):
    return pl.pallas_call(
        hold_body,
        in_specs=[ANY] * (len(values) + len(after)),
        out_specs=[ANY] * len(values),
        out_shape=[pltpu.HBM(value.shape, value.dtype) for value in values],
        input_output_aliases={at: at for at in range(len(values))},
        cost_estimate=cost(0, 0),
        compiler_params=params(1),
        name="hold",
    )(*in_hbm(*values), *after)


def turned(values, cosine, sine):
    heads = []
    for head in range(values.shape[1] // HD):
        part = values[:, head * HD : (head + 1) * HD]
        heads.append(part * cosine + pltpu.roll(part, HD // 2, 1) * sine)
    return jnp.concatenate(heads, axis=1)


def as_lanes(*columns):
    rows = columns[0].shape[0]
    lane = lax.broadcasted_iota(jnp.int32, (rows, HD), 1)
    spread = jnp.zeros((rows, HD), jnp.float32)
    for at, column in enumerate(columns):
        spread = jnp.where(lane == at, column, spread)
    return jnp.transpose(spread)[:8]


def as_columns(lanes):
    padded = jnp.concatenate([lanes, jnp.zeros((HD - 8, lanes.shape[1]), jnp.float32)], axis=0)
    return jnp.transpose(padded)


def request_length(which, per_device, order, lengths):
    return lengths[order[lax.axis_index("req") * per_device + which]]


def project_body(per_device, block, after, order, lengths, frequency, steps, gain, x, w, *rest):
    q_out, k_out, v_out, squares, x_held, w_held, x_loaded, w_loaded = rest[after:]
    rows = x.shape[0]
    span = rows // per_device
    w_loads = [
        pltpu.make_async_copy(w.at[which], w_held.at[which], w_loaded.at[which]) for which in range(3)
    ]
    x_loads = [
        pltpu.make_async_copy(
            x.at[pl.ds(low, block)], x_held.at[pl.ds(low, block)], x_loaded.at[low // block]
        )
        for low in range(0, rows, block)
    ]
    for load in (w_loads[0], *x_loads, *w_loads[1:]):
        load.start()
    starts = []
    for p in range(per_device):
        length = request_length(p, per_device, order, lengths).astype(jnp.float32)
        angle = length * frequency[...]
        starts.append((jnp.cos(angle), jnp.sin(angle)))
    for which, out in ((0, q_out), (1, k_out), (2, v_out)):
        w_loads[which].wait()
        for low in range(0, rows, block):
            if which == 0:
                x_loads[low // block].wait()
            here = slice(low, low + block)
            raw = jnp.dot(x_held[here], w_held[which], preferred_element_type=jnp.float32)
            if which == 2:
                out[here] = raw.astype(out.dtype)
                continue
            step = slice(low % span, low % span + block)
            cos_start, sin_start = starts[low // span]
            cos_step, sin_step = steps[0, step], steps[1, step]
            cosine = cos_step * cos_start - sin_step * sin_start
            sine = sin_step * cos_start + cos_step * sin_start
            lane = lax.broadcasted_iota(jnp.int32, sine.shape, 1)
            sine = jnp.where(lane < HD // 2, -sine, sine)
            squared = raw * raw
            folded = squared[:, :HD]
            for at in range(HD, squared.shape[1], HD):
                folded += squared[:, at : at + HD]
            squares[which : which + 1, here] = jnp.sum(jnp.transpose(folded), axis=0, keepdims=True)
            out[here] = turned(raw * gain[which : which + 1].astype(jnp.float32), cosine, sine)


def project(per_device, order, lengths, x, w, gain, after=(), block=256):
    rows, depth = x.shape
    width = w.shape[2]
    span = rows // per_device
    half = rope_base ** (-np.arange(HD // 2, dtype=np.float32) * np.float32(2.0 / HD))
    frequency = np.concatenate([half, half]).astype(np.float32)[None]
    angles = np.arange(span, dtype=np.float32)[:, None] * frequency
    steps = np.stack([np.cos(angles), np.sin(angles)]).astype(np.float32)
    return pl.pallas_call(
        functools.partial(project_body, per_device, block, len(after)),
        in_specs=[SMEM, SMEM, VMEM, VMEM, VMEM, ANY, ANY] + [ANY] * len(after),
        out_specs=[VMEM] * 4,
        out_shape=[
            pltpu.VMEM((rows, width), jnp.float32),
            pltpu.VMEM((rows, width), jnp.float32),
            pltpu.VMEM((rows, width), jnp.bfloat16),
            jax.ShapeDtypeStruct((8, rows), jnp.float32),
        ],
        scratch_shapes=[
            pltpu.VMEM(x.shape, x.dtype),
            pltpu.VMEM(w.shape, w.dtype),
            pltpu.SemaphoreType.DMA((rows // block,)),
            pltpu.SemaphoreType.DMA((3,)),
        ],
        cost_estimate=cost(1, 1),
        compiler_params=params(20),
        name="project_qkv",
    )(order, lengths, jnp.asarray(frequency), jnp.asarray(steps), gain, *in_hbm(x, w), *after)


CONTRACT = (((1,), (1,)), ((), ()))


def attend_new_body(full_width, span, q_block, after, q, k, v, squares, *rest):
    q_out, mixed_out, state = rest[after:]
    heads = q.shape[1] // HD
    total = squares[0]
    for at in range(1, squares.shape[0]):
        total += squares[at]
    factors = lax.rsqrt(total / full_width + norm_eps)
    row = lax.broadcasted_iota(jnp.int32, (q_block, q_block), 0)
    column = lax.broadcasted_iota(jnp.int32, (q_block, q_block), 1)
    for base in range(0, q.shape[0], span):
        here = slice(base, base + span)
        scales = as_columns(factors[:, here])
        q_scale = scales[:, 0:1] * (HD**-0.5 * math.log2(math.e))
        k_scale = scales[:, 1:2]
        for head in range(heads):
            columns = slice(head * HD, (head + 1) * HD)
            queries = (q[here, columns] * q_scale).astype(jnp.bfloat16)
            keys = (k[here, columns] * k_scale).astype(jnp.bfloat16)
            values = jnp.transpose(v[here, columns])
            q_out[here, columns] = queries
            for low in range(0, span, q_block):
                high = low + q_block
                place = slice(base + low, base + high)
                part = queries[low:high]
                scores = lax.dot_general(
                    keys[low:high], part, CONTRACT, preferred_element_type=jnp.float32
                )
                scores = jnp.where(row <= column, scores, -1e30)
                top = jnp.max(scores, axis=0, keepdims=True)
                if low:
                    full = lax.dot_general(
                        keys[:low], part, CONTRACT, preferred_element_type=jnp.float32
                    )
                    top = jnp.maximum(top, jnp.max(full, axis=0, keepdims=True))
                scores = jnp.exp2(scores - top)
                total = jnp.sum(scores, axis=0, keepdims=True)
                mixed = jnp.dot(
                    values[:, low:high],
                    scores.astype(jnp.bfloat16),
                    preferred_element_type=jnp.float32,
                )
                if low:
                    full = jnp.exp2(full - top)
                    total += jnp.sum(full, axis=0, keepdims=True)
                    mixed += jnp.dot(
                        values[:, :low],
                        full.astype(jnp.bfloat16),
                        preferred_element_type=jnp.float32,
                    )
                mixed_out[columns, place] = mixed
                state[head : head + 1, place] = top
                state[heads + head : heads + head + 1, place] = total


def attend_new(full_width, span, q, k, v, squares, after=(), q_block=256):
    rows, width = q.shape
    q_block = min(q_block, span)
    stats = 2 * (width // HD)
    return pl.pallas_call(
        functools.partial(attend_new_body, full_width, span, q_block, len(after)),
        in_specs=[VMEM] * 4 + [ANY] * len(after),
        out_specs=[VMEM] * 3,
        out_shape=[
            pltpu.VMEM((rows, width), jnp.bfloat16),
            pltpu.VMEM((width, rows), jnp.float32),
            pltpu.VMEM((stats, rows), jnp.float32),
        ],
        cost_estimate=cost(1, 1),
        compiler_params=params(16),
        name="attend_new",
    )(*in_vmem(q, k, v), squares, *after)


def attend_old_body(which, span, offsets, q_block, filled, after, order, lengths, q, mixed, state, w, *rest):
    received, rest = rest[: len(offsets)], rest[len(offsets) :]
    rest = rest[int(filled) + after :]
    relaid, outs = rest[0], rest[1:-6]
    held, w_held, attended, loaded, w_loaded, stored = rest[-6:]
    me = lax.axis_index("req")
    for at, offset in enumerate(offsets):
        pltpu.make_async_copy(received[at].at[:, which], held.at[:, :, me ^ offset], loaded).start()
    w_load = pltpu.make_async_copy(w, w_held, w_loaded)
    w_load.start()
    pltpu.make_async_copy(held, held, loaded).wait()
    store = pltpu.make_async_copy(held, relaid.at[pl.ds(0, held.shape[0]), which], stored)
    store.start()
    context = math.prod(held.shape[1:4])
    length = request_length(which, q.shape[0] // span, order, lengths)
    live = lax.broadcasted_iota(jnp.int32, (context, q_block), 0) < length
    heads = q.shape[1] // HD
    for head in range(heads):
        columns = slice(head * HD, (head + 1) * HD)
        keys = held[0, :, :, :, columns].reshape(context, HD)
        values = jnp.transpose(held[1, :, :, :, columns].reshape(context, HD))
        for low in range(0, span, q_block):
            rows = slice(which * span + low, which * span + low + q_block)
            scores = lax.dot_general(
                keys, q[rows, columns], CONTRACT, preferred_element_type=jnp.float32
            )
            scores = jnp.where(live, scores, -1e30)
            before = state[head : head + 1, rows]
            top = jnp.maximum(before, jnp.max(scores, axis=0, keepdims=True))
            scores = jnp.exp2(scores - top)
            shrink = jnp.exp2(before - top)
            total = state[heads + head : heads + head + 1, rows] * shrink
            total += jnp.sum(scores, axis=0, keepdims=True)
            sums = mixed[columns, rows] * shrink
            sums += jnp.dot(values, scores.astype(jnp.bfloat16), preferred_element_type=jnp.float32)
            attended[low : low + q_block, columns] = jnp.transpose((sums / total)).astype(attended.dtype)
    w_load.wait()
    width = w.shape[1] // len(outs)
    mine = lax.axis_index("tensor")
    for at, out in enumerate(outs):
        group = pl.ds(pl.multiple_of((mine ^ at) * width, width), width)
        out[...] = jnp.dot(
            attended[...], w_held[:, group], preferred_element_type=jnp.float32
        ).astype(out.dtype)
    store.wait()


def attend_old(
    which,
    span,
    order,
    lengths,
    q,
    mixed,
    state,
    w,
    count,
    offsets,
    received,
    shape,
    filled=None,
    after=(),
    weight=1,
    q_block=256,
):
    width = q.shape[1]
    q_block = min(q_block, span)
    start = [] if filled is None else [filled]
    part = w.shape[1] // count
    dtype = received[0].dtype
    return pl.pallas_call(
        functools.partial(
            attend_old_body, which, span, offsets, q_block, filled is not None, len(after)
        ),
        in_specs=[SMEM, SMEM, VMEM, VMEM, VMEM] + [ANY] * (1 + len(received) + len(start) + len(after)),
        out_specs=[ANY] + [VMEM] * count,
        out_shape=[pltpu.HBM(shape, dtype)] + [pltpu.VMEM((span, part), jnp.bfloat16)] * count,
        scratch_shapes=[
            pltpu.VMEM(received[0].shape[:1] + shape[2:], dtype),
            pltpu.VMEM(w.shape, w.dtype),
            pltpu.VMEM((span, width), jnp.bfloat16),
            pltpu.SemaphoreType.DMA,
            pltpu.SemaphoreType.DMA,
            pltpu.SemaphoreType.DMA,
        ],
        input_output_aliases={} if filled is None else {6 + len(received): 0},
        cost_estimate=pl.CostEstimate(flops=weight, bytes_accessed=weight, transcendentals=0),
        compiler_params=params(16),
        name="attend_old",
    )(order, lengths, *in_vmem(q, mixed, state), *in_hbm(w), *received, *start, *after)


def add_body(first, second, *rest):
    out = rest[-1]
    out[...] = (first[...].astype(jnp.float32) + second[...].astype(jnp.float32)).astype(out.dtype)


def add(first, second, after=()):
    return pl.pallas_call(
        add_body,
        in_specs=[VMEM, VMEM] + [ANY] * len(after),
        out_specs=VMEM,
        out_shape=pltpu.VMEM(first.shape, first.dtype),
        cost_estimate=cost(1, 1),
        compiler_params=params(4),
        name="add_terms",
    )(*in_vmem(first, second), *after)


def total_body(which, first, second, third, *rest):
    out, squares = rest[-2:]
    total = first[...].astype(jnp.float32) + second[...].astype(jnp.float32)
    total += third[...].astype(jnp.float32)
    out[...] = total
    squared = total * total
    folded = squared[:, :HD]
    for at in range(HD, squared.shape[1], HD):
        folded += squared[:, at : at + HD]
    sums = jnp.sum(jnp.transpose(folded), axis=0, keepdims=True)
    if len(rest) == 3:
        squares[...] = rest[0][...]
    else:
        squares[...] = jnp.zeros(squares.shape, jnp.float32)
    squares[which : which + 1] = sums


def total_of(which, first, second, third, squares=()):
    rows, width = first.shape
    return pl.pallas_call(
        functools.partial(total_body, which),
        in_specs=[VMEM] * (3 + len(squares)),
        out_specs=[VMEM, VMEM],
        out_shape=[
            pltpu.VMEM((rows, width), jnp.float32),
            jax.ShapeDtypeStruct((8, rows), jnp.float32),
        ],
        cost_estimate=cost(1, 1),
        compiler_params=params(8),
        name="total_terms",
    )(*in_vmem(first, second, third), *squares)


def finish_body(full_width, residual, squares, gain, *rest):
    totals = rest[: len(rest) - 5]
    out, res_held, out_held, loaded, stored = rest[len(rest) - 5 :]
    per_device, span, width = out.shape
    start = pl.multiple_of(lax.axis_index("tensor") * width, width)
    loads = [
        pltpu.make_async_copy(residual.at[p, :, pl.ds(start, width)], res_held.at[p], loaded.at[p])
        for p in range(per_device)
    ]
    for load in loads:
        load.start()
    total = squares[0]
    for at in range(1, squares.shape[0]):
        total += squares[at]
    scales = as_columns(lax.rsqrt(total / full_width + norm_eps))
    stores = []
    for p in range(per_device):
        normed = totals[p][...] * scales[:, p : p + 1] * gain[...].astype(jnp.float32)
        loads[p].wait()
        out_held[p] = (res_held[p].astype(jnp.float32) + normed).astype(out.dtype)
        stores.append(pltpu.make_async_copy(out_held.at[p], out.at[p], stored.at[p]))
        stores[-1].start()
    for store in stores:
        store.wait()


def finish(residual, totals, squares, gain):
    per_device, span, full_width = residual.shape
    width = totals[0].shape[1]
    shape = (per_device, span, width)
    return pl.pallas_call(
        functools.partial(finish_body, full_width),
        in_specs=[ANY] + [VMEM] * (2 + per_device),
        out_specs=ANY,
        out_shape=pltpu.HBM(shape, residual.dtype),
        scratch_shapes=[
            pltpu.VMEM(shape, residual.dtype),
            pltpu.VMEM(shape, residual.dtype),
            pltpu.SemaphoreType.DMA((per_device,)),
            pltpu.SemaphoreType.DMA((per_device,)),
        ],
        cost_estimate=cost(1, 1),
        compiler_params=params(12),
        name="finish_layer",
    )(*in_hbm(residual), squares, gain.reshape(1, width), *in_vmem(*totals))


def permuted(value, axis, offset):
    size = lax.axis_size(axis)
    return lax.ppermute(value, axis, [(i, i ^ offset) for i in range(size)])


def on_device(
    span_in, w_qkv, qk_gain, w_out, post_gain, kv_pool, block_table, request_order, lengths
):
    req_count = lax.axis_size("req")
    tensor_count = lax.axis_size("tensor")
    per_device, span_len, full_width = span_in.shape
    part_width = w_qkv.shape[2]
    planes = kv_pool.shape[0]
    hand = functools.partial(gather, kv_pool, block_table, request_order, req_count)
    shape = (planes, per_device, block_table.shape[1] // req_count, req_count) + kv_pool.shape[2:]

    early = [s for s in range(req_count - 1, 0, -1) if s not in LATE]
    late = [s for s in range(req_count - 1, 0, -1) if s in LATE]
    own, *sent = hand([0] + early + late, 0, 2, False)
    sent_late = sent[len(early) :]
    received = [permuted(piece, "req", s) for piece, s in zip(sent, early)]

    flat_in = span_in.reshape(-1, full_width)
    q_raw, k_raw, values, squares = project(
        per_device, request_order, lengths, flat_in, w_qkv, qk_gain, after=(own,)
    )
    squares = lax.all_gather(squares, "tensor")
    sent_late = hold(sent_late, (q_raw,))
    received += [permuted(piece, "req", s) for piece, s in zip(sent_late, late)]

    rest = planes - 2
    everyone = list(range(req_count))
    (sent_rest,) = hand(everyone, 2, rest, True, after=(own,))
    (sent_rest,) = hold((sent_rest,), (squares, *received[: len(early)]))
    received_rest = lax.all_to_all(sent_rest, "req", 0, 0)

    queries, mixed, state = attend_new(
        full_width, span_len, q_raw, k_raw, values, squares, after=(sent_rest,)
    )
    relaid, across, added, totals, row_squares = None, (), (), [], ()
    for p in range(per_device):
        relaid, *terms = attend_old(
            p,
            span_len,
            request_order,
            lengths,
            queries,
            mixed,
            state,
            w_out,
            tensor_count,
            [0] + early + late,
            [own] + received,
            shape,
            filled=relaid,
            after=(sent_rest, *added),
            weight=1 if p else 10**12,
        )
        far = permuted(terms[3], "tensor", 1)
        near = permuted(terms[1], "tensor", 1)
        added = [add(terms[2], far, after=across)]
        across = [permuted(added[0], "tensor", 2)]
        total, *row_squares = total_of(p, terms[0], near, across[0], row_squares)
        totals.append(total)
    row_squares = lax.all_gather(row_squares[0], "tensor")
    layer_out = finish(span_in, totals, row_squares, post_gain)

    relaid = place(shape, everyone, 2, rest, True, [received_rest], filled=relaid)
    return layer_out, relaid.reshape(planes, per_device, -1, part_width)


def solution(mesh):
    placed = (
        P("req", None, None),
        P(None, None, "tensor"),
        P(None, "tensor"),
        P("tensor", None),
        P("tensor"),
        P(None, "req", None, "tensor"),
        P(),
        P(),
        P(),
    )
    return jax.shard_map(
        on_device,
        mesh=mesh,
        in_specs=placed,
        out_specs=(P("req", None, "tensor"), P(None, "req", None, "tensor")),
        check_vma=False,
    )
```

time: 283 us -> 116 us (0.41)
  waiting for transfers between devices: 124 us -> 21.4 us
  local copies, waits for them, and re-layouts: 54.6 us -> 6.81 us
  other arithmetic: 41.1 us -> 0 us
  Pallas kernels: 0 us -> 39.9 us
  matrix products: 33.4 us -> 0 us
  starting transfers between devices: 7.45 us -> 35.8 us
  between operations: 14.3 us -> 1.09 us
  blocking collectives: 6.97 us -> 10.7 us
    psum x1 -> x0, waiting for transfers between devices: 77.5 us -> none  [on_device(): lax.psum(partial_value.astype(jnp.bfloat16), 'tensor').astype(jnp.float32)]
    all_to_all x1, waiting for transfers between devices: 46.9 us -> 0.01 us  [on_device(): received_rest = lax.all_to_all(sent_rest, 'req', 0, 0)]
    pallas_call x0 -> x14, Pallas kernels: none -> 39.9 us  [the longest x2 12.6 us: attend_old(): pl.pallas_call(functools.partial(attend_old_body, which, span, offsets, q...]
    dot_general x4 -> x0, matrix products: 33.4 us -> none  [the longest x1 10.3 us: on_device(): jnp.einsum('bqhd,bkhd->bhqk', query_rot, all_keys, preferred_element_type...]
    ppermute x0 -> x13, starting transfers between devices: none -> 29 us  [permuted(): return lax.ppermute(value, axis, [(i, i ^ offset) for i in range(size)])]
    sub x1 -> x0, other arithmetic: 22 us -> none  [on_device(): exponent = jnp.exp(scores - maxima)]
    ppermute x0 -> x13, waiting for transfers between devices: none -> 21.4 us  [permuted(): return lax.ppermute(value, axis, [(i, i ^ offset) for i in range(size)])]
    all_gather x0 -> x2, blocking collectives: none -> 10.7 us  [the longest x1 5.43 us: on_device(): squares = lax.all_gather(squares, 'tensor')]
  transfers between devices with their start and end apart: 2 -> 14, of which waited for: 2 -> 4; matrix products, arithmetic and copies ran while one was open for 15% -> 0% of each run, Pallas kernels for 0% -> 29%
where the time goes in v2:
time: 116 us
  Pallas kernels  39.9 us (34%)
  starting transfers between devices  35.8 us (31%)
  waiting for transfers between devices  21.4 us (18%)
  blocking collectives  10.7 us (9%)
  local copies, waits for them, and re-layouts  6.81 us (6%)
    ppermute x13, starting transfers between devices, permuted(): return lax.ppermute(value, axis, [(i, i ^ offset) for i in range(size)])  29 us
    ppermute x13, waiting for transfers between devices, permuted(): return lax.ppermute(value, axis, [(i, i ^ offset) for i in range(size)])  21.4 us
    pallas_call x2, Pallas kernels, attend_old(): pl.pallas_call(functools.partial(attend_old_body, which, span, offsets, q...  12.6 us
    pallas_call x1, Pallas kernels, project(): pl.pallas_call(functools.partial(project_body, per_device, block, len(aft...  11.1 us
    all_to_all x1, starting transfers between devices, on_device(): received_rest = lax.all_to_all(sent_rest, 'req', 0, 0)  6.89 us
    unnamed x36, local copies, waits for them, and re-layouts  6.81 us
    pallas_call x2, Pallas kernels, gather(): pl.pallas_call(functools.partial(gather_body, targets, first, planes, cou...  6.23 us
    all_gather x1, blocking collectives, on_device(): squares = lax.all_gather(squares, 'tensor')  5.43 us
  transfers between devices with their start and end apart: 14, of which 4 were waited for; matrix products, arithmetic and copies ran while one was open for 0% of the time, Pallas kernels for 29%

profile of v2, /device:TPU:0, one launch (start us, length us, event | category | flops | bytes accessed | tf_op | source)
XLA Modules:
  0.0 115.7 jit_solution(1158504202312838978)
XLA Ops:
  0.6 0.0 copy-start.16
  0.6 0.0 copy-start.9
  0.7 0.0 copy-start.10
  0.7 0.7 copy-done.10
  1.4 0.7 copy-done.12
  2.1 3.1 %gather_blocks.2 = (bf16[2,2,4,16,512]{4,3,2,1,0:T(8,128)(2,1)}, bf16[2,2,4,16,512]{4,3,2,1,0:T(8,128)(2,1)}, bf16[2,2,4,16,512]{4,3,2,1,0:T(8,128)(2,1)}, bf16[...) custom-call(s32[16,32]{1,0:T(8,128)S(1)} %copy-done.10, ...), custom_call_target="tpu_custom_call" | custom-call | flops 1 | bytes 1 | tf_op jit(solution)/shard_map/gather_blocks/pallas_call | solution.py:68
  5.2 6.1 %collective-permute-start = (bf16[2,2,4,16,512]{4,3,2,1,0:T(8,128)(2,1)}, bf16[2,2,4,16,512]{4,3,2,1,0:T(8,128)(2,1)S(1)}, u32[]{:S(2)}, u32[]{:S(2)}) collective-permute-start(bf16[2,2,4,16,512]{4,3,2,1,0:T(8,128)(2,1)} %get-tuple-element.38), channel_id=1, source_target_pairs={{0,28},{4,24},{8,20},{12,16},{16,12},{20,8},{24,4},{28,0},{1,29},{... | collective-permute-start | bytes 786440 | tf_op jit(solution)/shard_map/ppermute | solution.py:503
  11.2 0.2 collective-permute-start.1
  11.5 0.7 collective-permute-start.2
  12.2 4.3 %collective-permute-start.3 = (bf16[2,2,4,16,512]{4,3,2,1,0:T(8,128)(2,1)}, bf16[2,2,4,16,512]{4,3,2,1,0:T(8,128)(2,1)S(1)}, u32[]{:S(2)}, u32[]{:S(2)}) collective-permute-start(bf16[2,2,4,16,512]{4,3,2,1,0:T(8,128)(2,1)} %get-tuple-element.41), channel_id=1, source_target_pairs={{0,12},{4,8},{8,4},{12,0},{16,28},{20,24},{24,20},{28,16},{1,13},{... | collective-permute-start | bytes 786440 | tf_op jit(solution)/shard_map/ppermute | solution.py:503
  16.5 0.0 collective-permute-start.4
  16.6 0.9 copy-done.3
  17.5 11.1 %project_qkv.1 = (f32[1024,512]{1,0:T(8,128)S(1)}, f32[1024,512]{1,0:T(8,128)S(1)}, bf16[1024,512]{1,0:T(8,128)(2,1)S(1)}, f32[8,1024]{1,0:T(8,128)S(1)}) custom-call(s32[16]{0:T(128)S(1)} %copy-done.13, s32[16]{0:T(128)S(1)} %copy-done.14, f32[1,128]{1,0:T(1,128)S(1)} %copy-done.16, f32[2,512,128]{2,1,0:T(8,128)S(1)} %copy-done.9, ...), custom_call_target="tpu_custom_call" | custom-call | flops 1 | bytes 1 | tf_op jit(solution)/shard_map/project_qkv/pallas_call | solution.py:214
  28.6 0.0 copy-start.1
  28.6 0.0 copy-start.7
  28.6 0.0 copy-start.11
  28.6 0.0 collective-permute-done.refs_2_.rest_1_
  28.7 12.2 %collective-permute-start.5 = (bf16[2,2,4,16,512]{4,3,2,1,0:T(8,128)(2,1)}, bf16[2,2,4,16,512]{4,3,2,1,0:T(8,128)(2,1)}, u32[]{:S(2)}, u32[]{:S(2)}) collective-permute-start(bf16[2,2,4,16,512]{4,3,2,1,0:T(8,128)(2,1)} %get-tuple-element.48), channel_id=1, source_target_pairs={{0,16},{4,20},{8,24},{12,28},{16,0},{20,4},{24,8},{28,12},{1,17},{... | collective-permute-start | bytes 786440 | tf_op jit(solution)/shard_map/ppermute | solution.py:503
  40.9 0.0 collective-permute-done.1.refs_3_.rest_2_
  40.9 1.5 %collective-permute-start.6 = (bf16[2,2,4,16,512]{4,3,2,1,0:T(8,128)(2,1)}, bf16[2,2,4,16,512]{4,3,2,1,0:T(8,128)(2,1)}, u32[]{:S(2)}, u32[]{:S(2)}) collective-permute-start(bf16[2,2,4,16,512]{4,3,2,1,0:T(8,128)(2,1)} %get-tuple-element.49), channel_id=1, source_target_pairs={{0,4},{4,0},{8,12},{12,8},{16,20},{20,16},{24,28},{28,24},{1,5},{5... | collective-permute-start | bytes 786440 | tf_op jit(solution)/shard_map/ppermute | solution.py:503
  42.4 3.1 %gather_blocks.3.refs_0_ = bf16[8,2,2,4,16,512]{5,4,3,2,1,0:T(8,128)(2,1)} custom-call(s32[16,32]{1,0:T(8,128)S(1)} %copy-done.11, s32[16]{0:T(128)S(1)} %copy-done.13, bf16[4,64,16,512]{3,2,1,0:T(8,128)(2,1)} %pool.3, bf16[2,2,4,16,512]{4,3,2,1,0:T(8,128)(2,1)S(1)} %copy-done.3), custom_call_target="tpu_custom_call" | custom-call | flops 1 | bytes 1 | tf_op jit(solution)/shard_map/gather_blocks/pallas_call | solution.py:68
  45.6 5.4 %all-gather = f32[32,1024]{1,0:T(8,128)S(1)} all-gather(f32[8,1024]{1,0:T(8,128)S(1)} %get-tuple-element.37), channel_id=2, replica_groups=mesh['req'=8,'tensor'=4] {'tensor'}, dimensions={0}, use_global_device_ids=true | all-gather | bytes 163840 | tf_op jit(solution)/shard_map/all_gather | solution.py:527
  51.0 2.6 %collective-permute-done.2.refs_4_.rest_3_ = bf16[2,2,4,16,512]{4,3,2,1,0:T(8,128)(2,1)S(1)} collective-permute-done((bf16[2,2,4,16,512]{4,3,2,1,0:T(8,128)(2,1)}, bf16[2,2,4,16,512]{4,3,2,1,0:T(8,128)(2,1)S(1)}, u32[]{:S(2)}, u32[]{:S(2)}) %collective-permute-start.2) | collective-permute-done | bytes 262176 | tf_op jit(solution)/shard_map/ppermute | solution.py:503
  53.6 6.9 %all-to-all-start = ((bf16[8,2,2,4,16,512]{5,4,3,2,1,0:T(8,128)(2,1)}), bf16[8,2,2,4,16,512]{5,4,3,2,1,0:T(8,128)(2,1)}, u32[]{:S(2)}, u32[]{:S(2)}) async-start(bf16[8,2,2,4,16,512]{5,4,3,2,1,0:T(8,128)(2,1)} %hold.2.rest_0_.rest_8_.rest_9_), calls=%async_computation | async-start | bytes 4194304 | tf_op jit(solution)/shard_map/all_to_all | solution.py:535
  60.5 0.0 copy-start.2
  60.5 1.6 %copy-done.2 = f32[1024,512]{1,0:T(8,128)S(1)} copy-done((f32[1024,512]{1,0:T(8,128)S(1)}, f32[1024,512]{1,0:T(8,128)}, u32[]{:S(2)}) %copy-start.2) | copy-done | bytes 2097176
  62.1 1.6 %copy-done.6 = f32[1024,512]{1,0:T(8,128)S(1)} copy-done((f32[1024,512]{1,0:T(8,128)S(1)}, f32[1024,512]{1,0:T(8,128)}, u32[]{:S(2)}) %copy-start.6) | copy-done | bytes 2097176
  63.7 1.2 %copy-done.8 = bf16[1024,512]{1,0:T(8,128)(2,1)S(1)} copy-done((bf16[1024,512]{1,0:T(8,128)(2,1)S(1)}, bf16[1024,512]{1,0:T(8,128)(2,1)}, u32[]{:S(2)}) %copy-start.8) | copy-done | bytes 1048600
  64.9 3.9 %attend_new.1 = (bf16[1024,512]{1,0:T(8,128)(2,1)S(1)}, f32[512,1024]{1,0:T(8,128)S(1)}, f32[8,1024]{1,0:T(8,128)S(1)}) custom-call(f32[1024,512]{1,0:T(8,128)S(1)} %copy-done.2, f32[1024,512]{1,0:T(8,128)S(1)} %copy-done.6, bf16[1024,512]{1,0:T(8,128)(2,1)S(1)} %copy-done.8, f32[4,8,1024]{2,1,0:T(8,128)S(1)} %bitcast.5, ...), custom_call_target="tpu_custom_call" | custom-call | flops 1 | bytes 1 | tf_op jit(solution)/shard_map/attend_new/pallas_call | solution.py:297
  68.8 6.3 %attend_old.2 = (bf16[4,2,4,8,16,512]{5,4,3,2,1,0:T(8,128)(2,1)}, bf16[512,512]{1,0:T(8,128)(2,1)S(1)}, bf16[512,512]{1,0:T(8,128)(2,1)S(1)}, bf16[512,512]{1,0:T(8,128)(2,1)S(1)}, bf16[512,512]{1,0:T(8,128)(2,1)S(1)}) custom-call(s32[16]{0:T(128)S(1)} %copy-done.13, s32[16]{0:T(128)S(1)} %copy-done.14, bf16[1024,512]{1,0:T(8,128)(2,1)S(1)} %get-tuple-element.43.q, ...), custom_call_target="tpu_custom_call" | custom-call | flops 999999995904 | bytes 999999995904 | tf_op jit(solution)/shard_map/attend_old/pallas_call | solution.py:382
  75.1 0.1 collective-permute-start.7
  75.2 1.9 %collective-permute-done.7.second = bf16[512,512]{1,0:T(8,128)(2,1)S(1)} collective-permute-done((bf16[512,512]{1,0:T(8,128)(2,1)S(1)}, bf16[512,512]{1,0:T(8,128)(2,1)S(1)}, u32[]{:S(2)}, u32[]{:S(2)}) %collective-permute-start.7) | collective-permute-done | bytes 524320 | tf_op jit(solution)/shard_map/ppermute | solution.py:503
  77.1 0.1 add_terms.2.rest_10_
  77.2 1.6 %collective-permute-start.10 = (bf16[512,512]{1,0:T(8,128)(2,1)S(1)}, bf16[512,512]{1,0:T(8,128)(2,1)S(1)}, u32[]{:S(2)}, u32[]{:S(2)}) collective-permute-start(bf16[512,512]{1,0:T(8,128)(2,1)S(1)} %add_terms.2.rest_10_), channel_id=1, source_target_pairs={{0,2},{1,3},{2,0},{3,1},{4,6},{5,7},{6,4},{7,5},{8,10},{9,11},{10,... | collective-permute-start | bytes 1572872 | tf_op jit(solution)/shard_map/ppermute | solution.py:503
  78.8 6.3 %attend_old.3 = (bf16[4,2,4,8,16,512]{5,4,3,2,1,0:T(8,128)(2,1)}, bf16[512,512]{1,0:T(8,128)(2,1)S(1)}, bf16[512,512]{1,0:T(8,128)(2,1)S(1)}, bf16[512,512]{1,0:T(8,128)(2,1)S(1)}, bf16[512,512]{1,0:T(8,128)(2,1)S(1)}) custom-call(s32[16]{0:T(128)S(1)} %copy-done.13, s32[16]{0:T(128)S(1)} %copy-done.14, ...), custom_call_target="tpu_custom_call", output_to_operand_aliasing={{0}: (14, {})} | custom-call | flops 1 | bytes 1 | tf_op jit(solution)/shard_map/attend_old/pallas_call | solution.py:382
  85.1 0.0 copy-start.17
  85.1 0.1 collective-permute-start.9
  85.2 0.5 collective-permute-start.12
  85.7 0.1 collective-permute-start.8
  85.8 5.5 %collective-permute-done.10.rest_0_.third = bf16[512,512]{1,0:T(8,128)(2,1)S(1)} collective-permute-done((bf16[512,512]{1,0:T(8,128)(2,1)S(1)}, bf16[512,512]{1,0:T(8,128)(2,1)S(1)}, u32[]{:S(2)}, u32[]{:S(2)}) %collective-permute-start.10) | collective-permute-done | bytes 524320 | tf_op jit(solution)/shard_map/ppermute | solution.py:503
  91.3 0.1 add_terms.3
  91.4 1.6 %collective-permute-start.11 = (bf16[512,512]{1,0:T(8,128)(2,1)S(1)}, bf16[512,512]{1,0:T(8,128)(2,1)S(1)}, u32[]{:S(2)}, u32[]{:S(2)}) collective-permute-start(bf16[512,512]{1,0:T(8,128)(2,1)S(1)} %add_terms.3), channel_id=1, source_target_pairs={{0,2},{1,3},{2,0},{3,1},{4,6},{5,7},{6,4},{7,5},{8,10},{9,11},{10,... | collective-permute-start | bytes 1572872 | tf_op jit(solution)/shard_map/ppermute | solution.py:503
  93.0 0.3 total_terms.2
  93.3 11.4 %collective-permute-done.11.third = bf16[512,512]{1,0:T(8,128)(2,1)S(1)} collective-permute-done((bf16[512,512]{1,0:T(8,128)(2,1)S(1)}, bf16[512,512]{1,0:T(8,128)(2,1)S(1)}, u32[]{:S(2)}, u32[]{:S(2)}) %collective-permute-start.11) | collective-permute-done | bytes 524320 | tf_op jit(solution)/shard_map/ppermute | solution.py:503
  104.7 0.3 total_terms.3
  105.0 5.2 %all-gather.1 = f32[32,512]{1,0:T(8,128)S(1)} all-gather(f32[8,512]{1,0:T(8,128)S(1)} %get-tuple-element.60), channel_id=3, replica_groups=mesh['req'=8,'tensor'=4] {'tensor'}, dimensions={0}, use_global_device_ids=true | all-gather | bytes 81920 | tf_op jit(solution)/shard_map/all_gather | solution.py:565
  110.3 2.4 %finish_layer.1 = bf16[2,512,512]{2,1,0:T(8,128)(2,1)} custom-call(bf16[2,512,2048]{2,1,0:T(8,128)(2,1)} %residual.1, f32[4,8,512]{2,1,0:T(8,128)S(1)} %bitcast.6, bf16[1,512]{1,0:T(2,128)(2,1)S(1)} %reshape.14.gain, f32[512,512]{1,0:T(8,128)S(1)} %get-tuple-element.61.rest_0_, f32[512,512]{1,0:T(8,128)S(1)} %get-tuple-element.62.rest_1_), custom_call_target="tpu_custom_call" | custom-call | flops 1 | bytes 1 | tf_op jit(solution)/shard_map/finish_layer/pallas_call | solution.py:484
  112.7 2.9 %place_blocks.1 = bf16[4,2,4,8,16,512]{5,4,3,2,1,0:T(8,128)(2,1)} custom-call(bf16[4,2,4,8,16,512]{5,4,3,2,1,0:T(8,128)(2,1)} %get-tuple-element.63.rest_0_, bf16[8,2,2,4,16,512]{5,4,3,2,1,0:T(8,128)(2,1)} %all-to-all-done.rest_1_), custom_call_target="tpu_custom_call", output_to_operand_aliasing={{}: (0, {})} | custom-call | flops 1 | bytes 1 | tf_op jit(solution)/shard_map/place_blocks/pallas_call | solution.py:101
  (33 shorter events, 0.1 us)
Async XLA Ops:
  0.6 15.9 %copy-start.16 = (f32[1,128]{1,0:T(1,128)S(1)}, f32[1,128]{1,0:T(1,128)}, u32[]{:S(2)}) copy-start(f32[1,128]{1,0:T(1,128)} %constant.4.clone.frequency) | copy-start | bytes 1540
  0.6 15.9 %copy-start.9 = (f32[2,512,128]{2,1,0:T(8,128)S(1)}, f32[2,512,128]{2,1,0:T(8,128)}, u32[]{:S(2)}) copy-start(f32[2,512,128]{2,1,0:T(8,128)} %constant.5.clone.steps) | copy-start | bytes 1572868
  0.7 0.8 copy-start.10
  1.4 0.7 copy-start.12
  2.1 14.5 %copy-start.13 = (s32[16]{0:T(128)S(1)}, s32[16]{0:T(128)}, u32[]{:S(2)}) copy-start(s32[16]{0:T(128)} %order.9) | copy-start | bytes 196
  2.1 14.5 %copy-start.14 = (s32[16]{0:T(128)S(1)}, s32[16]{0:T(128)}, u32[]{:S(2)}) copy-start(s32[16]{0:T(128)} %lengths.5) | copy-start | bytes 196
  2.1 14.5 %copy-start.15 = (bf16[2,512]{1,0:T(2,128)(2,1)S(1)}, bf16[2,512]{1,0:T(2,128)(2,1)}, u32[]{:S(2)}) copy-start(bf16[2,512]{1,0:T(2,128)(2,1)} %gain.1) | copy-start | bytes 6148
  5.2 23.5 %collective-permute-start = (bf16[2,2,4,16,512]{4,3,2,1,0:T(8,128)(2,1)}, bf16[2,2,4,16,512]{4,3,2,1,0:T(8,128)(2,1)S(1)}, u32[]{:S(2)}, u32[]{:S(2)}) collective-permute-start(bf16[2,2,4,16,512]{4,3,2,1,0:T(8,128)(2,1)} %get-tuple-element.38), channel_id=1, source_target_pairs={{0,28},{4,24},{8,20},{12,16},{16,12},{20,8},{24,4},{28,0},{1,29},{... | collective-permute-start | bytes 786440 | tf_op jit(solution)/shard_map/ppermute | solution.py:503
  11.2 29.7 %collective-permute-start.1 = (bf16[2,2,4,16,512]{4,3,2,1,0:T(8,128)(2,1)}, bf16[2,2,4,16,512]{4,3,2,1,0:T(8,128)(2,1)S(1)}, u32[]{:S(2)}, u32[]{:S(2)}) collective-permute-start(bf16[2,2,4,16,512]{4,3,2,1,0:T(8,128)(2,1)} %get-tuple-element.39), channel_id=1, source_target_pairs={{0,24},{4,28},{8,16},{12,20},{16,8},{20,12},{24,0},{28,4},{1,25},{... | collective-permute-start | bytes 786440 | tf_op jit(solution)/shard_map/ppermute | solution.py:503
  11.5 42.1 %collective-permute-start.2 = (bf16[2,2,4,16,512]{4,3,2,1,0:T(8,128)(2,1)}, bf16[2,2,4,16,512]{4,3,2,1,0:T(8,128)(2,1)S(1)}, u32[]{:S(2)}, u32[]{:S(2)}) collective-permute-start(bf16[2,2,4,16,512]{4,3,2,1,0:T(8,128)(2,1)} %get-tuple-element.40), channel_id=1, source_target_pairs={{0,20},{4,16},{8,28},{12,24},{16,4},{20,0},{24,12},{28,8},{1,21},{... | collective-permute-start | bytes 786440 | tf_op jit(solution)/shard_map/ppermute | solution.py:503
  12.2 41.4 %collective-permute-start.3 = (bf16[2,2,4,16,512]{4,3,2,1,0:T(8,128)(2,1)}, bf16[2,2,4,16,512]{4,3,2,1,0:T(8,128)(2,1)S(1)}, u32[]{:S(2)}, u32[]{:S(2)}) collective-permute-start(bf16[2,2,4,16,512]{4,3,2,1,0:T(8,128)(2,1)} %get-tuple-element.41), channel_id=1, source_target_pairs={{0,12},{4,8},{8,4},{12,0},{16,28},{20,24},{24,20},{28,16},{1,13},{... | collective-permute-start | bytes 786440 | tf_op jit(solution)/shard_map/ppermute | solution.py:503
  16.5 37.1 %collective-permute-start.4 = (bf16[2,2,4,16,512]{4,3,2,1,0:T(8,128)(2,1)}, bf16[2,2,4,16,512]{4,3,2,1,0:T(8,128)(2,1)S(1)}, u32[]{:S(2)}, u32[]{:S(2)}) collective-permute-start(bf16[2,2,4,16,512]{4,3,2,1,0:T(8,128)(2,1)} %get-tuple-element.42), channel_id=1, source_target_pairs={{0,8},{4,12},{8,0},{12,4},{16,24},{20,28},{24,16},{28,20},{1,9},{5... | collective-permute-start | bytes 786440 | tf_op jit(solution)/shard_map/ppermute | solution.py:503
  16.6 1.0 copy-start.3
  28.6 17.0 %copy-start.1 = (f32[1024,512]{1,0:T(8,128)}, f32[1024,512]{1,0:T(8,128)S(1)}, u32[]{:S(2)}) copy-start(f32[1024,512]{1,0:T(8,128)S(1)} %get-tuple-element.34.q.refs_2_) | copy-start | bytes 6291460
  28.6 17.0 %copy-start.5 = (f32[1024,512]{1,0:T(8,128)}, f32[1024,512]{1,0:T(8,128)S(1)}, u32[]{:S(2)}) copy-start(f32[1024,512]{1,0:T(8,128)S(1)} %get-tuple-element.35.k) | copy-start | bytes 6291460
  28.6 17.0 %copy-start.7 = (bf16[1024,512]{1,0:T(8,128)(2,1)}, bf16[1024,512]{1,0:T(8,128)(2,1)S(1)}, u32[]{:S(2)}) copy-start(bf16[1024,512]{1,0:T(8,128)(2,1)S(1)} %get-tuple-element.36.v) | copy-start | bytes 3145732
  28.6 13.8 %copy-start.11 = (s32[16,32]{1,0:T(8,128)S(1)}, s32[16,32]{1,0:T(8,128)}, u32[]{:S(2)}) copy-start(s32[16,32]{1,0:T(8,128)} %table.3) | copy-start | bytes 6148
  28.7 40.1 %collective-permute-start.5 = (bf16[2,2,4,16,512]{4,3,2,1,0:T(8,128)(2,1)}, bf16[2,2,4,16,512]{4,3,2,1,0:T(8,128)(2,1)}, u32[]{:S(2)}, u32[]{:S(2)}) collective-permute-start(bf16[2,2,4,16,512]{4,3,2,1,0:T(8,128)(2,1)} %get-tuple-element.48), channel_id=1, source_target_pairs={{0,16},{4,20},{8,24},{12,28},{16,0},{20,4},{24,8},{28,12},{1,17},{... | collective-permute-start | bytes 786440 | tf_op jit(solution)/shard_map/ppermute | solution.py:503
  40.9 27.9 %collective-permute-start.6 = (bf16[2,2,4,16,512]{4,3,2,1,0:T(8,128)(2,1)}, bf16[2,2,4,16,512]{4,3,2,1,0:T(8,128)(2,1)}, u32[]{:S(2)}, u32[]{:S(2)}) collective-permute-start(bf16[2,2,4,16,512]{4,3,2,1,0:T(8,128)(2,1)} %get-tuple-element.49), channel_id=1, source_target_pairs={{0,4},{4,0},{8,12},{12,8},{16,20},{20,16},{24,28},{28,24},{1,5},{5... | collective-permute-start | bytes 786440 | tf_op jit(solution)/shard_map/ppermute | solution.py:503
  53.6 6.9 %copy-start = (bf16[8,2,2,4,16,512]{5,4,3,2,1,0:T(8,128)(2,1)S(1)}, bf16[8,2,2,4,16,512]{5,4,3,2,1,0:T(8,128)(2,1)}, u32[]{:S(2)}) copy-start(bf16[8,2,2,4,16,512]{5,4,3,2,1,0:T(8,128)(2,1)} %hold.2.rest_0_.rest_8_.rest_9_) | copy-start | bytes 6291460
  53.6 59.1 %all-to-all-start = ((bf16[8,2,2,4,16,512]{5,4,3,2,1,0:T(8,128)(2,1)}), bf16[8,2,2,4,16,512]{5,4,3,2,1,0:T(8,128)(2,1)}, u32[]{:S(2)}, u32[]{:S(2)}) async-start(bf16[8,2,2,4,16,512]{5,4,3,2,1,0:T(8,128)(2,1)} %hold.2.rest_0_.rest_8_.rest_9_), calls=%async_computation | async-start | bytes 4194304 | tf_op jit(solution)/shard_map/all_to_all | solution.py:535
  60.5 1.6 %copy-start.2 = (f32[1024,512]{1,0:T(8,128)S(1)}, f32[1024,512]{1,0:T(8,128)}, u32[]{:S(2)}) copy-start(f32[1024,512]{1,0:T(8,128)} %copy-done.1) | copy-start | bytes 6291460
  62.1 1.6 %copy-start.6 = (f32[1024,512]{1,0:T(8,128)S(1)}, f32[1024,512]{1,0:T(8,128)}, u32[]{:S(2)}) copy-start(f32[1024,512]{1,0:T(8,128)} %copy-done.5) | copy-start | bytes 6291460
  63.7 1.2 %copy-start.8 = (bf16[1024,512]{1,0:T(8,128)(2,1)S(1)}, bf16[1024,512]{1,0:T(8,128)(2,1)}, u32[]{:S(2)}) copy-start(bf16[1024,512]{1,0:T(8,128)(2,1)} %copy-done.7) | copy-start | bytes 3145732
  64.9 3.9 %copy-start.4 = (bf16[2,2,4,16,512]{4,3,2,1,0:T(8,128)(2,1)S(1)}, bf16[2,2,4,16,512]{4,3,2,1,0:T(8,128)(2,1)}, u32[]{:S(2)}) copy-start(bf16[2,2,4,16,512]{4,3,2,1,0:T(8,128)(2,1)} %get-tuple-element.33.rest_0_) | copy-start | bytes 786436
  75.1 2.0 %collective-permute-start.7 = (bf16[512,512]{1,0:T(8,128)(2,1)S(1)}, bf16[512,512]{1,0:T(8,128)(2,1)S(1)}, u32[]{:S(2)}, u32[]{:S(2)}) collective-permute-start(bf16[512,512]{1,0:T(8,128)(2,1)S(1)} %get-tuple-element.52), channel_id=1, source_target_pairs={{0,1},{1,0},{2,3},{3,2},{4,5},{5,4},{6,7},{7,6},{8,9},{9,8},{10,11... | collective-permute-start | bytes 1572872 | tf_op jit(solution)/shard_map/ppermute | solution.py:503
  77.2 14.0 %collective-permute-start.10 = (bf16[512,512]{1,0:T(8,128)(2,1)S(1)}, bf16[512,512]{1,0:T(8,128)(2,1)S(1)}, u32[]{:S(2)}, u32[]{:S(2)}) collective-permute-start(bf16[512,512]{1,0:T(8,128)(2,1)S(1)} %add_terms.2.rest_10_), channel_id=1, source_target_pairs={{0,2},{1,3},{2,0},{3,1},{4,6},{5,7},{6,4},{7,5},{8,10},{9,11},{10,... | collective-permute-start | bytes 1572872 | tf_op jit(solution)/shard_map/ppermute | solution.py:503
  85.1 7.8 %copy-start.17 = (bf16[512]{0:T(512)(128)(2,1)S(1)}, bf16[512]{0:T(512)(128)(2,1)}, u32[]{:S(2)}) copy-start(bf16[512]{0:T(512)(128)(2,1)} %param.15) | copy-start | bytes 3076
  85.1 6.1 %collective-permute-start.9 = (bf16[512,512]{1,0:T(8,128)(2,1)S(1)}, bf16[512,512]{1,0:T(8,128)(2,1)S(1)}, u32[]{:S(2)}, u32[]{:S(2)}) collective-permute-start(bf16[512,512]{1,0:T(8,128)(2,1)S(1)} %get-tuple-element.56), channel_id=1, source_target_pairs={{0,1},{1,0},{2,3},{3,2},{4,5},{5,4},{6,7},{7,6},{8,9},{9,8},{10,11... | collective-permute-start | bytes 1572872 | tf_op jit(solution)/shard_map/ppermute | solution.py:503
  85.2 7.8 %collective-permute-start.12 = (bf16[512,512]{1,0:T(8,128)(2,1)S(1)}, bf16[512,512]{1,0:T(8,128)(2,1)S(1)}, u32[]{:S(2)}, u32[]{:S(2)}) collective-permute-start(bf16[512,512]{1,0:T(8,128)(2,1)S(1)} %get-tuple-element.58), channel_id=1, source_target_pairs={{0,1},{1,0},{2,3},{3,2},{4,5},{5,4},{6,7},{7,6},{8,9},{9,8},{10,11... | collective-permute-start | bytes 1572872 | tf_op jit(solution)/shard_map/ppermute | solution.py:503
  85.7 7.6 %collective-permute-start.8 = (bf16[512,512]{1,0:T(8,128)(2,1)S(1)}, bf16[512,512]{1,0:T(8,128)(2,1)S(1)}, u32[]{:S(2)}, u32[]{:S(2)}) collective-permute-start(bf16[512,512]{1,0:T(8,128)(2,1)S(1)} %get-tuple-element.54), channel_id=1, source_target_pairs={{0,1},{1,0},{2,3},{3,2},{4,5},{5,4},{6,7},{7,6},{8,9},{9,8},{10,11... | collective-permute-start | bytes 1572872 | tf_op jit(solution)/shard_map/ppermute | solution.py:503
  91.4 13.3 %collective-permute-start.11 = (bf16[512,512]{1,0:T(8,128)(2,1)S(1)}, bf16[512,512]{1,0:T(8,128)(2,1)S(1)}, u32[]{:S(2)}, u32[]{:S(2)}) collective-permute-start(bf16[512,512]{1,0:T(8,128)(2,1)S(1)} %add_terms.3), channel_id=1, source_target_pairs={{0,2},{1,3},{2,0},{3,1},{4,6},{5,7},{6,4},{7,5},{8,10},{9,11},{10,... | collective-permute-start | bytes 1572872 | tf_op jit(solution)/shard_map/ppermute | solution.py:503

commit v3 on v2

--- a/solution.py
+++ b/solution.py
@@ -36,8 +36,11 @@
 
 
 def gather_body(targets, first, planes, count, per_device, blocks, together, table, order, pool, *rest):
-    held, loaded, stored = rest[-3:]
-    outs = rest[-4:-3] if together else rest[-3 - len(targets) : -3]
+    if together:
+        out, held, stored, loaded = rest[-4:]
+        places = [held.at[at] for at in range(len(targets))]
+    else:
+        places, loaded = rest[-1 - len(targets) : -1], rest[-1]
     me = lax.axis_index("req")
     for at, target in enumerate(targets):
         if not together:
@@ -47,14 +50,14 @@
             for b in range(blocks):
                 slot = table[request, b * count + me]
                 pltpu.make_async_copy(
-                    pool.at[pl.ds(first, planes), slot], held.at[at, :, p, b], loaded.at[at]
+                    pool.at[pl.ds(first, planes), slot], places[at].at[:, p, b], loaded.at[at]
                 ).start()
     stores = []
-    for at in range(len(targets)):
-        pltpu.make_async_copy(held.at[at], held.at[at], loaded.at[at]).wait()
-        place = outs[0].at[at] if together else outs[at]
-        stores.append(pltpu.make_async_copy(held.at[at], place, stored.at[at]))
-        stores[-1].start()
+    for at, place in enumerate(places):
+        pltpu.make_async_copy(place, place, loaded.at[at]).wait()
+        if together:
+            stores.append(pltpu.make_async_copy(place, out.at[at], stored.at[at]))
+            stores[-1].start()
     for store in stores:
         store.wait()
 
@@ -64,21 +67,22 @@
     blocks = table.shape[1] // count
     piece = (planes, per_device, blocks) + pool.shape[2:]
     whole = (len(targets),) + piece
-    shapes = [whole] if together else [piece] * len(targets)
+    if together:
+        shapes = [pltpu.HBM(whole, pool.dtype)]
+        staging = [pltpu.VMEM(whole, pool.dtype), pltpu.SemaphoreType.DMA((len(targets),))]
+    else:
+        shapes = [pltpu.VMEM(piece, pool.dtype)] * len(targets)
+        staging = []
     return pl.pallas_call(
         functools.partial(gather_body, targets, first, planes, count, per_device, blocks, together),
         in_specs=[SMEM, SMEM, ANY] + [ANY] * len(after),
-        out_specs=[ANY] * len(shapes),
-        out_shape=[pltpu.HBM(shape, pool.dtype) for shape in shapes],
-        scratch_shapes=[
-            pltpu.VMEM(whole, pool.dtype),
-            pltpu.SemaphoreType.DMA((len(targets),)),
-            pltpu.SemaphoreType.DMA((len(targets),)),
-        ],
+        out_specs=[ANY if together else VMEM] * len(shapes),
+        out_shape=shapes,
+        scratch_shapes=staging + [pltpu.SemaphoreType.DMA((len(targets),))],
         cost_estimate=cost(0, 4 * math.prod(whole)),
         compiler_params=params(8),
         name="gather_blocks",
-    )(table, order, *in_hbm(pool), *after)
+    )(*in_hbm(table, order, pool), *after)
 
 
 def place_body(offsets, first, planes, together, filled, *rest):
@@ -119,17 +123,17 @@
     pass
 
 
-def hold(values, after):
+def hold(values, after, pin=pltpu.HBM):
     return pl.pallas_call(
         hold_body,
         in_specs=[ANY] * (len(values) + len(after)),
         out_specs=[ANY] * len(values),
-        out_shape=[pltpu.HBM(value.shape, value.dtype) for value in values],
+        out_shape=[pin(value.shape, value.dtype) for value in values],
         input_output_aliases={at: at for at in range(len(values))},
         cost_estimate=cost(0, 0),
         compiler_params=params(1),
         name="hold",
-    )(*in_hbm(*values), *after)
+    )(*[pltpu.with_memory_space_constraint(value, pin) for value in values], *after)
 
 
 def turned(values, cosine, sine):
@@ -159,7 +163,9 @@
 
 
 def project_body(per_device, block, after, order, lengths, frequency, steps, gain, x, w, *rest):
-    q_out, k_out, v_out, squares, x_held, w_held, x_loaded, w_loaded = rest[after:]
+    outs, squares, x_held, w_held, *rest = rest[after : after + 3], *rest[after + 3 :]
+    helds, (x_loaded, w_loaded, stored) = rest[:3], rest[3:]
+    stores = []
     rows = x.shape[0]
     span = rows // per_device
     w_loads = [
@@ -178,7 +184,8 @@
         length = request_length(p, per_device, order, lengths).astype(jnp.float32)
         angle = length * frequency[...]
         starts.append((jnp.cos(angle), jnp.sin(angle)))
-    for which, out in ((0, q_out), (1, k_out), (2, v_out)):
+        squares[2:3, p * span : (p + 1) * span] = jnp.full((1, span), length)
+    for which, out in enumerate(helds):
         w_loads[which].wait()
         for low in range(0, rows, block):
             if which == 0:
@@ -201,6 +208,10 @@
                 folded += squared[:, at : at + HD]
             squares[which : which + 1, here] = jnp.sum(jnp.transpose(folded), axis=0, keepdims=True)
             out[here] = turned(raw * gain[which : which + 1].astype(jnp.float32), cosine, sine)
+        stores.append(pltpu.make_async_copy(out, outs[which], stored.at[which]))
+        stores[-1].start()
+    for store in stores:
+        store.wait()
 
 
 def project(per_device, order, lengths, x, w, gain, after=(), block=256):
@@ -214,31 +225,51 @@
     return pl.pallas_call(
         functools.partial(project_body, per_device, block, len(after)),
         in_specs=[SMEM, SMEM, VMEM, VMEM, VMEM, ANY, ANY] + [ANY] * len(after),
-        out_specs=[VMEM] * 4,
+        out_specs=[ANY] * 3 + [VMEM],
         out_shape=[
+            pltpu.HBM((rows, width), jnp.float32),
+            pltpu.HBM((rows, width), jnp.float32),
+            pltpu.HBM((rows, width), jnp.bfloat16),
+            jax.ShapeDtypeStruct((8, rows), jnp.float32),
+        ],
+        scratch_shapes=[
+            pltpu.VMEM(x.shape, x.dtype),
+            pltpu.VMEM(w.shape, w.dtype),
             pltpu.VMEM((rows, width), jnp.float32),
             pltpu.VMEM((rows, width), jnp.float32),
             pltpu.VMEM((rows, width), jnp.bfloat16),
-            jax.ShapeDtypeStruct((8, rows), jnp.float32),
-        ],
-        scratch_shapes=[
-            pltpu.VMEM(x.shape, x.dtype),
-            pltpu.VMEM(w.shape, w.dtype),
             pltpu.SemaphoreType.DMA((rows // block,)),
             pltpu.SemaphoreType.DMA((3,)),
+            pltpu.SemaphoreType.DMA((3,)),
         ],
         cost_estimate=cost(1, 1),
-        compiler_params=params(20),
+        compiler_params=params(24),
         name="project_qkv",
-    )(order, lengths, jnp.asarray(frequency), jnp.asarray(steps), gain, *in_hbm(x, w), *after)
+    )(*in_hbm(order, lengths), jnp.asarray(frequency), jnp.asarray(steps), gain, *in_hbm(x, w), *after)
 
 
 CONTRACT = (((1,), (1,)), ((), ()))
 
 
-def attend_new_body(full_width, span, q_block, after, q, k, v, squares, *rest):
-    q_out, mixed_out, state = rest[after:]
+def attend_new_body(full_width, span, q_block, after, squares, *rest):
+    sources, rest = rest[:3], rest[3 + after :]
+    q_final, mixed_final, state, *helds, q_out, mixed_out, loaded, stored = rest
+    q, k, v = helds
+    stores = []
     heads = q.shape[1] // HD
+    loads = []
+    for base in range(0, q.shape[0], span):
+        at = pl.ds(base, span)
+        number = base // span
+        loads.append(
+            [
+                pltpu.make_async_copy(source.at[at], held.at[at], loaded.at[number, which])
+                for which, (source, held) in enumerate(zip(sources, helds))
+            ]
+        )
+        for load in loads[-1]:
+            load.start()
+    state[2 * heads : 2 * heads + 1] = squares[0, 2:3]
     total = squares[0]
     for at in range(1, squares.shape[0]):
         total += squares[at]
@@ -250,6 +281,8 @@
         scales = as_columns(factors[:, here])
         q_scale = scales[:, 0:1] * (HD**-0.5 * math.log2(math.e))
         k_scale = scales[:, 1:2]
+        for load in loads[base // span]:
+            load.wait()
         for head in range(heads):
             columns = slice(head * HD, (head + 1) * HD)
             queries = (q[here, columns] * q_scale).astype(jnp.bfloat16)
@@ -285,47 +318,70 @@
                         full.astype(jnp.bfloat16),
                         preferred_element_type=jnp.float32,
                     )
-                mixed_out[columns, place] = mixed
+                mixed_out[base // span, columns, low:high] = mixed
                 state[head : head + 1, place] = top
                 state[heads + head : heads + head + 1, place] = total
+        for at, (held, final) in enumerate(((q_out.at[here], q_final.at[here]), (mixed_out.at[base // span], mixed_final.at[base // span]))):
+            stores.append(pltpu.make_async_copy(held, final, stored.at[base // span, at]))
+            stores[-1].start()
+    for store in stores:
+        store.wait()
 
 
 def attend_new(full_width, span, q, k, v, squares, after=(), q_block=256):
     rows, width = q.shape
     q_block = min(q_block, span)
-    stats = 2 * (width // HD)
+    stats = 2 * (width // HD) + 8
     return pl.pallas_call(
         functools.partial(attend_new_body, full_width, span, q_block, len(after)),
-        in_specs=[VMEM] * 4 + [ANY] * len(after),
-        out_specs=[VMEM] * 3,
+        in_specs=[VMEM] + [ANY] * (3 + len(after)),
+        out_specs=[ANY, ANY, VMEM],
         out_shape=[
+            pltpu.HBM((rows, width), jnp.bfloat16),
+            pltpu.HBM((rows // span, width, span), jnp.float32),
+            jax.ShapeDtypeStruct((stats, rows), jnp.float32),
+        ],
+        scratch_shapes=[
+            pltpu.VMEM(q.shape, q.dtype),
+            pltpu.VMEM(k.shape, k.dtype),
+            pltpu.VMEM(v.shape, v.dtype),
             pltpu.VMEM((rows, width), jnp.bfloat16),
-            pltpu.VMEM((width, rows), jnp.float32),
-            pltpu.VMEM((stats, rows), jnp.float32),
+            pltpu.VMEM((rows // span, width, span), jnp.float32),
+            pltpu.SemaphoreType.DMA((rows // span, 3)),
+            pltpu.SemaphoreType.DMA((rows // span, 2)),
         ],
         cost_estimate=cost(1, 1),
-        compiler_params=params(16),
+        compiler_params=params(20),
         name="attend_new",
-    )(*in_vmem(q, k, v), squares, *after)
-
-
-def attend_old_body(which, span, offsets, q_block, filled, after, order, lengths, q, mixed, state, w, *rest):
-    received, rest = rest[: len(offsets)], rest[len(offsets) :]
-    rest = rest[int(filled) + after :]
-    relaid, outs = rest[0], rest[1:-6]
-    held, w_held, attended, loaded, w_loaded, stored = rest[-6:]
+    )(squares, *in_hbm(q, k, v), *after)
+
+
+def attend_old_body(which, span, offsets, q_block, filled, after, state, q_all, mixed_all, w, *rest):
+    received, rest = rest[: len(offsets)], rest[len(offsets) + int(filled) + after :]
+    relaid, outs = rest[0], rest[1:-9]
+    held, q, mixed, w_held, attended, loaded, q_loaded, w_loaded, stored = rest[-9:]
     me = lax.axis_index("req")
-    for at, offset in enumerate(offsets):
-        pltpu.make_async_copy(received[at].at[:, which], held.at[:, :, me ^ offset], loaded).start()
+    q_load = pltpu.make_async_copy(q_all.at[pl.ds(which * span, span)], q, q_loaded.at[0])
+    mixed_load = pltpu.make_async_copy(mixed_all.at[which], mixed, q_loaded.at[1])
     w_load = pltpu.make_async_copy(w, w_held, w_loaded)
+    q_load.start()
+    for plane in range(held.shape[0]):
+        for at, offset in enumerate(offsets):
+            pltpu.make_async_copy(
+                received[at].at[plane, which], held.at[plane, :, me ^ offset], loaded.at[plane]
+            ).start()
+    mixed_load.start()
     w_load.start()
-    pltpu.make_async_copy(held, held, loaded).wait()
+    q_load.wait()
+    for plane in range(held.shape[0]):
+        pltpu.make_async_copy(held.at[plane], held.at[plane], loaded.at[plane]).wait()
+    mixed_load.wait()
     store = pltpu.make_async_copy(held, relaid.at[pl.ds(0, held.shape[0]), which], stored)
     store.start()
     context = math.prod(held.shape[1:4])
-    length = request_length(which, q.shape[0] // span, order, lengths)
-    live = lax.broadcasted_iota(jnp.int32, (context, q_block), 0) < length
+    token = lax.broadcasted_iota(jnp.int32, (context, q_block), 0).astype(jnp.float32)
     heads = q.shape[1] // HD
+    live = token < state[2 * heads : 2 * heads + 1, which * span : which * span + q_block]
     for head in range(heads):
         columns = slice(head * HD, (head + 1) * HD)
         keys = held[0, :, :, :, columns].reshape(context, HD)
@@ -333,7 +389,7 @@
         for low in range(0, span, q_block):
             rows = slice(which * span + low, which * span + low + q_block)
             scores = lax.dot_general(
-                keys, q[rows, columns], CONTRACT, preferred_element_type=jnp.float32
+                keys, q[low : low + q_block, columns], CONTRACT, preferred_element_type=jnp.float32
             )
             scores = jnp.where(live, scores, -1e30)
             before = state[head : head + 1, rows]
@@ -342,7 +398,7 @@
             shrink = jnp.exp2(before - top)
             total = state[heads + head : heads + head + 1, rows] * shrink
             total += jnp.sum(scores, axis=0, keepdims=True)
-            sums = mixed[columns, rows] * shrink
+            sums = mixed[columns, low : low + q_block] * shrink
             sums += jnp.dot(values, scores.astype(jnp.bfloat16), preferred_element_type=jnp.float32)
             attended[low : low + q_block, columns] = jnp.transpose((sums / total)).astype(attended.dtype)
     w_load.wait()
@@ -359,8 +415,6 @@
 def attend_old(
     which,
     span,
-    order,
-    lengths,
     q,
     mixed,
     state,
@@ -383,22 +437,25 @@
         functools.partial(
             attend_old_body, which, span, offsets, q_block, filled is not None, len(after)
         ),
-        in_specs=[SMEM, SMEM, VMEM, VMEM, VMEM] + [ANY] * (1 + len(received) + len(start) + len(after)),
+        in_specs=[VMEM] + [ANY] * (3 + len(received) + len(start) + len(after)),
         out_specs=[ANY] + [VMEM] * count,
         out_shape=[pltpu.HBM(shape, dtype)] + [pltpu.VMEM((span, part), jnp.bfloat16)] * count,
         scratch_shapes=[
             pltpu.VMEM(received[0].shape[:1] + shape[2:], dtype),
+            pltpu.VMEM((span, width), q.dtype),
+            pltpu.VMEM((width, span), mixed.dtype),
             pltpu.VMEM(w.shape, w.dtype),
             pltpu.VMEM((span, width), jnp.bfloat16),
+            pltpu.SemaphoreType.DMA((received[0].shape[0],)),
+            pltpu.SemaphoreType.DMA((2,)),
             pltpu.SemaphoreType.DMA,
             pltpu.SemaphoreType.DMA,
-            pltpu.SemaphoreType.DMA,
-        ],
-        input_output_aliases={} if filled is None else {6 + len(received): 0},
+        ],
+        input_output_aliases={} if filled is None else {4 + len(received): 0},
         cost_estimate=pl.CostEstimate(flops=weight, bytes_accessed=weight, transcendentals=0),
         compiler_params=params(16),
         name="attend_old",
-    )(order, lengths, *in_vmem(q, mixed, state), *in_hbm(w), *received, *start, *after)
+    )(state, *in_hbm(q, mixed, w), *received, *start, *after)
 
 
 def add_body(first, second, *rest):
@@ -451,9 +508,9 @@
     )(*in_vmem(first, second, third), *squares)
 
 
-def finish_body(full_width, residual, squares, gain, *rest):
-    totals = rest[: len(rest) - 5]
-    out, res_held, out_held, loaded, stored = rest[len(rest) - 5 :]
+def finish_body(full_width, count, residual, gain, *rest):
+    squares, totals = rest[:count], rest[count:-5]
+    out, res_held, out_held, loaded, stored = rest[-5:]
     per_device, span, width = out.shape
     start = pl.multiple_of(lax.axis_index("tensor") * width, width)
     loads = [
@@ -462,9 +519,9 @@
     ]
     for load in loads:
         load.start()
-    total = squares[0]
-    for at in range(1, squares.shape[0]):
-        total += squares[at]
+    total = squares[0][...]
+    for part in squares[1:]:
+        total += part[...]
     scales = as_columns(lax.rsqrt(total / full_width + norm_eps))
     stores = []
     for p in range(per_device):
@@ -482,8 +539,8 @@
     width = totals[0].shape[1]
     shape = (per_device, span, width)
     return pl.pallas_call(
-        functools.partial(finish_body, full_width),
-        in_specs=[ANY] + [VMEM] * (2 + per_device),
+        functools.partial(finish_body, full_width, len(squares)),
+        in_specs=[ANY] + [VMEM] * (1 + len(squares) + per_device),
         out_specs=ANY,
         out_shape=pltpu.HBM(shape, residual.dtype),
         scratch_shapes=[
@@ -495,7 +552,7 @@
         cost_estimate=cost(1, 1),
         compiler_params=params(12),
         name="finish_layer",
-    )(*in_hbm(residual), squares, gain.reshape(1, width), *in_vmem(*totals))
+    )(*in_hbm(residual), gain.reshape(1, width), *squares, *in_vmem(*totals))
 
 
 def permuted(value, axis, offset):
@@ -514,43 +571,42 @@
     hand = functools.partial(gather, kv_pool, block_table, request_order, req_count)
     shape = (planes, per_device, block_table.shape[1] // req_count, req_count) + kv_pool.shape[2:]
 
-    early = [s for s in range(req_count - 1, 0, -1) if s not in LATE]
-    late = [s for s in range(req_count - 1, 0, -1) if s in LATE]
-    own, *sent = hand([0] + early + late, 0, 2, False)
-    sent_late = sent[len(early) :]
-    received = [permuted(piece, "req", s) for piece, s in zip(sent, early)]
+    others = list(range(req_count - 1, 0, -1))
+    early = [s for s in others if s not in LATE]
+    late = [s for s in others if s in LATE]
+    sent = dict(zip([0] + others, hand([0] + others, 0, 2, False)))
+    received = {s: permuted(sent[s], "req", s) for s in early}
+    own = received[0] = sent[0]
 
     flat_in = span_in.reshape(-1, full_width)
     q_raw, k_raw, values, squares = project(
         per_device, request_order, lengths, flat_in, w_qkv, qk_gain, after=(own,)
     )
+    own_squares = squares
     squares = lax.all_gather(squares, "tensor")
-    sent_late = hold(sent_late, (q_raw,))
-    received += [permuted(piece, "req", s) for piece, s in zip(sent_late, late)]
+    queries, mixed, state = attend_new(full_width, span_len, q_raw, k_raw, values, squares)
+    arrived = [received[s] for s in reversed(early)]
+    sent_late = hold([sent[s] for s in late], (own_squares, *arrived[:2]), pltpu.VMEM)
+    received.update({s: permuted(piece, "req", s) for s, piece in zip(late, sent_late)})
 
     rest = planes - 2
     everyone = list(range(req_count))
     (sent_rest,) = hand(everyone, 2, rest, True, after=(own,))
-    (sent_rest,) = hold((sent_rest,), (squares, *received[: len(early)]))
+    (sent_rest,) = hold((sent_rest,), (state, *arrived))
     received_rest = lax.all_to_all(sent_rest, "req", 0, 0)
 
-    queries, mixed, state = attend_new(
-        full_width, span_len, q_raw, k_raw, values, squares, after=(sent_rest,)
-    )
     relaid, across, added, totals, row_squares = None, (), (), [], ()
     for p in range(per_device):
         relaid, *terms = attend_old(
             p,
             span_len,
-            request_order,
-            lengths,
             queries,
             mixed,
             state,
             w_out,
             tensor_count,
-            [0] + early + late,
-            [own] + received,
+            list(received),
+            list(received.values()),
             shape,
             filled=relaid,
             after=(sent_rest, *added),
@@ -562,7 +618,9 @@
         across = [permuted(added[0], "tensor", 2)]
         total, *row_squares = total_of(p, terms[0], near, across[0], row_squares)
         totals.append(total)
-    row_squares = lax.all_gather(row_squares[0], "tensor")
+    row_squares = row_squares + [
+        permuted(row_squares[0], "tensor", at) for at in range(1, tensor_count)
+    ]
     layer_out = finish(span_in, totals, row_squares, post_gain)
 
     relaid = place(shape, everyone, 2, rest, True, [received_rest], filled=relaid)

time: 116 us -> 111 us (0.957)
  waiting for transfers between devices: 21.4 us -> 34.3 us
  starting transfers between devices: 35.8 us -> 23 us
  blocking collectives: 10.7 us -> 5.43 us
  local copies, waits for them, and re-layouts: 6.81 us -> 1.68 us
  Pallas kernels: 39.9 us -> 45 us
    ppermute x13 -> x16, waiting for transfers between devices: 21.4 us -> 33.5 us  [permuted(): return lax.ppermute(value, axis, [(i, i ^ offset) for i in range(size)])]
    ppermute x13 -> x16, starting transfers between devices: 29 us -> 18.3 us  [permuted(): return lax.ppermute(value, axis, [(i, i ^ offset) for i in range(size)])]
    all_gather x1 -> x0, blocking collectives: 5.25 us -> none  [on_device(): row_squares = lax.all_gather(row_squares[0], 'tensor')]
    unnamed x36 -> x16, local copies, waits for them, and re-layouts: 6.81 us -> 1.68 us
    pallas_call x1, Pallas kernels: 3.85 us -> 6.8 us  [attend_new(): pl.pallas_call(functools.partial(attend_new_body, full_width, span, q_blo...]
    all_to_all x1, starting transfers between devices: 6.89 us -> 4.65 us  [on_device(): received_rest = lax.all_to_all(sent_rest, 'req', 0, 0)]
  transfers between devices with their start and end apart: 14 -> 17, of which waited for: 4 -> 7; matrix products, arithmetic and copies ran while one was open for 0% -> 0% of each run, Pallas kernels for 29% -> 35%
where the time goes in v3:
time: 111 us; the launch traced here: 110 us
  Pallas kernels  45 us (41%)
  waiting for transfers between devices  34.3 us (31%)
  starting transfers between devices  23 us (21%)
  blocking collectives  5.43 us (5%)
  local copies, waits for them, and re-layouts  1.68 us (2%)
    ppermute x16, waiting for transfers between devices, permuted(): return lax.ppermute(value, axis, [(i, i ^ offset) for i in range(size)])  33.5 us
    ppermute x16, starting transfers between devices, permuted(): return lax.ppermute(value, axis, [(i, i ^ offset) for i in range(size)])  18.3 us
    pallas_call x2, Pallas kernels, attend_old(): pl.pallas_call(functools.partial(attend_old_body, which, span, offsets, q...  13.3 us
    pallas_call x1, Pallas kernels, project(): pl.pallas_call(functools.partial(project_body, per_device, block, len(aft...  12.2 us
    pallas_call x1, Pallas kernels, attend_new(): pl.pallas_call(functools.partial(attend_new_body, full_width, span, q_blo...  6.8 us
    pallas_call x2, Pallas kernels, gather(): pl.pallas_call(functools.partial(gather_body, targets, first, planes, cou...  6.68 us
    all_gather x1, blocking collectives, on_device(): squares = lax.all_gather(squares, 'tensor')  5.43 us
    all_to_all x1, starting transfers between devices, on_device(): received_rest = lax.all_to_all(sent_rest, 'req', 0, 0)  4.65 us
  transfers between devices with their start and end apart: 17, of which 7 were waited for; matrix products, arithmetic and copies ran while one was open for 0% of the time, Pallas kernels for 35%

profile of v3, /device:TPU:0, one launch (start us, length us, event | category | flops | bytes accessed | tf_op | source)
XLA Modules:
  0.0 110.4 jit_solution(2269363402529419086)
XLA Ops:
  0.6 0.0 copy-start.4
  0.6 0.0 copy-start.6
  0.7 3.4 %gather_blocks.2 = (bf16[2,2,4,16,512]{4,3,2,1,0:T(8,128)(2,1)S(1)}, bf16[2,2,4,16,512]{4,3,2,1,0:T(8,128)(2,1)S(1)}, bf16[2,2,4,16,512]{4,3,2,1,0:T(8,128)(2,1)...) custom-call(s32[16,32]{1,0:T(8,128)} %table.3, ...), custom_call_target="tpu_custom_call" | custom-call | flops 1 | bytes 1 | tf_op jit(solution)/shard_map/gather_blocks/pallas_call | solution.py:76
  4.1 4.0 %collective-permute-start.3 = (bf16[2,2,4,16,512]{4,3,2,1,0:T(8,128)(2,1)S(1)}, bf16[2,2,4,16,512]{4,3,2,1,0:T(8,128)(2,1)S(1)}, u32[]{:S(2)}, u32[]{:S(2)}) collective-permute-start(bf16[2,2,4,16,512]{4,3,2,1,0:T(8,128)(2,1)S(1)} %get-tuple-element.44), channel_id=1, source_target_pairs={{0,12},{4,8},{8,4},{12,0},{16,28},{20,24},{24,20},{28,16},{1,13},{... | collective-permute-start | bytes 786440 | tf_op jit(solution)/shard_map/ppermute | solution.py:560
  8.1 0.4 collective-permute-start.4
  8.6 3.5 %collective-permute-start = (bf16[2,2,4,16,512]{4,3,2,1,0:T(8,128)(2,1)S(1)}, bf16[2,2,4,16,512]{4,3,2,1,0:T(8,128)(2,1)S(1)}, u32[]{:S(2)}, u32[]{:S(2)}) collective-permute-start(bf16[2,2,4,16,512]{4,3,2,1,0:T(8,128)(2,1)S(1)} %get-tuple-element.41), channel_id=1, source_target_pairs={{0,28},{4,24},{8,20},{12,16},{16,12},{20,8},{24,4},{28,0},{1,29},{... | collective-permute-start | bytes 786440 | tf_op jit(solution)/shard_map/ppermute | solution.py:560
  12.1 0.1 collective-permute-start.1
  12.2 1.9 %collective-permute-start.2 = (bf16[2,2,4,16,512]{4,3,2,1,0:T(8,128)(2,1)S(1)}, bf16[2,2,4,16,512]{4,3,2,1,0:T(8,128)(2,1)S(1)}, u32[]{:S(2)}, u32[]{:S(2)}) collective-permute-start(bf16[2,2,4,16,512]{4,3,2,1,0:T(8,128)(2,1)S(1)} %get-tuple-element.43), channel_id=1, source_target_pairs={{0,20},{4,16},{8,28},{12,24},{16,4},{20,0},{24,12},{28,8},{1,21},{... | collective-permute-start | bytes 786440 | tf_op jit(solution)/shard_map/ppermute | solution.py:560
  14.1 12.2 %project_qkv.1 = (f32[1024,512]{1,0:T(8,128)}, f32[1024,512]{1,0:T(8,128)}, bf16[1024,512]{1,0:T(8,128)(2,1)}, f32[8,1024]{1,0:T(8,128)S(1)}) custom-call(s32[16]{0:T(128)} %order.5, s32[16]{0:T(128)} %lengths.1, f32[1,128]{1,0:T(1,128)S(1)} %copy-done.6, f32[2,512,128]{2,1,0:T(8,128)S(1)} %copy-done.4, bf16[2,512]{1,0:T(2,128)(2,1)S(1)} %copy-done.5, ...), custom_call_target="tpu_custom_call" | custom-call | flops 1 | bytes 1 | tf_op jit(solution)/shard_map/project_qkv/pallas_call | solution.py:225
  26.3 0.0 collective-permute-done.4.refs_3_.refs_2_.rest_4_
  26.3 2.2 %collective-permute-start.5 = (bf16[2,2,4,16,512]{4,3,2,1,0:T(8,128)(2,1)}, bf16[2,2,4,16,512]{4,3,2,1,0:T(8,128)(2,1)}, u32[]{:S(2)}, u32[]{:S(2)}) collective-permute-start(bf16[2,2,4,16,512]{4,3,2,1,0:T(8,128)(2,1)} %get-tuple-element.48), channel_id=1, source_target_pairs={{0,16},{4,20},{8,24},{12,28},{16,0},{20,4},{24,8},{28,12},{1,17},{... | collective-permute-start | bytes 786440 | tf_op jit(solution)/shard_map/ppermute | solution.py:560
  28.5 0.3 collective-permute-start.6
  28.9 3.3 %gather_blocks.3.refs_0_ = bf16[8,2,2,4,16,512]{5,4,3,2,1,0:T(8,128)(2,1)} custom-call(s32[16,32]{1,0:T(8,128)} %table.3, s32[16]{0:T(128)} %order.5, bf16[4,64,16,512]{3,2,1,0:T(8,128)(2,1)} %pool.3, bf16[2,2,4,16,512]{4,3,2,1,0:T(8,128)(2,1)S(1)} %get-tuple-element.33.rest_0_.rest_5_), custom_call_target="tpu_custom_call" | custom-call | flops 1 | bytes 1 | tf_op jit(solution)/shard_map/gather_blocks/pallas_call | solution.py:76
  32.2 5.4 %all-gather = f32[32,1024]{1,0:T(8,128)S(1)} all-gather(f32[8,1024]{1,0:T(8,128)S(1)} %get-tuple-element.34.refs_2_), channel_id=2, replica_groups=mesh['req'=8,'tensor'=4] {'tensor'}, dimensions={0}, use_global_device_ids=true | all-gather | bytes 163840 | tf_op jit(solution)/shard_map/all_gather | solution.py:586
  37.6 6.8 %attend_new.1 = (bf16[1024,512]{1,0:T(8,128)(2,1)}, f32[2,512,512]{2,1,0:T(8,128)}, f32[16,1024]{1,0:T(8,128)S(1)}) custom-call(f32[4,8,1024]{2,1,0:T(8,128)S(1)} %bitcast.3, f32[1024,512]{1,0:T(8,128)} %get-tuple-element.35.rest_0_, f32[1024,512]{1,0:T(8,128)} %get-tuple-element.36.rest_1_, bf16[1024,512]{1,0:T(8,128)(2,1)} %get-tuple-element.37.rest_2_), custom_call_target="tpu_custom_call" | custom-call | flops 1 | bytes 1 | tf_op jit(solution)/shard_map/attend_new/pallas_call | solution.py:335
  44.4 0.0 collective-permute-done.refs_6_.rest_0_
  44.4 11.8 %collective-permute-done.2.refs_4_.rest_2_ = bf16[2,2,4,16,512]{4,3,2,1,0:T(8,128)(2,1)S(1)} collective-permute-done((bf16[2,2,4,16,512]{4,3,2,1,0:T(8,128)(2,1)S(1)}, bf16[2,2,4,16,512]{4,3,2,1,0:T(8,128)(2,1)S(1)}, u32[]{:S(2)}, u32[]{:S(2)}) %collective-permute-start.2) | collective-permute-done | bytes 262176 | tf_op jit(solution)/shard_map/ppermute | solution.py:560
  56.2 0.7 copy-done.1
  56.9 4.6 %all-to-all-start = ((bf16[8,2,2,4,16,512]{5,4,3,2,1,0:T(8,128)(2,1)}), bf16[8,2,2,4,16,512]{5,4,3,2,1,0:T(8,128)(2,1)}, u32[]{:S(2)}, u32[]{:S(2)}) async-start(bf16[8,2,2,4,16,512]{5,4,3,2,1,0:T(8,128)(2,1)} %hold.3.rest_8_.rest_9_), calls=%async_computation | async-start | bytes 4194304 | tf_op jit(solution)/shard_map/all_to_all | solution.py:596
  61.6 0.0 collective-permute-done.5.rest_6_
  61.6 0.0 collective-permute-done.6.rest_7_
  61.6 0.0 copy-start.2
  61.6 0.9 copy-done.2
  62.6 6.9 %attend_old.2 = (bf16[4,2,4,8,16,512]{5,4,3,2,1,0:T(8,128)(2,1)}, bf16[512,512]{1,0:T(8,128)(2,1)S(1)}, bf16[512,512]{1,0:T(8,128)(2,1)S(1)}, bf16[512,512]{1,0:T(8,128)(2,1)S(1)}, bf16[512,512]{1,0:T(8,128)(2,1)S(1)}) custom-call(f32[16,1024]{1,0:T(8,128)S(1)} %get-tuple-element.38.refs_1_.state, bf16[1024,512]{1,0:T(8,128)(2,1)} %get-tuple-element.39.q_all, ...), custom_call_target="tpu_custom_call" | custom-call | flops 999999995904 | bytes 999999995904 | tf_op jit(solution)/shard_map/attend_old/pallas_call | solution.py:436
  69.5 0.1 collective-permute-start.7
  69.6 1.9 %collective-permute-done.7.second = bf16[512,512]{1,0:T(8,128)(2,1)S(1)} collective-permute-done((bf16[512,512]{1,0:T(8,128)(2,1)S(1)}, bf16[512,512]{1,0:T(8,128)(2,1)S(1)}, u32[]{:S(2)}, u32[]{:S(2)}) %collective-permute-start.7) | collective-permute-done | bytes 524320 | tf_op jit(solution)/shard_map/ppermute | solution.py:560
  71.5 0.1 add_terms.2.rest_10_
  71.6 1.6 %collective-permute-start.10 = (bf16[512,512]{1,0:T(8,128)(2,1)S(1)}, bf16[512,512]{1,0:T(8,128)(2,1)S(1)}, u32[]{:S(2)}, u32[]{:S(2)}) collective-permute-start(bf16[512,512]{1,0:T(8,128)(2,1)S(1)} %add_terms.2.rest_10_), channel_id=1, source_target_pairs={{0,2},{1,3},{2,0},{3,1},{4,6},{5,7},{6,4},{7,5},{8,10},{9,11},{10,... | collective-permute-start | bytes 1572872 | tf_op jit(solution)/shard_map/ppermute | solution.py:560
  73.2 6.3 %attend_old.3 = (bf16[4,2,4,8,16,512]{5,4,3,2,1,0:T(8,128)(2,1)}, bf16[512,512]{1,0:T(8,128)(2,1)S(1)}, bf16[512,512]{1,0:T(8,128)(2,1)S(1)}, bf16[512,512]{1,0:T(8,128)(2,1)S(1)}, bf16[512,512]{1,0:T(8,128)(2,1)S(1)}) custom-call(f32[16,1024]{1,0:T(8,128)S(1)} %get-tuple-element.38.refs_1_.state, ...), custom_call_target="tpu_custom_call", output_to_operand_aliasing={{0}: (12, {})} | custom-call | flops 1 | bytes 1 | tf_op jit(solution)/shard_map/attend_old/pallas_call | solution.py:436
  79.5 0.1 collective-permute-start.9
  79.6 0.5 collective-permute-start.12
  80.1 0.1 collective-permute-start.8
  80.2 5.5 %collective-permute-done.10.rest_0_.third = bf16[512,512]{1,0:T(8,128)(2,1)S(1)} collective-permute-done((bf16[512,512]{1,0:T(8,128)(2,1)S(1)}, bf16[512,512]{1,0:T(8,128)(2,1)S(1)}, u32[]{:S(2)}, u32[]{:S(2)}) %collective-permute-start.10) | collective-permute-done | bytes 524320 | tf_op jit(solution)/shard_map/ppermute | solution.py:560
  85.7 0.0 collective-permute-done.9.second
  85.7 0.1 add_terms.3
  85.8 0.0 copy-start.7
  85.8 1.6 %collective-permute-start.11 = (bf16[512,512]{1,0:T(8,128)(2,1)S(1)}, bf16[512,512]{1,0:T(8,128)(2,1)S(1)}, u32[]{:S(2)}, u32[]{:S(2)}) collective-permute-start(bf16[512,512]{1,0:T(8,128)(2,1)S(1)} %add_terms.3), channel_id=1, source_target_pairs={{0,2},{1,3},{2,0},{3,1},{4,6},{5,7},{6,4},{7,5},{8,10},{9,11},{10,... | collective-permute-start | bytes 1572872 | tf_op jit(solution)/shard_map/ppermute | solution.py:560
  87.4 0.3 total_terms.2
  87.7 11.4 %collective-permute-done.11.third = bf16[512,512]{1,0:T(8,128)(2,1)S(1)} collective-permute-done((bf16[512,512]{1,0:T(8,128)(2,1)S(1)}, bf16[512,512]{1,0:T(8,128)(2,1)S(1)}, u32[]{:S(2)}, u32[]{:S(2)}) %collective-permute-start.11) | collective-permute-done | bytes 524320 | tf_op jit(solution)/shard_map/ppermute | solution.py:560
  99.1 0.3 total_terms.3
  99.4 0.1 collective-permute-start.13
  99.5 1.6 %collective-permute-start.14 = (f32[8,512]{1,0:T(8,128)S(1)}, f32[8,512]{1,0:T(8,128)S(1)}, u32[]{:S(2)}, u32[]{:S(2)}) collective-permute-start(f32[8,512]{1,0:T(8,128)S(1)} %get-tuple-element.60.rest_0_), channel_id=1, source_target_pairs={{0,2},{1,3},{2,0},{3,1},{4,6},{5,7},{6,4},{7,5},{8,10},{9,11},{10,... | collective-permute-start | bytes 49160 | tf_op jit(solution)/shard_map/ppermute | solution.py:560
  101.1 0.3 collective-permute-start.15
  101.4 1.9 %collective-permute-done.14.rest_2_ = f32[8,512]{1,0:T(8,128)S(1)} collective-permute-done((f32[8,512]{1,0:T(8,128)S(1)}, f32[8,512]{1,0:T(8,128)S(1)}, u32[]{:S(2)}, u32[]{:S(2)}) %collective-permute-start.14) | collective-permute-done | bytes 16416 | tf_op jit(solution)/shard_map/ppermute | solution.py:560
  103.3 0.9 collective-permute-done.15.rest_3_
  104.2 2.4 %finish_layer.1 = bf16[2,512,512]{2,1,0:T(8,128)(2,1)} custom-call(bf16[2,512,2048]{2,1,0:T(8,128)(2,1)} %residual.1, bf16[1,512]{1,0:T(2,128)(2,1)S(1)} %reshape.13.gain, f32[8,512]{1,0:T(8,128)S(1)} %get-tuple-element.60.rest_0_, f32[8,512]{1,0:T(8,128)S(1)} %collective-permute-done.13.rest_1_, f32[8,512]{1,0:T(8,128)S(1)} %collective-permute-done.14.rest_2_, ...), custom_call_target="tpu_custom_call" | custom-call | flops 1 | bytes 1 | tf_op jit(solution)/shard_map/finish_layer/pallas_call | solution.py:541
  106.6 0.8 all-to-all-done.rest_1_
  107.4 2.8 %place_blocks.1 = bf16[4,2,4,8,16,512]{5,4,3,2,1,0:T(8,128)(2,1)} custom-call(bf16[4,2,4,8,16,512]{5,4,3,2,1,0:T(8,128)(2,1)} %get-tuple-element.63.rest_0_, bf16[8,2,2,4,16,512]{5,4,3,2,1,0:T(8,128)(2,1)} %all-to-all-done.rest_1_), custom_call_target="tpu_custom_call", output_to_operand_aliasing={{}: (0, {})} | custom-call | flops 1 | bytes 1 | tf_op jit(solution)/shard_map/place_blocks/pallas_call | solution.py:105
  (18 shorter events, 0.0 us)
Async XLA Ops:
  0.6 13.5 %copy-start.4 = (f32[2,512,128]{2,1,0:T(8,128)S(1)}, f32[2,512,128]{2,1,0:T(8,128)}, u32[]{:S(2)}) copy-start(f32[2,512,128]{2,1,0:T(8,128)} %constant.5.clone.steps) | copy-start | bytes 1572868
  0.6 13.5 %copy-start.6 = (f32[1,128]{1,0:T(1,128)S(1)}, f32[1,128]{1,0:T(1,128)}, u32[]{:S(2)}) copy-start(f32[1,128]{1,0:T(1,128)} %constant.4.clone.frequency) | copy-start | bytes 1540
  0.7 13.4 %copy-start.5 = (bf16[2,512]{1,0:T(2,128)(2,1)S(1)}, bf16[2,512]{1,0:T(2,128)(2,1)}, u32[]{:S(2)}) copy-start(bf16[2,512]{1,0:T(2,128)(2,1)} %gain.1) | copy-start | bytes 6148
  4.1 22.2 %collective-permute-start.3 = (bf16[2,2,4,16,512]{4,3,2,1,0:T(8,128)(2,1)S(1)}, bf16[2,2,4,16,512]{4,3,2,1,0:T(8,128)(2,1)S(1)}, u32[]{:S(2)}, u32[]{:S(2)}) collective-permute-start(bf16[2,2,4,16,512]{4,3,2,1,0:T(8,128)(2,1)S(1)} %get-tuple-element.44), channel_id=1, source_target_pairs={{0,12},{4,8},{8,4},{12,0},{16,28},{20,24},{24,20},{28,16},{1,13},{... | collective-permute-start | bytes 786440 | tf_op jit(solution)/shard_map/ppermute | solution.py:560
  8.1 18.2 %collective-permute-start.4 = (bf16[2,2,4,16,512]{4,3,2,1,0:T(8,128)(2,1)S(1)}, bf16[2,2,4,16,512]{4,3,2,1,0:T(8,128)(2,1)S(1)}, u32[]{:S(2)}, u32[]{:S(2)}) collective-permute-start(bf16[2,2,4,16,512]{4,3,2,1,0:T(8,128)(2,1)S(1)} %get-tuple-element.45), channel_id=1, source_target_pairs={{0,8},{4,12},{8,0},{12,4},{16,24},{20,28},{24,16},{28,20},{1,9},{5... | collective-permute-start | bytes 786440 | tf_op jit(solution)/shard_map/ppermute | solution.py:560
  8.6 35.8 %collective-permute-start = (bf16[2,2,4,16,512]{4,3,2,1,0:T(8,128)(2,1)S(1)}, bf16[2,2,4,16,512]{4,3,2,1,0:T(8,128)(2,1)S(1)}, u32[]{:S(2)}, u32[]{:S(2)}) collective-permute-start(bf16[2,2,4,16,512]{4,3,2,1,0:T(8,128)(2,1)S(1)} %get-tuple-element.41), channel_id=1, source_target_pairs={{0,28},{4,24},{8,20},{12,16},{16,12},{20,8},{24,4},{28,0},{1,29},{... | collective-permute-start | bytes 786440 | tf_op jit(solution)/shard_map/ppermute | solution.py:560
  12.1 32.3 %collective-permute-start.1 = (bf16[2,2,4,16,512]{4,3,2,1,0:T(8,128)(2,1)S(1)}, bf16[2,2,4,16,512]{4,3,2,1,0:T(8,128)(2,1)S(1)}, u32[]{:S(2)}, u32[]{:S(2)}) collective-permute-start(bf16[2,2,4,16,512]{4,3,2,1,0:T(8,128)(2,1)S(1)} %get-tuple-element.42), channel_id=1, source_target_pairs={{0,24},{4,28},{8,16},{12,20},{16,8},{20,12},{24,0},{28,4},{1,25},{... | collective-permute-start | bytes 786440 | tf_op jit(solution)/shard_map/ppermute | solution.py:560
  12.2 44.1 %collective-permute-start.2 = (bf16[2,2,4,16,512]{4,3,2,1,0:T(8,128)(2,1)S(1)}, bf16[2,2,4,16,512]{4,3,2,1,0:T(8,128)(2,1)S(1)}, u32[]{:S(2)}, u32[]{:S(2)}) collective-permute-start(bf16[2,2,4,16,512]{4,3,2,1,0:T(8,128)(2,1)S(1)} %get-tuple-element.43), channel_id=1, source_target_pairs={{0,20},{4,16},{8,28},{12,24},{16,4},{20,0},{24,12},{28,8},{1,21},{... | collective-permute-start | bytes 786440 | tf_op jit(solution)/shard_map/ppermute | solution.py:560
  26.3 35.3 %collective-permute-start.5 = (bf16[2,2,4,16,512]{4,3,2,1,0:T(8,128)(2,1)}, bf16[2,2,4,16,512]{4,3,2,1,0:T(8,128)(2,1)}, u32[]{:S(2)}, u32[]{:S(2)}) collective-permute-start(bf16[2,2,4,16,512]{4,3,2,1,0:T(8,128)(2,1)} %get-tuple-element.48), channel_id=1, source_target_pairs={{0,16},{4,20},{8,24},{12,28},{16,0},{20,4},{24,8},{28,12},{1,17},{... | collective-permute-start | bytes 786440 | tf_op jit(solution)/shard_map/ppermute | solution.py:560
  28.5 33.1 %collective-permute-start.6 = (bf16[2,2,4,16,512]{4,3,2,1,0:T(8,128)(2,1)}, bf16[2,2,4,16,512]{4,3,2,1,0:T(8,128)(2,1)}, u32[]{:S(2)}, u32[]{:S(2)}) collective-permute-start(bf16[2,2,4,16,512]{4,3,2,1,0:T(8,128)(2,1)} %get-tuple-element.49), channel_id=1, source_target_pairs={{0,4},{4,0},{8,12},{12,8},{16,20},{20,16},{24,28},{28,24},{1,5},{5... | collective-permute-start | bytes 786440 | tf_op jit(solution)/shard_map/ppermute | solution.py:560
  56.2 0.7 copy-start.1
  56.9 4.7 %copy-start = (bf16[8,2,2,4,16,512]{5,4,3,2,1,0:T(8,128)(2,1)S(1)}, bf16[8,2,2,4,16,512]{5,4,3,2,1,0:T(8,128)(2,1)}, u32[]{:S(2)}) copy-start(bf16[8,2,2,4,16,512]{5,4,3,2,1,0:T(8,128)(2,1)} %hold.3.rest_8_.rest_9_) | copy-start | bytes 6291460
  56.9 50.4 %all-to-all-start = ((bf16[8,2,2,4,16,512]{5,4,3,2,1,0:T(8,128)(2,1)}), bf16[8,2,2,4,16,512]{5,4,3,2,1,0:T(8,128)(2,1)}, u32[]{:S(2)}, u32[]{:S(2)}) async-start(bf16[8,2,2,4,16,512]{5,4,3,2,1,0:T(8,128)(2,1)} %hold.3.rest_8_.rest_9_), calls=%async_computation | async-start | bytes 4194304 | tf_op jit(solution)/shard_map/all_to_all | solution.py:596
  61.6 1.0 copy-start.2
  62.6 10.6 %copy-start.3 = (bf16[2,2,4,16,512]{4,3,2,1,0:T(8,128)(2,1)S(1)}, bf16[2,2,4,16,512]{4,3,2,1,0:T(8,128)(2,1)}, u32[]{:S(2)}) copy-start(bf16[2,2,4,16,512]{4,3,2,1,0:T(8,128)(2,1)} %copy-done.1) | copy-start | bytes 786436
  69.5 2.0 %collective-permute-start.7 = (bf16[512,512]{1,0:T(8,128)(2,1)S(1)}, bf16[512,512]{1,0:T(8,128)(2,1)S(1)}, u32[]{:S(2)}, u32[]{:S(2)}) collective-permute-start(bf16[512,512]{1,0:T(8,128)(2,1)S(1)} %get-tuple-element.52), channel_id=1, source_target_pairs={{0,1},{1,0},{2,3},{3,2},{4,5},{5,4},{6,7},{7,6},{8,9},{9,8},{10,11... | collective-permute-start | bytes 1572872 | tf_op jit(solution)/shard_map/ppermute | solution.py:560
  71.6 14.0 %collective-permute-start.10 = (bf16[512,512]{1,0:T(8,128)(2,1)S(1)}, bf16[512,512]{1,0:T(8,128)(2,1)S(1)}, u32[]{:S(2)}, u32[]{:S(2)}) collective-permute-start(bf16[512,512]{1,0:T(8,128)(2,1)S(1)} %add_terms.2.rest_10_), channel_id=1, source_target_pairs={{0,2},{1,3},{2,0},{3,1},{4,6},{5,7},{6,4},{7,5},{8,10},{9,11},{10,... | collective-permute-start | bytes 1572872 | tf_op jit(solution)/shard_map/ppermute | solution.py:560
  79.5 6.2 %collective-permute-start.9 = (bf16[512,512]{1,0:T(8,128)(2,1)S(1)}, bf16[512,512]{1,0:T(8,128)(2,1)S(1)}, u32[]{:S(2)}, u32[]{:S(2)}) collective-permute-start(bf16[512,512]{1,0:T(8,128)(2,1)S(1)} %get-tuple-element.56), channel_id=1, source_target_pairs={{0,1},{1,0},{2,3},{3,2},{4,5},{5,4},{6,7},{7,6},{8,9},{9,8},{10,11... | collective-permute-start | bytes 1572872 | tf_op jit(solution)/shard_map/ppermute | solution.py:560
  79.6 7.8 %collective-permute-start.12 = (bf16[512,512]{1,0:T(8,128)(2,1)S(1)}, bf16[512,512]{1,0:T(8,128)(2,1)S(1)}, u32[]{:S(2)}, u32[]{:S(2)}) collective-permute-start(bf16[512,512]{1,0:T(8,128)(2,1)S(1)} %get-tuple-element.58), channel_id=1, source_target_pairs={{0,1},{1,0},{2,3},{3,2},{4,5},{5,4},{6,7},{7,6},{8,9},{9,8},{10,11... | collective-permute-start | bytes 1572872 | tf_op jit(solution)/shard_map/ppermute | solution.py:560
  80.1 7.6 %collective-permute-start.8 = (bf16[512,512]{1,0:T(8,128)(2,1)S(1)}, bf16[512,512]{1,0:T(8,128)(2,1)S(1)}, u32[]{:S(2)}, u32[]{:S(2)}) collective-permute-start(bf16[512,512]{1,0:T(8,128)(2,1)S(1)} %get-tuple-element.54), channel_id=1, source_target_pairs={{0,1},{1,0},{2,3},{3,2},{4,5},{5,4},{6,7},{7,6},{8,9},{9,8},{10,11... | collective-permute-start | bytes 1572872 | tf_op jit(solution)/shard_map/ppermute | solution.py:560
  85.8 15.6 %copy-start.7 = (bf16[512]{0:T(512)(128)(2,1)S(1)}, bf16[512]{0:T(512)(128)(2,1)}, u32[]{:S(2)}) copy-start(bf16[512]{0:T(512)(128)(2,1)} %param.15) | copy-start | bytes 3076
  85.8 13.3 %collective-permute-start.11 = (bf16[512,512]{1,0:T(8,128)(2,1)S(1)}, bf16[512,512]{1,0:T(8,128)(2,1)S(1)}, u32[]{:S(2)}, u32[]{:S(2)}) collective-permute-start(bf16[512,512]{1,0:T(8,128)(2,1)S(1)} %add_terms.3), channel_id=1, source_target_pairs={{0,2},{1,3},{2,0},{3,1},{4,6},{5,7},{6,4},{7,5},{8,10},{9,11},{10,... | collective-permute-start | bytes 1572872 | tf_op jit(solution)/shard_map/ppermute | solution.py:560
  99.4 2.0 %collective-permute-start.13 = (f32[8,512]{1,0:T(8,128)S(1)}, f32[8,512]{1,0:T(8,128)S(1)}, u32[]{:S(2)}, u32[]{:S(2)}) collective-permute-start(f32[8,512]{1,0:T(8,128)S(1)} %get-tuple-element.60.rest_0_), channel_id=1, source_target_pairs={{0,1},{1,0},{2,3},{3,2},{4,5},{5,4},{6,7},{7,6},{8,9},{9,8},{10,11... | collective-permute-start | bytes 49160 | tf_op jit(solution)/shard_map/ppermute | solution.py:560
  99.5 3.8 %collective-permute-start.14 = (f32[8,512]{1,0:T(8,128)S(1)}, f32[8,512]{1,0:T(8,128)S(1)}, u32[]{:S(2)}, u32[]{:S(2)}) collective-permute-start(f32[8,512]{1,0:T(8,128)S(1)} %get-tuple-element.60.rest_0_), channel_id=1, source_target_pairs={{0,2},{1,3},{2,0},{3,1},{4,6},{5,7},{6,4},{7,5},{8,10},{9,11},{10,... | collective-permute-start | bytes 49160 | tf_op jit(solution)/shard_map/ppermute | solution.py:560
  101.1 3.2 %collective-permute-start.15 = (f32[8,512]{1,0:T(8,128)S(1)}, f32[8,512]{1,0:T(8,128)S(1)}, u32[]{:S(2)}, u32[]{:S(2)}) collective-permute-start(f32[8,512]{1,0:T(8,128)S(1)} %get-tuple-element.60.rest_0_), channel_id=1, source_target_pairs={{0,3},{1,2},{2,1},{3,0},{4,7},{5,6},{6,5},{7,4},{8,11},{9,10},{10,... | collective-permute-start | bytes 49160 | tf_op jit(solution)/shard_map/ppermute | solution.py:560

commit v4 on v3

--- a/solution.py
+++ b/solution.py
@@ -12,7 +12,8 @@
 HD = 128
 norm_eps = 1e-06
 rope_base = 500000.0
-LATE = (4, 1)
+LATE = (5, 1)
+GATE = 6
 
 ANY = pl.BlockSpec(memory_space=pl.ANY)
 SMEM = pl.BlockSpec(memory_space=pltpu.SMEM)
@@ -592,7 +593,7 @@
     rest = planes - 2
     everyone = list(range(req_count))
     (sent_rest,) = hand(everyone, 2, rest, True, after=(own,))
-    (sent_rest,) = hold((sent_rest,), (state, *arrived))
+    (sent_rest,) = hold((sent_rest,), (state, *arrived[:2], received[GATE]))
     received_rest = lax.all_to_all(sent_rest, "req", 0, 0)
 
     relaid, across, added, totals, row_squares = None, (), (), [], ()

time: 111 us -> 107 us (0.964)
  waiting for transfers between devices: 34.3 us -> 26.5 us
  starting transfers between devices: 23 us -> 27.8 us
  local copies, waits for them, and re-layouts: 1.68 us -> 0.03 us
    ppermute x16, waiting for transfers between devices: 33.5 us -> 24.3 us  [permuted(): return lax.ppermute(value, axis, [(i, i ^ offset) for i in range(size)])]
    ppermute x16, starting transfers between devices: 18.3 us -> 23.2 us  [permuted(): return lax.ppermute(value, axis, [(i, i ^ offset) for i in range(size)])]
    unnamed x16 -> x10, local copies, waits for them, and re-layouts: 1.68 us -> 0.03 us
    all_to_all x1, waiting for transfers between devices: 0.76 us -> 2.25 us  [on_device(): received_rest = lax.all_to_all(sent_rest, 'req', 0, 0)]
  transfers between devices with their start and end apart: 17 -> 17, of which waited for: 7 -> 7; matrix products, arithmetic and copies ran while one was open for 0% -> 0% of each run, Pallas kernels for 35% -> 37%
where the time goes in v4:
time: 107 us; the launch traced here: 106 us
  Pallas kernels  45.1 us (42%)
  starting transfers between devices  27.8 us (26%)
  waiting for transfers between devices  26.5 us (25%)
  blocking collectives  5.43 us (5%)
    ppermute x16, waiting for transfers between devices, permuted(): return lax.ppermute(value, axis, [(i, i ^ offset) for i in range(size)])  24.3 us
    ppermute x16, starting transfers between devices, permuted(): return lax.ppermute(value, axis, [(i, i ^ offset) for i in range(size)])  23.2 us
    pallas_call x2, Pallas kernels, attend_old(): pl.pallas_call(functools.partial(attend_old_body, which, span, offsets, q...  13.2 us
    pallas_call x1, Pallas kernels, project(): pl.pallas_call(functools.partial(project_body, per_device, block, len(aft...  12.2 us
    pallas_call x2, Pallas kernels, gather(): pl.pallas_call(functools.partial(gather_body, targets, first, planes, cou...  6.83 us
    pallas_call x1, Pallas kernels, attend_new(): pl.pallas_call(functools.partial(attend_new_body, full_width, span, q_blo...  6.79 us
    all_gather x1, blocking collectives, on_device(): squares = lax.all_gather(squares, 'tensor')  5.43 us
    all_to_all x1, starting transfers between devices, on_device(): received_rest = lax.all_to_all(sent_rest, 'req', 0, 0)  4.68 us
  transfers between devices with their start and end apart: 17, of which 7 were waited for; matrix products, arithmetic and copies ran while one was open for 0% of the time, Pallas kernels for 37%

profile of v4, /device:TPU:0, one launch (start us, length us, event | category | flops | bytes accessed | tf_op | source)
XLA Modules:
  0.0 105.9 jit_solution(12561726702346378356)
XLA Ops:
  0.6 0.0 copy-start.1
  0.6 0.0 copy-start.3
  0.7 3.6 %gather_blocks.2 = (bf16[2,2,4,16,512]{4,3,2,1,0:T(8,128)(2,1)S(1)}, bf16[2,2,4,16,512]{4,3,2,1,0:T(8,128)(2,1)}, bf16[2,2,4,16,512]{4,3,2,1,0:T(8,128)(2,1)S(1)...) custom-call(s32[16,32]{1,0:T(8,128)} %table.3, ...), custom_call_target="tpu_custom_call" | custom-call | flops 1 | bytes 1 | tf_op jit(solution)/shard_map/gather_blocks/pallas_call | solution.py:77
  4.2 4.0 %collective-permute-start.3 = (bf16[2,2,4,16,512]{4,3,2,1,0:T(8,128)(2,1)S(1)}, bf16[2,2,4,16,512]{4,3,2,1,0:T(8,128)(2,1)S(1)}, u32[]{:S(2)}, u32[]{:S(2)}) collective-permute-start(bf16[2,2,4,16,512]{4,3,2,1,0:T(8,128)(2,1)S(1)} %get-tuple-element.44), channel_id=1, source_target_pairs={{0,12},{4,8},{8,4},{12,0},{16,28},{20,24},{24,20},{28,16},{1,13},{... | collective-permute-start | bytes 786440 | tf_op jit(solution)/shard_map/ppermute | solution.py:561
  8.3 0.4 collective-permute-start.4
  8.7 3.6 %collective-permute-start.1 = (bf16[2,2,4,16,512]{4,3,2,1,0:T(8,128)(2,1)S(1)}, bf16[2,2,4,16,512]{4,3,2,1,0:T(8,128)(2,1)S(1)}, u32[]{:S(2)}, u32[]{:S(2)}) collective-permute-start(bf16[2,2,4,16,512]{4,3,2,1,0:T(8,128)(2,1)S(1)} %get-tuple-element.42), channel_id=1, source_target_pairs={{0,24},{4,28},{8,16},{12,20},{16,8},{20,12},{24,0},{28,4},{1,25},{... | collective-permute-start | bytes 786440 | tf_op jit(solution)/shard_map/ppermute | solution.py:561
  12.3 0.0 collective-permute-start
  12.3 1.0 collective-permute-start.2
  13.3 12.2 %project_qkv.1 = (f32[1024,512]{1,0:T(8,128)}, f32[1024,512]{1,0:T(8,128)}, bf16[1024,512]{1,0:T(8,128)(2,1)}, f32[8,1024]{1,0:T(8,128)S(1)}) custom-call(s32[16]{0:T(128)} %order.5, s32[16]{0:T(128)} %lengths.1, f32[1,128]{1,0:T(1,128)S(1)} %copy-done.3, f32[2,512,128]{2,1,0:T(8,128)S(1)} %copy-done.1, bf16[2,512]{1,0:T(2,128)(2,1)S(1)} %copy-done.2, ...), custom_call_target="tpu_custom_call" | custom-call | flops 1 | bytes 1 | tf_op jit(solution)/shard_map/project_qkv/pallas_call | solution.py:226
  25.5 0.0 collective-permute-done.3.refs_4_.refs_3_.rest_3_
  25.5 0.0 collective-permute-done.4.refs_3_.refs_2_.rest_4_
  25.5 6.8 %collective-permute-start.5 = (bf16[2,2,4,16,512]{4,3,2,1,0:T(8,128)(2,1)}, bf16[2,2,4,16,512]{4,3,2,1,0:T(8,128)(2,1)}, u32[]{:S(2)}, u32[]{:S(2)}) collective-permute-start(bf16[2,2,4,16,512]{4,3,2,1,0:T(8,128)(2,1)} %get-tuple-element.48), channel_id=1, source_target_pairs={{0,20},{4,16},{8,28},{12,24},{16,4},{20,0},{24,12},{28,8},{1,21},{... | collective-permute-start | bytes 786440 | tf_op jit(solution)/shard_map/ppermute | solution.py:561
  32.4 1.5 %collective-permute-start.6 = (bf16[2,2,4,16,512]{4,3,2,1,0:T(8,128)(2,1)}, bf16[2,2,4,16,512]{4,3,2,1,0:T(8,128)(2,1)}, u32[]{:S(2)}, u32[]{:S(2)}) collective-permute-start(bf16[2,2,4,16,512]{4,3,2,1,0:T(8,128)(2,1)} %get-tuple-element.49), channel_id=1, source_target_pairs={{0,4},{4,0},{8,12},{12,8},{16,20},{20,16},{24,28},{28,24},{1,5},{5... | collective-permute-start | bytes 786440 | tf_op jit(solution)/shard_map/ppermute | solution.py:561
  33.9 3.3 %gather_blocks.3.refs_0_ = bf16[8,2,2,4,16,512]{5,4,3,2,1,0:T(8,128)(2,1)} custom-call(s32[16,32]{1,0:T(8,128)} %table.3, s32[16]{0:T(128)} %order.5, bf16[4,64,16,512]{3,2,1,0:T(8,128)(2,1)} %pool.3, bf16[2,2,4,16,512]{4,3,2,1,0:T(8,128)(2,1)S(1)} %get-tuple-element.33.rest_0_.rest_5_), custom_call_target="tpu_custom_call" | custom-call | flops 1 | bytes 1 | tf_op jit(solution)/shard_map/gather_blocks/pallas_call | solution.py:77
  37.1 5.4 %all-gather = f32[32,1024]{1,0:T(8,128)S(1)} all-gather(f32[8,1024]{1,0:T(8,128)S(1)} %get-tuple-element.34.refs_2_), channel_id=2, replica_groups=mesh['req'=8,'tensor'=4] {'tensor'}, dimensions={0}, use_global_device_ids=true | all-gather | bytes 163840 | tf_op jit(solution)/shard_map/all_gather | solution.py:587
  42.6 6.8 %attend_new.1 = (bf16[1024,512]{1,0:T(8,128)(2,1)}, f32[2,512,512]{2,1,0:T(8,128)}, f32[16,1024]{1,0:T(8,128)S(1)}) custom-call(f32[4,8,1024]{2,1,0:T(8,128)S(1)} %bitcast.3, f32[1024,512]{1,0:T(8,128)} %get-tuple-element.35.rest_0_, f32[1024,512]{1,0:T(8,128)} %get-tuple-element.36.rest_1_, bf16[1024,512]{1,0:T(8,128)(2,1)} %get-tuple-element.37.rest_2_), custom_call_target="tpu_custom_call" | custom-call | flops 1 | bytes 1 | tf_op jit(solution)/shard_map/attend_new/pallas_call | solution.py:336
  49.4 0.0 collective-permute-done.1.refs_4_.rest_1_
  49.4 4.7 %all-to-all-start = ((bf16[8,2,2,4,16,512]{5,4,3,2,1,0:T(8,128)(2,1)}), bf16[8,2,2,4,16,512]{5,4,3,2,1,0:T(8,128)(2,1)}, u32[]{:S(2)}, u32[]{:S(2)}) async-start(bf16[8,2,2,4,16,512]{5,4,3,2,1,0:T(8,128)(2,1)} %hold.3.rest_8_.rest_9_), calls=%async_computation | async-start | bytes 4194304 | tf_op jit(solution)/shard_map/all_to_all | solution.py:597
  54.1 0.0 collective-permute-done.rest_0_
  54.1 0.0 collective-permute-done.2.rest_2_
  54.1 2.5 %collective-permute-done.5.rest_6_ = bf16[2,2,4,16,512]{4,3,2,1,0:T(8,128)(2,1)} collective-permute-done((bf16[2,2,4,16,512]{4,3,2,1,0:T(8,128)(2,1)}, bf16[2,2,4,16,512]{4,3,2,1,0:T(8,128)(2,1)}, u32[]{:S(2)}, u32[]{:S(2)}) %collective-permute-start.5) | collective-permute-done | bytes 262176 | tf_op jit(solution)/shard_map/ppermute | solution.py:561
  56.7 0.0 collective-permute-done.6.rest_7_
  56.7 6.9 %attend_old.2 = (bf16[4,2,4,8,16,512]{5,4,3,2,1,0:T(8,128)(2,1)}, bf16[512,512]{1,0:T(8,128)(2,1)S(1)}, bf16[512,512]{1,0:T(8,128)(2,1)S(1)}, bf16[512,512]{1,0:T(8,128)(2,1)S(1)}, bf16[512,512]{1,0:T(8,128)(2,1)S(1)}) custom-call(f32[16,1024]{1,0:T(8,128)S(1)} %get-tuple-element.38.refs_1_.state, bf16[1024,512]{1,0:T(8,128)(2,1)} %get-tuple-element.39.q_all, ...), custom_call_target="tpu_custom_call" | custom-call | flops 999999995904 | bytes 999999995904 | tf_op jit(solution)/shard_map/attend_old/pallas_call | solution.py:437
  63.6 0.1 collective-permute-start.7
  63.7 1.9 %collective-permute-done.7.second = bf16[512,512]{1,0:T(8,128)(2,1)S(1)} collective-permute-done((bf16[512,512]{1,0:T(8,128)(2,1)S(1)}, bf16[512,512]{1,0:T(8,128)(2,1)S(1)}, u32[]{:S(2)}, u32[]{:S(2)}) %collective-permute-start.7) | collective-permute-done | bytes 524320 | tf_op jit(solution)/shard_map/ppermute | solution.py:561
  65.6 0.1 add_terms.2.rest_10_
  65.7 1.6 %collective-permute-start.10 = (bf16[512,512]{1,0:T(8,128)(2,1)S(1)}, bf16[512,512]{1,0:T(8,128)(2,1)S(1)}, u32[]{:S(2)}, u32[]{:S(2)}) collective-permute-start(bf16[512,512]{1,0:T(8,128)(2,1)S(1)} %add_terms.2.rest_10_), channel_id=1, source_target_pairs={{0,2},{1,3},{2,0},{3,1},{4,6},{5,7},{6,4},{7,5},{8,10},{9,11},{10,... | collective-permute-start | bytes 1572872 | tf_op jit(solution)/shard_map/ppermute | solution.py:561
  67.3 6.3 %attend_old.3 = (bf16[4,2,4,8,16,512]{5,4,3,2,1,0:T(8,128)(2,1)}, bf16[512,512]{1,0:T(8,128)(2,1)S(1)}, bf16[512,512]{1,0:T(8,128)(2,1)S(1)}, bf16[512,512]{1,0:T(8,128)(2,1)S(1)}, bf16[512,512]{1,0:T(8,128)(2,1)S(1)}) custom-call(f32[16,1024]{1,0:T(8,128)S(1)} %get-tuple-element.38.refs_1_.state, ...), custom_call_target="tpu_custom_call", output_to_operand_aliasing={{0}: (12, {})} | custom-call | flops 1 | bytes 1 | tf_op jit(solution)/shard_map/attend_old/pallas_call | solution.py:437
  73.6 0.1 collective-permute-start.9
  73.6 0.5 collective-permute-start.12
  74.1 0.1 collective-permute-start.8
  74.2 5.5 %collective-permute-done.10.rest_0_.third = bf16[512,512]{1,0:T(8,128)(2,1)S(1)} collective-permute-done((bf16[512,512]{1,0:T(8,128)(2,1)S(1)}, bf16[512,512]{1,0:T(8,128)(2,1)S(1)}, u32[]{:S(2)}, u32[]{:S(2)}) %collective-permute-start.10) | collective-permute-done | bytes 524320 | tf_op jit(solution)/shard_map/ppermute | solution.py:561
  79.7 0.0 collective-permute-done.9.second
  79.7 0.1 add_terms.3
  79.9 0.0 copy-start.4
  79.9 1.6 %collective-permute-start.11 = (bf16[512,512]{1,0:T(8,128)(2,1)S(1)}, bf16[512,512]{1,0:T(8,128)(2,1)S(1)}, u32[]{:S(2)}, u32[]{:S(2)}) collective-permute-start(bf16[512,512]{1,0:T(8,128)(2,1)S(1)} %add_terms.3), channel_id=1, source_target_pairs={{0,2},{1,3},{2,0},{3,1},{4,6},{5,7},{6,4},{7,5},{8,10},{9,11},{10,... | collective-permute-start | bytes 1572872 | tf_op jit(solution)/shard_map/ppermute | solution.py:561
  81.4 0.0 collective-permute-done.12.second
  81.4 0.3 total_terms.2
  81.8 11.4 %collective-permute-done.11.third = bf16[512,512]{1,0:T(8,128)(2,1)S(1)} collective-permute-done((bf16[512,512]{1,0:T(8,128)(2,1)S(1)}, bf16[512,512]{1,0:T(8,128)(2,1)S(1)}, u32[]{:S(2)}, u32[]{:S(2)}) %collective-permute-start.11) | collective-permute-done | bytes 524320 | tf_op jit(solution)/shard_map/ppermute | solution.py:561
  93.2 0.3 total_terms.3
  93.5 0.1 collective-permute-start.13
  93.6 1.6 %collective-permute-start.14 = (f32[8,512]{1,0:T(8,128)S(1)}, f32[8,512]{1,0:T(8,128)S(1)}, u32[]{:S(2)}, u32[]{:S(2)}) collective-permute-start(f32[8,512]{1,0:T(8,128)S(1)} %get-tuple-element.60.rest_0_), channel_id=1, source_target_pairs={{0,2},{1,3},{2,0},{3,1},{4,6},{5,7},{6,4},{7,5},{8,10},{9,11},{10,... | collective-permute-start | bytes 49160 | tf_op jit(solution)/shard_map/ppermute | solution.py:561
  95.1 0.3 collective-permute-start.15
  95.4 1.9 %collective-permute-done.14.rest_2_ = f32[8,512]{1,0:T(8,128)S(1)} collective-permute-done((f32[8,512]{1,0:T(8,128)S(1)}, f32[8,512]{1,0:T(8,128)S(1)}, u32[]{:S(2)}, u32[]{:S(2)}) %collective-permute-start.14) | collective-permute-done | bytes 16416 | tf_op jit(solution)/shard_map/ppermute | solution.py:561
  97.4 0.9 collective-permute-done.15.rest_3_
  98.3 2.4 %finish_layer.1 = bf16[2,512,512]{2,1,0:T(8,128)(2,1)} custom-call(bf16[2,512,2048]{2,1,0:T(8,128)(2,1)} %residual.1, bf16[1,512]{1,0:T(2,128)(2,1)S(1)} %reshape.13.gain, f32[8,512]{1,0:T(8,128)S(1)} %get-tuple-element.60.rest_0_, f32[8,512]{1,0:T(8,128)S(1)} %collective-permute-done.13.rest_1_, f32[8,512]{1,0:T(8,128)S(1)} %collective-permute-done.14.rest_2_, ...), custom_call_target="tpu_custom_call" | custom-call | flops 1 | bytes 1 | tf_op jit(solution)/shard_map/finish_layer/pallas_call | solution.py:542
  100.7 2.2 %all-to-all-done.rest_1_ = bf16[8,2,2,4,16,512]{5,4,3,2,1,0:T(8,128)(2,1)} async-done(((bf16[8,2,2,4,16,512]{5,4,3,2,1,0:T(8,128)(2,1)}), bf16[8,2,2,4,16,512]{5,4,3,2,1,0:T(8,128)(2,1)}, u32[]{:S(2)}, u32[]{:S(2)}) %all-to-all-start) | async-done | bytes 2097184 | tf_op jit(solution)/shard_map/all_to_all | solution.py:597
  102.9 2.8 %place_blocks.1 = bf16[4,2,4,8,16,512]{5,4,3,2,1,0:T(8,128)(2,1)} custom-call(bf16[4,2,4,8,16,512]{5,4,3,2,1,0:T(8,128)(2,1)} %get-tuple-element.63.rest_0_, bf16[8,2,2,4,16,512]{5,4,3,2,1,0:T(8,128)(2,1)} %all-to-all-done.rest_1_), custom_call_target="tpu_custom_call", output_to_operand_aliasing={{}: (0, {})} | custom-call | flops 1 | bytes 1 | tf_op jit(solution)/shard_map/place_blocks/pallas_call | solution.py:106
  (12 shorter events, 0.0 us)
Async XLA Ops:
  0.6 12.7 %copy-start.1 = (f32[2,512,128]{2,1,0:T(8,128)S(1)}, f32[2,512,128]{2,1,0:T(8,128)}, u32[]{:S(2)}) copy-start(f32[2,512,128]{2,1,0:T(8,128)} %constant.5.clone.steps) | copy-start | bytes 1572868
  0.6 12.7 %copy-start.3 = (f32[1,128]{1,0:T(1,128)S(1)}, f32[1,128]{1,0:T(1,128)}, u32[]{:S(2)}) copy-start(f32[1,128]{1,0:T(1,128)} %constant.4.clone.frequency) | copy-start | bytes 1540
  0.7 12.7 %copy-start.2 = (bf16[2,512]{1,0:T(2,128)(2,1)S(1)}, bf16[2,512]{1,0:T(2,128)(2,1)}, u32[]{:S(2)}) copy-start(bf16[2,512]{1,0:T(2,128)(2,1)} %gain.1) | copy-start | bytes 6148
  4.2 21.3 %collective-permute-start.3 = (bf16[2,2,4,16,512]{4,3,2,1,0:T(8,128)(2,1)S(1)}, bf16[2,2,4,16,512]{4,3,2,1,0:T(8,128)(2,1)S(1)}, u32[]{:S(2)}, u32[]{:S(2)}) collective-permute-start(bf16[2,2,4,16,512]{4,3,2,1,0:T(8,128)(2,1)S(1)} %get-tuple-element.44), channel_id=1, source_target_pairs={{0,12},{4,8},{8,4},{12,0},{16,28},{20,24},{24,20},{28,16},{1,13},{... | collective-permute-start | bytes 786440 | tf_op jit(solution)/shard_map/ppermute | solution.py:561
  8.3 17.2 %collective-permute-start.4 = (bf16[2,2,4,16,512]{4,3,2,1,0:T(8,128)(2,1)S(1)}, bf16[2,2,4,16,512]{4,3,2,1,0:T(8,128)(2,1)S(1)}, u32[]{:S(2)}, u32[]{:S(2)}) collective-permute-start(bf16[2,2,4,16,512]{4,3,2,1,0:T(8,128)(2,1)S(1)} %get-tuple-element.45), channel_id=1, source_target_pairs={{0,8},{4,12},{8,0},{12,4},{16,24},{20,28},{24,16},{28,20},{1,9},{5... | collective-permute-start | bytes 786440 | tf_op jit(solution)/shard_map/ppermute | solution.py:561
  8.7 40.6 %collective-permute-start.1 = (bf16[2,2,4,16,512]{4,3,2,1,0:T(8,128)(2,1)S(1)}, bf16[2,2,4,16,512]{4,3,2,1,0:T(8,128)(2,1)S(1)}, u32[]{:S(2)}, u32[]{:S(2)}) collective-permute-start(bf16[2,2,4,16,512]{4,3,2,1,0:T(8,128)(2,1)S(1)} %get-tuple-element.42), channel_id=1, source_target_pairs={{0,24},{4,28},{8,16},{12,20},{16,8},{20,12},{24,0},{28,4},{1,25},{... | collective-permute-start | bytes 786440 | tf_op jit(solution)/shard_map/ppermute | solution.py:561
  12.3 41.8 %collective-permute-start = (bf16[2,2,4,16,512]{4,3,2,1,0:T(8,128)(2,1)}, bf16[2,2,4,16,512]{4,3,2,1,0:T(8,128)(2,1)S(1)}, u32[]{:S(2)}, u32[]{:S(2)}) collective-permute-start(bf16[2,2,4,16,512]{4,3,2,1,0:T(8,128)(2,1)} %get-tuple-element.41), channel_id=1, source_target_pairs={{0,28},{4,24},{8,20},{12,16},{16,12},{20,8},{24,4},{28,0},{1,29},{... | collective-permute-start | bytes 786440 | tf_op jit(solution)/shard_map/ppermute | solution.py:561
  12.3 41.8 %collective-permute-start.2 = (bf16[2,2,4,16,512]{4,3,2,1,0:T(8,128)(2,1)}, bf16[2,2,4,16,512]{4,3,2,1,0:T(8,128)(2,1)}, u32[]{:S(2)}, u32[]{:S(2)}) collective-permute-start(bf16[2,2,4,16,512]{4,3,2,1,0:T(8,128)(2,1)} %get-tuple-element.43), channel_id=1, source_target_pairs={{0,16},{4,20},{8,24},{12,28},{16,0},{20,4},{24,8},{28,12},{1,17},{... | collective-permute-start | bytes 786440 | tf_op jit(solution)/shard_map/ppermute | solution.py:561
  25.5 31.1 %collective-permute-start.5 = (bf16[2,2,4,16,512]{4,3,2,1,0:T(8,128)(2,1)}, bf16[2,2,4,16,512]{4,3,2,1,0:T(8,128)(2,1)}, u32[]{:S(2)}, u32[]{:S(2)}) collective-permute-start(bf16[2,2,4,16,512]{4,3,2,1,0:T(8,128)(2,1)} %get-tuple-element.48), channel_id=1, source_target_pairs={{0,20},{4,16},{8,28},{12,24},{16,4},{20,0},{24,12},{28,8},{1,21},{... | collective-permute-start | bytes 786440 | tf_op jit(solution)/shard_map/ppermute | solution.py:561
  32.4 24.3 %collective-permute-start.6 = (bf16[2,2,4,16,512]{4,3,2,1,0:T(8,128)(2,1)}, bf16[2,2,4,16,512]{4,3,2,1,0:T(8,128)(2,1)}, u32[]{:S(2)}, u32[]{:S(2)}) collective-permute-start(bf16[2,2,4,16,512]{4,3,2,1,0:T(8,128)(2,1)} %get-tuple-element.49), channel_id=1, source_target_pairs={{0,4},{4,0},{8,12},{12,8},{16,20},{20,16},{24,28},{28,24},{1,5},{5... | collective-permute-start | bytes 786440 | tf_op jit(solution)/shard_map/ppermute | solution.py:561
  49.4 7.3 %copy-start = (bf16[8,2,2,4,16,512]{5,4,3,2,1,0:T(8,128)(2,1)S(1)}, bf16[8,2,2,4,16,512]{5,4,3,2,1,0:T(8,128)(2,1)}, u32[]{:S(2)}) copy-start(bf16[8,2,2,4,16,512]{5,4,3,2,1,0:T(8,128)(2,1)} %hold.3.rest_8_.rest_9_) | copy-start | bytes 6291460
  49.4 53.5 %all-to-all-start = ((bf16[8,2,2,4,16,512]{5,4,3,2,1,0:T(8,128)(2,1)}), bf16[8,2,2,4,16,512]{5,4,3,2,1,0:T(8,128)(2,1)}, u32[]{:S(2)}, u32[]{:S(2)}) async-start(bf16[8,2,2,4,16,512]{5,4,3,2,1,0:T(8,128)(2,1)} %hold.3.rest_8_.rest_9_), calls=%async_computation | async-start | bytes 4194304 | tf_op jit(solution)/shard_map/all_to_all | solution.py:597
  63.6 2.0 %collective-permute-start.7 = (bf16[512,512]{1,0:T(8,128)(2,1)S(1)}, bf16[512,512]{1,0:T(8,128)(2,1)S(1)}, u32[]{:S(2)}, u32[]{:S(2)}) collective-permute-start(bf16[512,512]{1,0:T(8,128)(2,1)S(1)} %get-tuple-element.52), channel_id=1, source_target_pairs={{0,1},{1,0},{2,3},{3,2},{4,5},{5,4},{6,7},{7,6},{8,9},{9,8},{10,11... | collective-permute-start | bytes 1572872 | tf_op jit(solution)/shard_map/ppermute | solution.py:561
  65.7 14.0 %collective-permute-start.10 = (bf16[512,512]{1,0:T(8,128)(2,1)S(1)}, bf16[512,512]{1,0:T(8,128)(2,1)S(1)}, u32[]{:S(2)}, u32[]{:S(2)}) collective-permute-start(bf16[512,512]{1,0:T(8,128)(2,1)S(1)} %add_terms.2.rest_10_), channel_id=1, source_target_pairs={{0,2},{1,3},{2,0},{3,1},{4,6},{5,7},{6,4},{7,5},{8,10},{9,11},{10,... | collective-permute-start | bytes 1572872 | tf_op jit(solution)/shard_map/ppermute | solution.py:561
  73.6 6.2 %collective-permute-start.9 = (bf16[512,512]{1,0:T(8,128)(2,1)S(1)}, bf16[512,512]{1,0:T(8,128)(2,1)S(1)}, u32[]{:S(2)}, u32[]{:S(2)}) collective-permute-start(bf16[512,512]{1,0:T(8,128)(2,1)S(1)} %get-tuple-element.56), channel_id=1, source_target_pairs={{0,1},{1,0},{2,3},{3,2},{4,5},{5,4},{6,7},{7,6},{8,9},{9,8},{10,11... | collective-permute-start | bytes 1572872 | tf_op jit(solution)/shard_map/ppermute | solution.py:561
  73.6 7.8 %collective-permute-start.12 = (bf16[512,512]{1,0:T(8,128)(2,1)S(1)}, bf16[512,512]{1,0:T(8,128)(2,1)S(1)}, u32[]{:S(2)}, u32[]{:S(2)}) collective-permute-start(bf16[512,512]{1,0:T(8,128)(2,1)S(1)} %get-tuple-element.58), channel_id=1, source_target_pairs={{0,1},{1,0},{2,3},{3,2},{4,5},{5,4},{6,7},{7,6},{8,9},{9,8},{10,11... | collective-permute-start | bytes 1572872 | tf_op jit(solution)/shard_map/ppermute | solution.py:561
  74.1 7.6 %collective-permute-start.8 = (bf16[512,512]{1,0:T(8,128)(2,1)S(1)}, bf16[512,512]{1,0:T(8,128)(2,1)S(1)}, u32[]{:S(2)}, u32[]{:S(2)}) collective-permute-start(bf16[512,512]{1,0:T(8,128)(2,1)S(1)} %get-tuple-element.54), channel_id=1, source_target_pairs={{0,1},{1,0},{2,3},{3,2},{4,5},{5,4},{6,7},{7,6},{8,9},{9,8},{10,11... | collective-permute-start | bytes 1572872 | tf_op jit(solution)/shard_map/ppermute | solution.py:561
  79.9 15.6 %copy-start.4 = (bf16[512]{0:T(512)(128)(2,1)S(1)}, bf16[512]{0:T(512)(128)(2,1)}, u32[]{:S(2)}) copy-start(bf16[512]{0:T(512)(128)(2,1)} %param.15) | copy-start | bytes 3076
  79.9 13.3 %collective-permute-start.11 = (bf16[512,512]{1,0:T(8,128)(2,1)S(1)}, bf16[512,512]{1,0:T(8,128)(2,1)S(1)}, u32[]{:S(2)}, u32[]{:S(2)}) collective-permute-start(bf16[512,512]{1,0:T(8,128)(2,1)S(1)} %add_terms.3), channel_id=1, source_target_pairs={{0,2},{1,3},{2,0},{3,1},{4,6},{5,7},{6,4},{7,5},{8,10},{9,11},{10,... | collective-permute-start | bytes 1572872 | tf_op jit(solution)/shard_map/ppermute | solution.py:561
  93.5 2.0 %collective-permute-start.13 = (f32[8,512]{1,0:T(8,128)S(1)}, f32[8,512]{1,0:T(8,128)S(1)}, u32[]{:S(2)}, u32[]{:S(2)}) collective-permute-start(f32[8,512]{1,0:T(8,128)S(1)} %get-tuple-element.60.rest_0_), channel_id=1, source_target_pairs={{0,1},{1,0},{2,3},{3,2},{4,5},{5,4},{6,7},{7,6},{8,9},{9,8},{10,11... | collective-permute-start | bytes 49160 | tf_op jit(solution)/shard_map/ppermute | solution.py:561
  93.6 3.8 %collective-permute-start.14 = (f32[8,512]{1,0:T(8,128)S(1)}, f32[8,512]{1,0:T(8,128)S(1)}, u32[]{:S(2)}, u32[]{:S(2)}) collective-permute-start(f32[8,512]{1,0:T(8,128)S(1)} %get-tuple-element.60.rest_0_), channel_id=1, source_target_pairs={{0,2},{1,3},{2,0},{3,1},{4,6},{5,7},{6,4},{7,5},{8,10},{9,11},{10,... | collective-permute-start | bytes 49160 | tf_op jit(solution)/shard_map/ppermute | solution.py:561
  95.1 3.2 %collective-permute-start.15 = (f32[8,512]{1,0:T(8,128)S(1)}, f32[8,512]{1,0:T(8,128)S(1)}, u32[]{:S(2)}, u32[]{:S(2)}) collective-permute-start(f32[8,512]{1,0:T(8,128)S(1)} %get-tuple-element.60.rest_0_), channel_id=1, source_target_pairs={{0,3},{1,2},{2,1},{3,0},{4,7},{5,6},{6,5},{7,4},{8,11},{9,10},{10,... | collective-permute-start | bytes 49160 | tf_op jit(solution)/shard_map/ppermute | solution.py:561

commit v5 on v4

--- a/solution.py
+++ b/solution.py
@@ -36,88 +36,114 @@
     return [pltpu.with_memory_space_constraint(array, pltpu.HBM) for array in arrays]
 
 
-def gather_body(targets, first, planes, count, per_device, blocks, together, table, order, pool, *rest):
-    if together:
-        out, held, stored, loaded = rest[-4:]
-        places = [held.at[at] for at in range(len(targets))]
+EVERYONE = -1
+
+
+def gather_body(wanted, staged, count, per_device, blocks, table_all, order_all, pool, *rest):
+    total = len(wanted)
+    *rest, table, order, listed = rest
+    lists = [
+        pltpu.make_async_copy(source, held, listed.at[at])
+        for at, (source, held) in enumerate(((order_all, order), (table_all, table)))
+    ]
+    for copy in lists:
+        copy.start()
+    for copy in lists:
+        copy.wait()
+    if staged:
+        *rest, loaded, stored = rest
+        outs, places = rest[-2 * total : -total], rest[-total:]
     else:
-        places, loaded = rest[-1 - len(targets) : -1], rest[-1]
+        *rest, loaded = rest
+        places = rest[-total:]
     me = lax.axis_index("req")
-    for at, target in enumerate(targets):
-        if not together:
-            target = me ^ target
+
+    def load(target, first, planes, place, semaphore):
         for p in range(per_device):
             request = order[target * per_device + p]
             for b in range(blocks):
                 slot = table[request, b * count + me]
                 pltpu.make_async_copy(
-                    pool.at[pl.ds(first, planes), slot], places[at].at[:, p, b], loaded.at[at]
+                    pool.at[pl.ds(first, planes), slot], place.at[:, p, b], semaphore
                 ).start()
+
+    for at, (kind, first, planes) in enumerate(wanted):
+        if kind == EVERYONE:
+            for target in range(count):
+                load(target, first, planes, places[at].at[target], loaded.at[at])
+        else:
+            load(me ^ kind, first, planes, places[at], loaded.at[at])
     stores = []
     for at, place in enumerate(places):
         pltpu.make_async_copy(place, place, loaded.at[at]).wait()
-        if together:
-            stores.append(pltpu.make_async_copy(place, out.at[at], stored.at[at]))
+        if staged:
+            stores.append(pltpu.make_async_copy(place, outs[at], stored.at[at]))
             stores[-1].start()
     for store in stores:
         store.wait()
 
 
-def gather(pool, table, order, count, targets, first, planes, together, after=()):
+def gather(pool, table, order, count, wanted, staged, after=()):
     per_device = order.shape[0] // count
     blocks = table.shape[1] // count
-    piece = (planes, per_device, blocks) + pool.shape[2:]
-    whole = (len(targets),) + piece
-    if together:
-        shapes = [pltpu.HBM(whole, pool.dtype)]
-        staging = [pltpu.VMEM(whole, pool.dtype), pltpu.SemaphoreType.DMA((len(targets),))]
-    else:
-        shapes = [pltpu.VMEM(piece, pool.dtype)] * len(targets)
-        staging = []
-    return pl.pallas_call(
-        functools.partial(gather_body, targets, first, planes, count, per_device, blocks, together),
-        in_specs=[SMEM, SMEM, ANY] + [ANY] * len(after),
-        out_specs=[ANY if together else VMEM] * len(shapes),
-        out_shape=shapes,
-        scratch_shapes=staging + [pltpu.SemaphoreType.DMA((len(targets),))],
-        cost_estimate=cost(0, 4 * math.prod(whole)),
+    lead = {EVERYONE: (count,)}
+    shapes = [
+        lead.get(kind, ()) + (planes, per_device, blocks) + pool.shape[2:]
+        for kind, _, planes in wanted
+    ]
+    where = pltpu.HBM if staged else pltpu.VMEM
+    semaphores = pltpu.SemaphoreType.DMA((len(wanted),))
+    staging = [pltpu.VMEM(shape, pool.dtype) for shape in shapes] + [semaphores] if staged else []
+    return pl.pallas_call(
+        functools.partial(gather_body, wanted, staged, count, per_device, blocks),
+        in_specs=[ANY] * (3 + len(after)),
+        out_specs=[ANY if staged else VMEM] * len(shapes),
+        out_shape=[where(shape, pool.dtype) for shape in shapes],
+        scratch_shapes=staging
+        + [semaphores]
+        + [pltpu.SMEM(table.shape, table.dtype), pltpu.SMEM(order.shape, order.dtype)]
+        + [pltpu.SemaphoreType.DMA((2,))],
+        cost_estimate=cost(0, 0),
         compiler_params=params(8),
         name="gather_blocks",
     )(*in_hbm(table, order, pool), *after)
 
 
-def place_body(offsets, first, planes, together, filled, *rest):
-    out, held, loaded, stored = rest[-4:]
-    received = rest[1:] if filled else rest
-    me = lax.axis_index("req")
-    for at, offset in enumerate(offsets):
-        source = me ^ offset
-        piece = received[0].at[source] if together else received[at]
-        pltpu.make_async_copy(piece, held.at[:, :, :, source], loaded).start()
-    pltpu.make_async_copy(held, held, loaded).wait()
-    store = pltpu.make_async_copy(held, out.at[pl.ds(first, planes)], stored)
-    store.start()
-    store.wait()
-
-
-def place(shape, offsets, first, planes, together, received, filled=None, after=(), weight=1):
-    start = [] if filled is None else [filled]
-    dtype = received[0].dtype
-    return pl.pallas_call(
-        functools.partial(place_body, offsets, first, planes, together, filled is not None),
-        in_specs=[ANY] * (len(start) + len(received) + len(after)),
+def place_body(first, planes, filled, received, out, held, loaded, stored):
+    del filled
+    count, _, per_device = received.shape[:3]
+    chunks = [(plane, p) for plane in range(planes) for p in range(per_device)]
+    for plane, p in chunks:
+        for source in range(count):
+            pltpu.make_async_copy(
+                received.at[source, plane, p], held.at[plane, p, :, source], loaded.at[plane, p]
+            ).start()
+    stores = []
+    for plane, p in chunks:
+        here = held.at[plane, p]
+        pltpu.make_async_copy(here, here, loaded.at[plane, p]).wait()
+        stores.append(pltpu.make_async_copy(here, out.at[first + plane, p], stored.at[plane, p]))
+        stores[-1].start()
+    for store in stores:
+        store.wait()
+
+
+def place(shape, first, planes, received, filled):
+    return pl.pallas_call(
+        functools.partial(place_body, first, planes),
+        in_specs=[ANY] * 2,
         out_specs=ANY,
-        out_shape=pltpu.HBM(shape, dtype),
+        out_shape=pltpu.HBM(shape, filled.dtype),
         scratch_shapes=[
-            pltpu.VMEM((planes,) + shape[1:], dtype),
-            pltpu.SemaphoreType.DMA,
-            pltpu.SemaphoreType.DMA,
-        ],
-        input_output_aliases={} if filled is None else {0: 0},
-        cost_estimate=pl.CostEstimate(flops=weight, bytes_accessed=weight, transcendentals=0),
+            pltpu.VMEM((planes,) + shape[1:], filled.dtype),
+            pltpu.SemaphoreType.DMA((planes, shape[1])),
+            pltpu.SemaphoreType.DMA((planes, shape[1])),
+        ],
+        input_output_aliases={0: 0},
+        cost_estimate=cost(0, 0),
         compiler_params=params(8),
         name="place_blocks",
-    )(*start, *received, *after)
+    )(filled, received)
 
 
 def hold_body(*refs):
@@ -359,8 +385,8 @@
 
 def attend_old_body(which, span, offsets, q_block, filled, after, state, q_all, mixed_all, w, *rest):
     received, rest = rest[: len(offsets)], rest[len(offsets) + int(filled) + after :]
-    relaid, outs = rest[0], rest[1:-9]
-    held, q, mixed, w_held, attended, loaded, q_loaded, w_loaded, stored = rest[-9:]
+    relaid, attended, keep, send = rest[:4]
+    held, q, mixed, w_held, loaded, q_loaded, w_loaded, stored = rest[4:]
     me = lax.axis_index("req")
     q_load = pltpu.make_async_copy(q_all.at[pl.ds(which * span, span)], q, q_loaded.at[0])
     mixed_load = pltpu.make_async_copy(mixed_all.at[which], mixed, q_loaded.at[1])
@@ -373,12 +399,18 @@
             ).start()
     mixed_load.start()
     w_load.start()
-    q_load.wait()
-    for plane in range(held.shape[0]):
+    stores = [
+        pltpu.make_async_copy(held.at[plane], relaid.at[plane, which], stored.at[plane])
+        for plane in range(held.shape[0])
+    ]
+
+    def arrive(plane, *others):
+        for other in others:
+            other.wait()
         pltpu.make_async_copy(held.at[plane], held.at[plane], loaded.at[plane]).wait()
-    mixed_load.wait()
-    store = pltpu.make_async_copy(held, relaid.at[pl.ds(0, held.shape[0]), which], stored)
-    store.start()
+        stores[plane].start()
+
+    arrive(0, q_load)
     context = math.prod(held.shape[1:4])
     token = lax.broadcasted_iota(jnp.int32, (context, q_block), 0).astype(jnp.float32)
     heads = q.shape[1] // HD
@@ -386,7 +418,7 @@
     for head in range(heads):
         columns = slice(head * HD, (head + 1) * HD)
         keys = held[0, :, :, :, columns].reshape(context, HD)
-        values = jnp.transpose(held[1, :, :, :, columns].reshape(context, HD))
+        values = None
         for low in range(0, span, q_block):
             rows = slice(which * span + low, which * span + low + q_block)
             scores = lax.dot_general(
@@ -399,64 +431,83 @@
             shrink = jnp.exp2(before - top)
             total = state[heads + head : heads + head + 1, rows] * shrink
             total += jnp.sum(scores, axis=0, keepdims=True)
+            if values is None:
+                if head == 0:
+                    arrive(1, mixed_load)
+                values = jnp.transpose(held[1, :, :, :, columns].reshape(context, HD))
             sums = mixed[columns, low : low + q_block] * shrink
             sums += jnp.dot(values, scores.astype(jnp.bfloat16), preferred_element_type=jnp.float32)
             attended[low : low + q_block, columns] = jnp.transpose((sums / total)).astype(attended.dtype)
     w_load.wait()
-    width = w.shape[1] // len(outs)
+    group_terms(attended, w_held, ((send, 3), (keep, 2)))
+    for store in stores:
+        store.wait()
+
+
+def group_terms(attended, w, wanted):
     mine = lax.axis_index("tensor")
-    for at, out in enumerate(outs):
-        group = pl.ds(pl.multiple_of((mine ^ at) * width, width), width)
+    for out, offset in wanted:
+        width = out.shape[1]
+        columns = pl.ds(pl.multiple_of((mine ^ offset) * width, width), width)
         out[...] = jnp.dot(
-            attended[...], w_held[:, group], preferred_element_type=jnp.float32
+            attended[...], w[:, columns], preferred_element_type=jnp.float32
         ).astype(out.dtype)
-    store.wait()
 
 
 def attend_old(
-    which,
-    span,
-    q,
-    mixed,
-    state,
-    w,
-    count,
-    offsets,
-    received,
-    shape,
-    filled=None,
-    after=(),
-    weight=1,
-    q_block=256,
+    which, span, q, mixed, state, w, part, offsets, received, shape, filled=None, after=(), weight=1, q_block=256
 ):
     width = q.shape[1]
     q_block = min(q_block, span)
     start = [] if filled is None else [filled]
-    part = w.shape[1] // count
-    dtype = received[0].dtype
     return pl.pallas_call(
         functools.partial(
             attend_old_body, which, span, offsets, q_block, filled is not None, len(after)
         ),
         in_specs=[VMEM] + [ANY] * (3 + len(received) + len(start) + len(after)),
-        out_specs=[ANY] + [VMEM] * count,
-        out_shape=[pltpu.HBM(shape, dtype)] + [pltpu.VMEM((span, part), jnp.bfloat16)] * count,
+        out_specs=[ANY] + [VMEM] * 3,
+        out_shape=[
+            pltpu.HBM(shape, received[0].dtype),
+            pltpu.VMEM((span, width), jnp.bfloat16),
+            pltpu.VMEM((span, part), jnp.bfloat16),
+            pltpu.VMEM((span, part), jnp.bfloat16),
+        ],
         scratch_shapes=[
-            pltpu.VMEM(received[0].shape[:1] + shape[2:], dtype),
+            pltpu.VMEM((2,) + shape[2:], received[0].dtype),
             pltpu.VMEM((span, width), q.dtype),
             pltpu.VMEM((width, span), mixed.dtype),
             pltpu.VMEM(w.shape, w.dtype),
-            pltpu.VMEM((span, width), jnp.bfloat16),
-            pltpu.SemaphoreType.DMA((received[0].shape[0],)),
+            pltpu.SemaphoreType.DMA((2,)),
             pltpu.SemaphoreType.DMA((2,)),
             pltpu.SemaphoreType.DMA,
-            pltpu.SemaphoreType.DMA,
+            pltpu.SemaphoreType.DMA((2,)),
         ],
         input_output_aliases={} if filled is None else {4 + len(received): 0},
         cost_estimate=pl.CostEstimate(flops=weight, bytes_accessed=weight, transcendentals=0),
         compiler_params=params(16),
         name="attend_old",
     )(state, *in_hbm(q, mixed, w), *received, *start, *after)
+
+
+def own_terms_body(attended, w, keep, send, w_held, loaded):
+    load = pltpu.make_async_copy(w, w_held, loaded)
+    load.start()
+    load.wait()
+    group_terms(attended, w_held, ((send, 1), (keep, 0)))
+
+
+def own_terms(attended, w, part):
+    span = attended.shape[0]
+    return pl.pallas_call(
+        own_terms_body,
+        in_specs=[VMEM, ANY],
+        out_specs=[VMEM] * 2,
+        out_shape=[pltpu.VMEM((span, part), jnp.bfloat16)] * 2,
+        scratch_shapes=[pltpu.VMEM(w.shape, w.dtype), pltpu.SemaphoreType.DMA],
+        cost_estimate=cost(1, 1),
+        compiler_params=params(8),
+        name="own_terms",
+    )(*in_vmem(attended), *in_hbm(w))
 
 
 def add_body(first, second, *rest):
@@ -575,37 +626,38 @@
     others = list(range(req_count - 1, 0, -1))
     early = [s for s in others if s not in LATE]
     late = [s for s in others if s in LATE]
-    sent = dict(zip([0] + others, hand([0] + others, 0, 2, False)))
+    rest = planes - 2
+    sent = dict(zip(early, hand([(s, 0, 2) for s in early], False)))
     received = {s: permuted(sent[s], "req", s) for s in early}
-    own = received[0] = sent[0]
+    others = hand([(s, 0, 2) for s in late + [0]], True, after=(sent[early[0]],))
+    sent.update(zip(late + [0], others))
+    received[0] = sent[0]
 
     flat_in = span_in.reshape(-1, full_width)
     q_raw, k_raw, values, squares = project(
-        per_device, request_order, lengths, flat_in, w_qkv, qk_gain, after=(own,)
+        per_device, request_order, lengths, flat_in, w_qkv, qk_gain, after=in_hbm(sent[0])
     )
     own_squares = squares
     squares = lax.all_gather(squares, "tensor")
     queries, mixed, state = attend_new(full_width, span_len, q_raw, k_raw, values, squares)
     arrived = [received[s] for s in reversed(early)]
-    sent_late = hold([sent[s] for s in late], (own_squares, *arrived[:2]), pltpu.VMEM)
+    sent_late = hold([sent[s] for s in late], (own_squares, *arrived[:2]))
     received.update({s: permuted(piece, "req", s) for s, piece in zip(late, sent_late)})
 
-    rest = planes - 2
-    everyone = list(range(req_count))
-    (sent_rest,) = hand(everyone, 2, rest, True, after=(own,))
+    (sent_rest,) = hand([(EVERYONE, 2, rest)], True, after=(state,))
     (sent_rest,) = hold((sent_rest,), (state, *arrived[:2], received[GATE]))
     received_rest = lax.all_to_all(sent_rest, "req", 0, 0)
 
     relaid, across, added, totals, row_squares = None, (), (), [], ()
     for p in range(per_device):
-        relaid, *terms = attend_old(
+        relaid, attended, keep_far, send_far = attend_old(
             p,
             span_len,
             queries,
             mixed,
             state,
             w_out,
-            tensor_count,
+            part_width,
             list(received),
             list(received.values()),
             shape,
@@ -613,18 +665,19 @@
             after=(sent_rest, *added),
             weight=1 if p else 10**12,
         )
-        far = permuted(terms[3], "tensor", 1)
-        near = permuted(terms[1], "tensor", 1)
-        added = [add(terms[2], far, after=across)]
+        added = [add(keep_far, permuted(send_far, "tensor", 1), after=across)]
         across = [permuted(added[0], "tensor", 2)]
-        total, *row_squares = total_of(p, terms[0], near, across[0], row_squares)
+        keep, send = own_terms(attended, w_out, part_width)
+        total, *row_squares = total_of(
+            p, keep, permuted(send, "tensor", 1), across[0], row_squares
+        )
         totals.append(total)
     row_squares = row_squares + [
         permuted(row_squares[0], "tensor", at) for at in range(1, tensor_count)
     ]
     layer_out = finish(span_in, totals, row_squares, post_gain)
 
-    relaid = place(shape, everyone, 2, rest, True, [received_rest], filled=relaid)
+    relaid = place(shape, 2, rest, received_rest, relaid)
     return layer_out, relaid.reshape(planes, per_device, -1, part_width)
 
 

time: 107 us -> 106 us (level)
  Pallas kernels: 45.1 us -> 49.7 us
  starting transfers between devices: 27.8 us -> 25.2 us
  waiting for transfers between devices: 26.5 us -> 24.1 us
    pallas_call x3 -> x6, Pallas kernels: 9.66 us -> 16.5 us  [the longest x3 9.46 us: gather(): pl.pallas_call(functools.partial(gather_body, wanted, staged, count, per_...]
    ppermute x16, waiting for transfers between devices: 24.3 us -> 19.9 us  [permuted(): return lax.ppermute(value, axis, [(i, i ^ offset) for i in range(size)])]
    ppermute x16, starting transfers between devices: 23.2 us -> 20.5 us  [permuted(): return lax.ppermute(value, axis, [(i, i ^ offset) for i in range(size)])]
    pallas_call x2, Pallas kernels: 13.2 us -> 10.9 us  [attend_old(): pl.pallas_call(functools.partial(attend_old_body, which, span, offsets, q...]
    all_to_all x1, waiting for transfers between devices: 2.25 us -> 4.22 us  [on_device(): received_rest = lax.all_to_all(sent_rest, 'req', 0, 0)]
  transfers between devices with their start and end apart: 17 -> 17, of which waited for: 7 -> 7; matrix products, arithmetic and copies ran while one was open for 0% -> 0% of each run, Pallas kernels for 37% -> 42%
where the time goes in v5:
time: 106 us; the launch traced here: 105 us
  Pallas kernels  49.7 us (47%)
  starting transfers between devices  25.2 us (24%)
  waiting for transfers between devices  24.1 us (23%)
  blocking collectives  5.41 us (5%)
    ppermute x16, starting transfers between devices, permuted(): return lax.ppermute(value, axis, [(i, i ^ offset) for i in range(size)])  20.5 us
    ppermute x16, waiting for transfers between devices, permuted(): return lax.ppermute(value, axis, [(i, i ^ offset) for i in range(size)])  19.9 us
    pallas_call x1, Pallas kernels, project(): pl.pallas_call(functools.partial(project_body, per_device, block, len(aft...  12.2 us
    pallas_call x2, Pallas kernels, attend_old(): pl.pallas_call(functools.partial(attend_old_body, which, span, offsets, q...  10.9 us
    pallas_call x3, Pallas kernels, gather(): pl.pallas_call(functools.partial(gather_body, wanted, staged, count, per_...  9.46 us
    pallas_call x1, Pallas kernels, attend_new(): pl.pallas_call(functools.partial(attend_new_body, full_width, span, q_blo...  6.8 us
    all_gather x1, blocking collectives, on_device(): squares = lax.all_gather(squares, 'tensor')  5.41 us
    all_to_all x1, starting transfers between devices, on_device(): received_rest = lax.all_to_all(sent_rest, 'req', 0, 0)  4.68 us
  transfers between devices with their start and end apart: 17, of which 7 were waited for; matrix products, arithmetic and copies ran while one was open for 0% of the time, Pallas kernels for 42%

profile of v5, /device:TPU:0, one launch (start us, length us, event | category | flops | bytes accessed | tf_op | source)
XLA Modules:
  0.0 105.4 jit_solution(17705642676427103204)
XLA Ops:
  0.6 3.0 %gather_blocks.3 = (bf16[2,2,4,16,512]{4,3,2,1,0:T(8,128)(2,1)}, bf16[2,2,4,16,512]{4,3,2,1,0:T(8,128)(2,1)S(1)}, bf16[2,2,4,16,512]{4,3,2,1,0:T(8,128)(2,1)}, b...) custom-call(s32[16,32]{1,0:T(8,128)} %table_all.5, s32[16]{0:T(128)} %order_all.5, ...), custom_call_target="tpu_custom_call" | custom-call | flops 1 | bytes 1 | tf_op jit(solution)/shard_map/gather_blocks/pallas_call | solution.py:97
  3.6 4.0 %collective-permute-start.3 = (bf16[2,2,4,16,512]{4,3,2,1,0:T(8,128)(2,1)S(1)}, bf16[2,2,4,16,512]{4,3,2,1,0:T(8,128)(2,1)S(1)}, u32[]{:S(2)}, u32[]{:S(2)}) collective-permute-start(bf16[2,2,4,16,512]{4,3,2,1,0:T(8,128)(2,1)S(1)} %get-tuple-element.46), channel_id=1, source_target_pairs={{0,12},{4,8},{8,4},{12,0},{16,28},{20,24},{24,20},{28,16},{1,13},{... | collective-permute-start | bytes 786440 | tf_op jit(solution)/shard_map/ppermute | solution.py:612
  7.7 0.4 collective-permute-start.4
  8.1 3.6 %collective-permute-start.1 = (bf16[2,2,4,16,512]{4,3,2,1,0:T(8,128)(2,1)S(1)}, bf16[2,2,4,16,512]{4,3,2,1,0:T(8,128)(2,1)S(1)}, u32[]{:S(2)}, u32[]{:S(2)}) collective-permute-start(bf16[2,2,4,16,512]{4,3,2,1,0:T(8,128)(2,1)S(1)} %get-tuple-element.44), channel_id=1, source_target_pairs={{0,24},{4,28},{8,16},{12,20},{16,8},{20,12},{24,0},{28,4},{1,25},{... | collective-permute-start | bytes 786440 | tf_op jit(solution)/shard_map/ppermute | solution.py:612
  11.7 0.0 collective-permute-start
  11.8 0.9 collective-permute-start.2
  12.7 2.7 %gather_blocks.4 = (bf16[2,2,4,16,512]{4,3,2,1,0:T(8,128)(2,1)}, bf16[2,2,4,16,512]{4,3,2,1,0:T(8,128)(2,1)}, bf16[2,2,4,16,512]{4,3,2,1,0:T(8,128)(2,1)}) custom-call(s32[16,32]{1,0:T(8,128)} %table_all.5, s32[16]{0:T(128)} %order_all.5, bf16[4,64,16,512]{3,2,1,0:T(8,128)(2,1)} %pool.5, bf16[2,2,4,16,512]{4,3,2,1,0:T(8,128)(2,1)} %get-tuple-element.35.rest_0_), custom_call_target="tpu_custom_call" | custom-call | flops 1 | bytes 1 | tf_op jit(solution)/shard_map/gather_blocks/pallas_call | solution.py:97
  15.4 12.2 %project_qkv.1 = (f32[1024,512]{1,0:T(8,128)}, f32[1024,512]{1,0:T(8,128)}, bf16[1024,512]{1,0:T(8,128)(2,1)}, f32[8,1024]{1,0:T(8,128)S(1)}) custom-call(s32[16]{0:T(128)} %order_all.5, s32[16]{0:T(128)} %lengths.1, f32[1,128]{1,0:T(1,128)S(1)} %copy-done.4, f32[2,512,128]{2,1,0:T(8,128)S(1)} %copy-done.2, bf16[2,512]{1,0:T(2,128)(2,1)S(1)} %copy-done.3, ...), custom_call_target="tpu_custom_call" | custom-call | flops 1 | bytes 1 | tf_op jit(solution)/shard_map/project_qkv/pallas_call | solution.py:252
  27.6 0.0 collective-permute-done.3.refs_4_.refs_3_.rest_3_
  27.7 4.1 %collective-permute-start.5 = (bf16[2,2,4,16,512]{4,3,2,1,0:T(8,128)(2,1)}, bf16[2,2,4,16,512]{4,3,2,1,0:T(8,128)(2,1)}, u32[]{:S(2)}, u32[]{:S(2)}) collective-permute-start(bf16[2,2,4,16,512]{4,3,2,1,0:T(8,128)(2,1)} %get-tuple-element.50), channel_id=1, source_target_pairs={{0,20},{4,16},{8,28},{12,24},{16,4},{20,0},{24,12},{28,8},{1,21},{... | collective-permute-start | bytes 786440 | tf_op jit(solution)/shard_map/ppermute | solution.py:612
  31.8 1.5 %collective-permute-start.6 = (bf16[2,2,4,16,512]{4,3,2,1,0:T(8,128)(2,1)}, bf16[2,2,4,16,512]{4,3,2,1,0:T(8,128)(2,1)}, u32[]{:S(2)}, u32[]{:S(2)}) collective-permute-start(bf16[2,2,4,16,512]{4,3,2,1,0:T(8,128)(2,1)} %get-tuple-element.51), channel_id=1, source_target_pairs={{0,4},{4,0},{8,12},{12,8},{16,20},{20,16},{24,28},{28,24},{1,5},{5... | collective-permute-start | bytes 786440 | tf_op jit(solution)/shard_map/ppermute | solution.py:612
  33.3 5.4 %all-gather = f32[32,1024]{1,0:T(8,128)S(1)} all-gather(f32[8,1024]{1,0:T(8,128)S(1)} %get-tuple-element.37.refs_2_), channel_id=2, replica_groups=mesh['req'=8,'tensor'=4] {'tensor'}, dimensions={0}, use_global_device_ids=true | all-gather | bytes 163840 | tf_op jit(solution)/shard_map/all_gather | solution.py:641
  38.7 6.8 %attend_new.1 = (bf16[1024,512]{1,0:T(8,128)(2,1)}, f32[2,512,512]{2,1,0:T(8,128)}, f32[16,1024]{1,0:T(8,128)S(1)}) custom-call(f32[4,8,1024]{2,1,0:T(8,128)S(1)} %bitcast.3, f32[1024,512]{1,0:T(8,128)} %get-tuple-element.38.rest_0_, f32[1024,512]{1,0:T(8,128)} %get-tuple-element.39.rest_1_, bf16[1024,512]{1,0:T(8,128)(2,1)} %get-tuple-element.40.rest_2_), custom_call_target="tpu_custom_call" | custom-call | flops 1 | bytes 1 | tf_op jit(solution)/shard_map/attend_new/pallas_call | solution.py:362
  45.5 3.8 %gather_blocks.5.refs_0_ = bf16[8,2,2,4,16,512]{5,4,3,2,1,0:T(8,128)(2,1)} custom-call(s32[16,32]{1,0:T(8,128)} %table_all.5, s32[16]{0:T(128)} %order_all.5, bf16[4,64,16,512]{3,2,1,0:T(8,128)(2,1)} %pool.5, f32[16,1024]{1,0:T(8,128)S(1)} %get-tuple-element.41.rest_0_.refs_1_.state), custom_call_target="tpu_custom_call" | custom-call | flops 1 | bytes 1 | tf_op jit(solution)/shard_map/gather_blocks/pallas_call | solution.py:97
  49.3 4.7 %all-to-all-start = ((bf16[8,2,2,4,16,512]{5,4,3,2,1,0:T(8,128)(2,1)}), bf16[8,2,2,4,16,512]{5,4,3,2,1,0:T(8,128)(2,1)}, u32[]{:S(2)}, u32[]{:S(2)}) async-start(bf16[8,2,2,4,16,512]{5,4,3,2,1,0:T(8,128)(2,1)} %hold.3.rest_8_.rest_9_), calls=%async_computation | async-start | bytes 4194304 | tf_op jit(solution)/shard_map/all_to_all | solution.py:649
  54.0 0.0 collective-permute-done.rest_0_
  54.0 0.0 collective-permute-done.2.rest_2_
  54.0 2.0 %collective-permute-done.5.rest_6_ = bf16[2,2,4,16,512]{4,3,2,1,0:T(8,128)(2,1)} collective-permute-done((bf16[2,2,4,16,512]{4,3,2,1,0:T(8,128)(2,1)}, bf16[2,2,4,16,512]{4,3,2,1,0:T(8,128)(2,1)}, u32[]{:S(2)}, u32[]{:S(2)}) %collective-permute-start.5) | collective-permute-done | bytes 262176 | tf_op jit(solution)/shard_map/ppermute | solution.py:612
  56.0 0.0 collective-permute-done.6.rest_7_
  56.1 5.4 %attend_old.2 = (bf16[4,2,4,8,16,512]{5,4,3,2,1,0:T(8,128)(2,1)}, bf16[512,512]{1,0:T(8,128)(2,1)S(1)}, bf16[512,512]{1,0:T(8,128)(2,1)S(1)}, bf16[512,512]{1,0:T(8,128)(2,1)S(1)}) custom-call(f32[16,1024]{1,0:T(8,128)S(1)} %get-tuple-element.41.rest_0_.refs_1_.state, bf16[1024,512]{1,0:T(8,128)(2,1)} %get-tuple-element.42.q_all, ...), custom_call_target="tpu_custom_call" | custom-call | flops 999999995904 | bytes 999999995904 | tf_op jit(solution)/shard_map/attend_old/pallas_call | solution.py:463
  61.5 0.1 collective-permute-start.7
  61.6 1.9 %collective-permute-done.7.second = bf16[512,512]{1,0:T(8,128)(2,1)S(1)} collective-permute-done((bf16[512,512]{1,0:T(8,128)(2,1)S(1)}, bf16[512,512]{1,0:T(8,128)(2,1)S(1)}, u32[]{:S(2)}, u32[]{:S(2)}) %collective-permute-start.7) | collective-permute-done | bytes 524320 | tf_op jit(solution)/shard_map/ppermute | solution.py:612
  63.5 0.1 add_terms.2.rest_10_
  63.6 1.6 %collective-permute-start.10 = (bf16[512,512]{1,0:T(8,128)(2,1)S(1)}, bf16[512,512]{1,0:T(8,128)(2,1)S(1)}, u32[]{:S(2)}, u32[]{:S(2)}) collective-permute-start(bf16[512,512]{1,0:T(8,128)(2,1)S(1)} %add_terms.2.rest_10_), channel_id=1, source_target_pairs={{0,2},{1,3},{2,0},{3,1},{4,6},{5,7},{6,4},{7,5},{8,10},{9,11},{10,... | collective-permute-start | bytes 1572872 | tf_op jit(solution)/shard_map/ppermute | solution.py:612
  65.2 5.4 %attend_old.3 = (bf16[4,2,4,8,16,512]{5,4,3,2,1,0:T(8,128)(2,1)}, bf16[512,512]{1,0:T(8,128)(2,1)S(1)}, bf16[512,512]{1,0:T(8,128)(2,1)S(1)}, bf16[512,512]{1,0:T(8,128)(2,1)S(1)}) custom-call(f32[16,1024]{1,0:T(8,128)S(1)} %get-tuple-element.41.rest_0_.refs_1_.state, bf16[1024,512]{1,0:T(8,128)(2,1)} %get-tuple-element.42.q_all, ...), custom_call_target="tpu_custom_call", output_to_operand_aliasing={{0}: (12, {})} | custom-call | flops 1 | bytes 1 | tf_op jit(solution)/shard_map/attend_old/pallas_call | solution.py:463
  70.6 0.1 collective-permute-start.9
  70.7 2.3 %own_terms.3 = (bf16[512,512]{1,0:T(8,128)(2,1)S(1)}, bf16[512,512]{1,0:T(8,128)(2,1)S(1)}) custom-call(bf16[512,512]{1,0:T(8,128)(2,1)S(1)} %get-tuple-element.60.attended, bf16[512,2048]{1,0:T(8,128)(2,1)} %w.9), custom_call_target="tpu_custom_call" | custom-call | flops 1 | bytes 1 | tf_op jit(solution)/shard_map/own_terms/pallas_call | solution.py:501
  73.0 0.6 collective-permute-start.12
  73.6 2.3 %own_terms.2 = (bf16[512,512]{1,0:T(8,128)(2,1)S(1)}, bf16[512,512]{1,0:T(8,128)(2,1)S(1)}) custom-call(bf16[512,512]{1,0:T(8,128)(2,1)S(1)} %get-tuple-element.55.attended, bf16[512,2048]{1,0:T(8,128)(2,1)} %w.9), custom_call_target="tpu_custom_call" | custom-call | flops 1 | bytes 1 | tf_op jit(solution)/shard_map/own_terms/pallas_call | solution.py:501
  75.9 0.1 collective-permute-start.8
  76.0 1.7 %collective-permute-done.10.rest_0_.third = bf16[512,512]{1,0:T(8,128)(2,1)S(1)} collective-permute-done((bf16[512,512]{1,0:T(8,128)(2,1)S(1)}, bf16[512,512]{1,0:T(8,128)(2,1)S(1)}, u32[]{:S(2)}, u32[]{:S(2)}) %collective-permute-start.10) | collective-permute-done | bytes 524320 | tf_op jit(solution)/shard_map/ppermute | solution.py:612
  77.6 0.0 collective-permute-done.9.second
  77.6 0.1 add_terms.3
  77.8 0.0 copy-start.5
  77.8 1.6 %collective-permute-start.11 = (bf16[512,512]{1,0:T(8,128)(2,1)S(1)}, bf16[512,512]{1,0:T(8,128)(2,1)S(1)}, u32[]{:S(2)}, u32[]{:S(2)}) collective-permute-start(bf16[512,512]{1,0:T(8,128)(2,1)S(1)} %add_terms.3), channel_id=1, source_target_pairs={{0,2},{1,3},{2,0},{3,1},{4,6},{5,7},{6,4},{7,5},{8,10},{9,11},{10,... | collective-permute-start | bytes 1572872 | tf_op jit(solution)/shard_map/ppermute | solution.py:612
  79.3 0.0 collective-permute-done.12.second
  79.3 0.3 total_terms.2
  79.7 0.0 collective-permute-done.8.second
  79.7 11.4 %collective-permute-done.11.third = bf16[512,512]{1,0:T(8,128)(2,1)S(1)} collective-permute-done((bf16[512,512]{1,0:T(8,128)(2,1)S(1)}, bf16[512,512]{1,0:T(8,128)(2,1)S(1)}, u32[]{:S(2)}, u32[]{:S(2)}) %collective-permute-start.11) | collective-permute-done | bytes 524320 | tf_op jit(solution)/shard_map/ppermute | solution.py:612
  91.1 0.3 total_terms.3
  91.4 0.1 collective-permute-start.13
  91.5 1.6 %collective-permute-start.14 = (f32[8,512]{1,0:T(8,128)S(1)}, f32[8,512]{1,0:T(8,128)S(1)}, u32[]{:S(2)}, u32[]{:S(2)}) collective-permute-start(f32[8,512]{1,0:T(8,128)S(1)} %get-tuple-element.64.rest_0_), channel_id=1, source_target_pairs={{0,2},{1,3},{2,0},{3,1},{4,6},{5,7},{6,4},{7,5},{8,10},{9,11},{10,... | collective-permute-start | bytes 49160 | tf_op jit(solution)/shard_map/ppermute | solution.py:612
  93.0 0.3 collective-permute-start.15
  93.4 1.9 %collective-permute-done.14.rest_2_ = f32[8,512]{1,0:T(8,128)S(1)} collective-permute-done((f32[8,512]{1,0:T(8,128)S(1)}, f32[8,512]{1,0:T(8,128)S(1)}, u32[]{:S(2)}, u32[]{:S(2)}) %collective-permute-start.14) | collective-permute-done | bytes 16416 | tf_op jit(solution)/shard_map/ppermute | solution.py:612
  95.3 0.9 collective-permute-done.15.rest_3_
  96.2 2.4 %finish_layer.1 = bf16[2,512,512]{2,1,0:T(8,128)(2,1)} custom-call(bf16[2,512,2048]{2,1,0:T(8,128)(2,1)} %residual.1, bf16[1,512]{1,0:T(2,128)(2,1)S(1)} %reshape.13.gain, f32[8,512]{1,0:T(8,128)S(1)} %get-tuple-element.64.rest_0_, f32[8,512]{1,0:T(8,128)S(1)} %collective-permute-done.13.rest_1_, f32[8,512]{1,0:T(8,128)S(1)} %collective-permute-done.14.rest_2_, ...), custom_call_target="tpu_custom_call" | custom-call | flops 1 | bytes 1 | tf_op jit(solution)/shard_map/finish_layer/pallas_call | solution.py:593
  98.6 4.2 %all-to-all-done.received = bf16[8,2,2,4,16,512]{5,4,3,2,1,0:T(8,128)(2,1)} async-done(((bf16[8,2,2,4,16,512]{5,4,3,2,1,0:T(8,128)(2,1)}), bf16[8,2,2,4,16,512]{5,4,3,2,1,0:T(8,128)(2,1)}, u32[]{:S(2)}, u32[]{:S(2)}) %all-to-all-start) | async-done | bytes 2097184 | tf_op jit(solution)/shard_map/all_to_all | solution.py:649
  102.8 2.4 %place_blocks.1 = bf16[4,2,4,8,16,512]{5,4,3,2,1,0:T(8,128)(2,1)} custom-call(bf16[4,2,4,8,16,512]{5,4,3,2,1,0:T(8,128)(2,1)} %get-tuple-element.67.filled, bf16[8,2,2,4,16,512]{5,4,3,2,1,0:T(8,128)(2,1)} %all-to-all-done.received), custom_call_target="tpu_custom_call", output_to_operand_aliasing={{}: (0, {})} | custom-call | flops 1 | bytes 1 | tf_op jit(solution)/shard_map/place_blocks/pallas_call | solution.py:132
  (17 shorter events, 0.0 us)
Async XLA Ops:
  3.6 24.0 %collective-permute-start.3 = (bf16[2,2,4,16,512]{4,3,2,1,0:T(8,128)(2,1)S(1)}, bf16[2,2,4,16,512]{4,3,2,1,0:T(8,128)(2,1)S(1)}, u32[]{:S(2)}, u32[]{:S(2)}) collective-permute-start(bf16[2,2,4,16,512]{4,3,2,1,0:T(8,128)(2,1)S(1)} %get-tuple-element.46), channel_id=1, source_target_pairs={{0,12},{4,8},{8,4},{12,0},{16,28},{20,24},{24,20},{28,16},{1,13},{... | collective-permute-start | bytes 786440 | tf_op jit(solution)/shard_map/ppermute | solution.py:612
  7.7 20.0 %collective-permute-start.4 = (bf16[2,2,4,16,512]{4,3,2,1,0:T(8,128)(2,1)S(1)}, bf16[2,2,4,16,512]{4,3,2,1,0:T(8,128)(2,1)S(1)}, u32[]{:S(2)}, u32[]{:S(2)}) collective-permute-start(bf16[2,2,4,16,512]{4,3,2,1,0:T(8,128)(2,1)S(1)} %get-tuple-element.47), channel_id=1, source_target_pairs={{0,8},{4,12},{8,0},{12,4},{16,24},{20,28},{24,16},{28,20},{1,9},{5... | collective-permute-start | bytes 786440 | tf_op jit(solution)/shard_map/ppermute | solution.py:612
  8.1 41.1 %collective-permute-start.1 = (bf16[2,2,4,16,512]{4,3,2,1,0:T(8,128)(2,1)S(1)}, bf16[2,2,4,16,512]{4,3,2,1,0:T(8,128)(2,1)S(1)}, u32[]{:S(2)}, u32[]{:S(2)}) collective-permute-start(bf16[2,2,4,16,512]{4,3,2,1,0:T(8,128)(2,1)S(1)} %get-tuple-element.44), channel_id=1, source_target_pairs={{0,24},{4,28},{8,16},{12,20},{16,8},{20,12},{24,0},{28,4},{1,25},{... | collective-permute-start | bytes 786440 | tf_op jit(solution)/shard_map/ppermute | solution.py:612
  11.7 42.2 %collective-permute-start = (bf16[2,2,4,16,512]{4,3,2,1,0:T(8,128)(2,1)}, bf16[2,2,4,16,512]{4,3,2,1,0:T(8,128)(2,1)S(1)}, u32[]{:S(2)}, u32[]{:S(2)}) collective-permute-start(bf16[2,2,4,16,512]{4,3,2,1,0:T(8,128)(2,1)} %get-tuple-element.35.rest_0_), channel_id=1, source_target_pairs={{0,28},{4,24},{8,20},{12,16},{16,12},{20,8},{24,4},{28,0},{1,29},{... | collective-permute-start | bytes 786440 | tf_op jit(solution)/shard_map/ppermute | solution.py:612
  11.7 3.7 %copy-start.2 = (f32[2,512,128]{2,1,0:T(8,128)S(1)}, f32[2,512,128]{2,1,0:T(8,128)}, u32[]{:S(2)}) copy-start(f32[2,512,128]{2,1,0:T(8,128)} %constant.5.clone.steps) | copy-start | bytes 1572868
  11.7 3.7 %copy-start.3 = (bf16[2,512]{1,0:T(2,128)(2,1)S(1)}, bf16[2,512]{1,0:T(2,128)(2,1)}, u32[]{:S(2)}) copy-start(bf16[2,512]{1,0:T(2,128)(2,1)} %gain.1) | copy-start | bytes 6148
  11.7 3.7 %copy-start.4 = (f32[1,128]{1,0:T(1,128)S(1)}, f32[1,128]{1,0:T(1,128)}, u32[]{:S(2)}) copy-start(f32[1,128]{1,0:T(1,128)} %constant.4.clone.frequency) | copy-start | bytes 1540
  11.8 42.2 %collective-permute-start.2 = (bf16[2,2,4,16,512]{4,3,2,1,0:T(8,128)(2,1)}, bf16[2,2,4,16,512]{4,3,2,1,0:T(8,128)(2,1)}, u32[]{:S(2)}, u32[]{:S(2)}) collective-permute-start(bf16[2,2,4,16,512]{4,3,2,1,0:T(8,128)(2,1)} %get-tuple-element.45), channel_id=1, source_target_pairs={{0,16},{4,20},{8,24},{12,28},{16,0},{20,4},{24,8},{28,12},{1,17},{... | collective-permute-start | bytes 786440 | tf_op jit(solution)/shard_map/ppermute | solution.py:612
  27.7 28.4 %collective-permute-start.5 = (bf16[2,2,4,16,512]{4,3,2,1,0:T(8,128)(2,1)}, bf16[2,2,4,16,512]{4,3,2,1,0:T(8,128)(2,1)}, u32[]{:S(2)}, u32[]{:S(2)}) collective-permute-start(bf16[2,2,4,16,512]{4,3,2,1,0:T(8,128)(2,1)} %get-tuple-element.50), channel_id=1, source_target_pairs={{0,20},{4,16},{8,28},{12,24},{16,4},{20,0},{24,12},{28,8},{1,21},{... | collective-permute-start | bytes 786440 | tf_op jit(solution)/shard_map/ppermute | solution.py:612
  31.8 24.3 %collective-permute-start.6 = (bf16[2,2,4,16,512]{4,3,2,1,0:T(8,128)(2,1)}, bf16[2,2,4,16,512]{4,3,2,1,0:T(8,128)(2,1)}, u32[]{:S(2)}, u32[]{:S(2)}) collective-permute-start(bf16[2,2,4,16,512]{4,3,2,1,0:T(8,128)(2,1)} %get-tuple-element.51), channel_id=1, source_target_pairs={{0,4},{4,0},{8,12},{12,8},{16,20},{20,16},{24,28},{28,24},{1,5},{5... | collective-permute-start | bytes 786440 | tf_op jit(solution)/shard_map/ppermute | solution.py:612
  49.3 6.8 %copy-start = (bf16[8,2,2,4,16,512]{5,4,3,2,1,0:T(8,128)(2,1)S(1)}, bf16[8,2,2,4,16,512]{5,4,3,2,1,0:T(8,128)(2,1)}, u32[]{:S(2)}) copy-start(bf16[8,2,2,4,16,512]{5,4,3,2,1,0:T(8,128)(2,1)} %hold.3.rest_8_.rest_9_) | copy-start | bytes 6291460
  49.3 6.8 %copy-start.1 = (bf16[2,2,4,16,512]{4,3,2,1,0:T(8,128)(2,1)S(1)}, bf16[2,2,4,16,512]{4,3,2,1,0:T(8,128)(2,1)}, u32[]{:S(2)}) copy-start(bf16[2,2,4,16,512]{4,3,2,1,0:T(8,128)(2,1)} %get-tuple-element.36.rest_0_.rest_5_) | copy-start | bytes 786436
  49.3 53.5 %all-to-all-start = ((bf16[8,2,2,4,16,512]{5,4,3,2,1,0:T(8,128)(2,1)}), bf16[8,2,2,4,16,512]{5,4,3,2,1,0:T(8,128)(2,1)}, u32[]{:S(2)}, u32[]{:S(2)}) async-start(bf16[8,2,2,4,16,512]{5,4,3,2,1,0:T(8,128)(2,1)} %hold.3.rest_8_.rest_9_), calls=%async_computation | async-start | bytes 4194304 | tf_op jit(solution)/shard_map/all_to_all | solution.py:649
  61.5 2.0 %collective-permute-start.7 = (bf16[512,512]{1,0:T(8,128)(2,1)S(1)}, bf16[512,512]{1,0:T(8,128)(2,1)S(1)}, u32[]{:S(2)}, u32[]{:S(2)}) collective-permute-start(bf16[512,512]{1,0:T(8,128)(2,1)S(1)} %get-tuple-element.54), channel_id=1, source_target_pairs={{0,1},{1,0},{2,3},{3,2},{4,5},{5,4},{6,7},{7,6},{8,9},{9,8},{10,11... | collective-permute-start | bytes 1572872 | tf_op jit(solution)/shard_map/ppermute | solution.py:612
  63.6 14.0 %collective-permute-start.10 = (bf16[512,512]{1,0:T(8,128)(2,1)S(1)}, bf16[512,512]{1,0:T(8,128)(2,1)S(1)}, u32[]{:S(2)}, u32[]{:S(2)}) collective-permute-start(bf16[512,512]{1,0:T(8,128)(2,1)S(1)} %add_terms.2.rest_10_), channel_id=1, source_target_pairs={{0,2},{1,3},{2,0},{3,1},{4,6},{5,7},{6,4},{7,5},{8,10},{9,11},{10,... | collective-permute-start | bytes 1572872 | tf_op jit(solution)/shard_map/ppermute | solution.py:612
  70.6 7.0 %collective-permute-start.9 = (bf16[512,512]{1,0:T(8,128)(2,1)S(1)}, bf16[512,512]{1,0:T(8,128)(2,1)S(1)}, u32[]{:S(2)}, u32[]{:S(2)}) collective-permute-start(bf16[512,512]{1,0:T(8,128)(2,1)S(1)} %get-tuple-element.59), channel_id=1, source_target_pairs={{0,1},{1,0},{2,3},{3,2},{4,5},{5,4},{6,7},{7,6},{8,9},{9,8},{10,11... | collective-permute-start | bytes 1572872 | tf_op jit(solution)/shard_map/ppermute | solution.py:612
  73.0 6.3 %collective-permute-start.12 = (bf16[512,512]{1,0:T(8,128)(2,1)S(1)}, bf16[512,512]{1,0:T(8,128)(2,1)S(1)}, u32[]{:S(2)}, u32[]{:S(2)}) collective-permute-start(bf16[512,512]{1,0:T(8,128)(2,1)S(1)} %get-tuple-element.62), channel_id=1, source_target_pairs={{0,1},{1,0},{2,3},{3,2},{4,5},{5,4},{6,7},{7,6},{8,9},{9,8},{10,11... | collective-permute-start | bytes 1572872 | tf_op jit(solution)/shard_map/ppermute | solution.py:612
  75.9 3.8 %collective-permute-start.8 = (bf16[512,512]{1,0:T(8,128)(2,1)S(1)}, bf16[512,512]{1,0:T(8,128)(2,1)S(1)}, u32[]{:S(2)}, u32[]{:S(2)}) collective-permute-start(bf16[512,512]{1,0:T(8,128)(2,1)S(1)} %get-tuple-element.57), channel_id=1, source_target_pairs={{0,1},{1,0},{2,3},{3,2},{4,5},{5,4},{6,7},{7,6},{8,9},{9,8},{10,11... | collective-permute-start | bytes 1572872 | tf_op jit(solution)/shard_map/ppermute | solution.py:612
  77.8 15.6 %copy-start.5 = (bf16[512]{0:T(512)(128)(2,1)S(1)}, bf16[512]{0:T(512)(128)(2,1)}, u32[]{:S(2)}) copy-start(bf16[512]{0:T(512)(128)(2,1)} %param.15) | copy-start | bytes 3076
  77.8 13.3 %collective-permute-start.11 = (bf16[512,512]{1,0:T(8,128)(2,1)S(1)}, bf16[512,512]{1,0:T(8,128)(2,1)S(1)}, u32[]{:S(2)}, u32[]{:S(2)}) collective-permute-start(bf16[512,512]{1,0:T(8,128)(2,1)S(1)} %add_terms.3), channel_id=1, source_target_pairs={{0,2},{1,3},{2,0},{3,1},{4,6},{5,7},{6,4},{7,5},{8,10},{9,11},{10,... | collective-permute-start | bytes 1572872 | tf_op jit(solution)/shard_map/ppermute | solution.py:612
  91.4 2.0 %collective-permute-start.13 = (f32[8,512]{1,0:T(8,128)S(1)}, f32[8,512]{1,0:T(8,128)S(1)}, u32[]{:S(2)}, u32[]{:S(2)}) collective-permute-start(f32[8,512]{1,0:T(8,128)S(1)} %get-tuple-element.64.rest_0_), channel_id=1, source_target_pairs={{0,1},{1,0},{2,3},{3,2},{4,5},{5,4},{6,7},{7,6},{8,9},{9,8},{10,11... | collective-permute-start | bytes 49160 | tf_op jit(solution)/shard_map/ppermute | solution.py:612
  91.5 3.8 %collective-permute-start.14 = (f32[8,512]{1,0:T(8,128)S(1)}, f32[8,512]{1,0:T(8,128)S(1)}, u32[]{:S(2)}, u32[]{:S(2)}) collective-permute-start(f32[8,512]{1,0:T(8,128)S(1)} %get-tuple-element.64.rest_0_), channel_id=1, source_target_pairs={{0,2},{1,3},{2,0},{3,1},{4,6},{5,7},{6,4},{7,5},{8,10},{9,11},{10,... | collective-permute-start | bytes 49160 | tf_op jit(solution)/shard_map/ppermute | solution.py:612
  93.0 3.2 %collective-permute-start.15 = (f32[8,512]{1,0:T(8,128)S(1)}, f32[8,512]{1,0:T(8,128)S(1)}, u32[]{:S(2)}, u32[]{:S(2)}) collective-permute-start(f32[8,512]{1,0:T(8,128)S(1)} %get-tuple-element.64.rest_0_), channel_id=1, source_target_pairs={{0,3},{1,2},{2,1},{3,0},{4,7},{5,6},{6,5},{7,4},{8,11},{9,10},{10,... | collective-permute-start | bytes 49160 | tf_op jit(solution)/shard_map/ppermute | solution.py:612

commit v6 on v5

--- a/solution.py
+++ b/solution.py
@@ -212,6 +212,16 @@
         angle = length * frequency[...]
         starts.append((jnp.cos(angle), jnp.sin(angle)))
         squares[2:3, p * span : (p + 1) * span] = jnp.full((1, span), length)
+
+    def keep(which, here):
+        at = pl.ds(here.start, block)
+        stores.append(
+            pltpu.make_async_copy(
+                helds[which].at[at], outs[which].at[at], stored.at[which, here.start // block]
+            )
+        )
+        stores[-1].start()
+
     for which, out in enumerate(helds):
         w_loads[which].wait()
         for low in range(0, rows, block):
@@ -221,6 +231,7 @@
             raw = jnp.dot(x_held[here], w_held[which], preferred_element_type=jnp.float32)
             if which == 2:
                 out[here] = raw.astype(out.dtype)
+                keep(which, here)
                 continue
             step = slice(low % span, low % span + block)
             cos_start, sin_start = starts[low // span]
@@ -235,8 +246,7 @@
                 folded += squared[:, at : at + HD]
             squares[which : which + 1, here] = jnp.sum(jnp.transpose(folded), axis=0, keepdims=True)
             out[here] = turned(raw * gain[which : which + 1].astype(jnp.float32), cosine, sine)
-        stores.append(pltpu.make_async_copy(out, outs[which], stored.at[which]))
-        stores[-1].start()
+            keep(which, here)
     for store in stores:
         store.wait()
 
@@ -267,7 +277,7 @@
             pltpu.VMEM((rows, width), jnp.bfloat16),
             pltpu.SemaphoreType.DMA((rows // block,)),
             pltpu.SemaphoreType.DMA((3,)),
-            pltpu.SemaphoreType.DMA((3,)),
+            pltpu.SemaphoreType.DMA((3, rows // block)),
         ],
         cost_estimate=cost(1, 1),
         compiler_params=params(24),
@@ -283,6 +293,11 @@
     q_final, mixed_final, state, *helds, q_out, mixed_out, loaded, stored = rest
     q, k, v = helds
     stores = []
+
+    def keep(held, final, *number):
+        stores.append(pltpu.make_async_copy(held, final, stored.at[number]))
+        stores[-1].start()
+
     heads = q.shape[1] // HD
     loads = []
     for base in range(0, q.shape[0], span):
@@ -348,9 +363,8 @@
                 mixed_out[base // span, columns, low:high] = mixed
                 state[head : head + 1, place] = top
                 state[heads + head : heads + head + 1, place] = total
-        for at, (held, final) in enumerate(((q_out.at[here], q_final.at[here]), (mixed_out.at[base // span], mixed_final.at[base // span]))):
-            stores.append(pltpu.make_async_copy(held, final, stored.at[base // span, at]))
-            stores[-1].start()
+            keep(mixed_out.at[base // span, columns], mixed_final.at[base // span, columns], base // span, head)
+        keep(q_out.at[here], q_final.at[here], base // span, heads)
     for store in stores:
         store.wait()
 
@@ -375,7 +389,7 @@
             pltpu.VMEM((rows, width), jnp.bfloat16),
             pltpu.VMEM((rows // span, width, span), jnp.float32),
             pltpu.SemaphoreType.DMA((rows // span, 3)),
-            pltpu.SemaphoreType.DMA((rows // span, 2)),
+            pltpu.SemaphoreType.DMA((rows // span, width // HD + 1)),
         ],
         cost_estimate=cost(1, 1),
         compiler_params=params(20),
@@ -641,7 +655,9 @@
     squares = lax.all_gather(squares, "tensor")
     queries, mixed, state = attend_new(full_width, span_len, q_raw, k_raw, values, squares)
     arrived = [received[s] for s in reversed(early)]
-    sent_late = hold([sent[s] for s in late], (own_squares, *arrived[:2]))
+    sent_late = [
+        hold((sent[s],), (own_squares, first))[0] for s, first in zip(late, arrived[1::-1])
+    ]
     received.update({s: permuted(piece, "req", s) for s, piece in zip(late, sent_late)})
 
     (sent_rest,) = hand([(EVERYONE, 2, rest)], True, after=(state,))

time: 106 us -> 106 us (level)
    ppermute x16, starting transfers between devices: 20.5 us -> 18.4 us  [permuted(): return lax.ppermute(value, axis, [(i, i ^ offset) for i in range(size)])]
    all_to_all x1, starting transfers between devices: 4.68 us -> 6.07 us  [on_device(): received_rest = lax.all_to_all(sent_rest, 'req', 0, 0)]
where the time goes in v6:
time: 106 us; the launch traced here: 105 us
  Pallas kernels  49.5 us (47%)
  starting transfers between devices  24.5 us (23%)
  waiting for transfers between devices  24.1 us (23%)
  blocking collectives  5.41 us (5%)
    ppermute x16, waiting for transfers between devices, permuted(): return lax.ppermute(value, axis, [(i, i ^ offset) for i in range(size)])  20.7 us
    ppermute x16, starting transfers between devices, permuted(): return lax.ppermute(value, axis, [(i, i ^ offset) for i in range(size)])  18.4 us
    pallas_call x1, Pallas kernels, project(): pl.pallas_call(functools.partial(project_body, per_device, block, len(aft...  12 us
    pallas_call x2, Pallas kernels, attend_old(): pl.pallas_call(functools.partial(attend_old_body, which, span, offsets, q...  10.9 us
    pallas_call x3, Pallas kernels, gather(): pl.pallas_call(functools.partial(gather_body, wanted, staged, count, per_...  9.47 us
    pallas_call x1, Pallas kernels, attend_new(): pl.pallas_call(functools.partial(attend_new_body, full_width, span, q_blo...  6.77 us
    all_to_all x1, starting transfers between devices, on_device(): received_rest = lax.all_to_all(sent_rest, 'req', 0, 0)  6.07 us
    all_gather x1, blocking collectives, on_device(): squares = lax.all_gather(squares, 'tensor')  5.41 us
  transfers between devices with their start and end apart: 17, of which 7 were waited for; matrix products, arithmetic and copies ran while one was open for 0% of the time, Pallas kernels for 42%

profile of v6, /device:TPU:0, one launch (start us, length us, event | category | flops | bytes accessed | tf_op | source)
XLA Modules:
  0.0 104.6 jit_solution(4721160363345479997)
XLA Ops:
  0.6 3.0 %gather_blocks.3 = (bf16[2,2,4,16,512]{4,3,2,1,0:T(8,128)(2,1)}, bf16[2,2,4,16,512]{4,3,2,1,0:T(8,128)(2,1)S(1)}, bf16[2,2,4,16,512]{4,3,2,1,0:T(8,128)(2,1)}, b...) custom-call(s32[16,32]{1,0:T(8,128)} %table_all.5, s32[16]{0:T(128)} %order_all.5, ...), custom_call_target="tpu_custom_call" | custom-call | flops 1 | bytes 1 | tf_op jit(solution)/shard_map/gather_blocks/pallas_call | solution.py:97
  3.6 4.0 %collective-permute-start.3 = (bf16[2,2,4,16,512]{4,3,2,1,0:T(8,128)(2,1)S(1)}, bf16[2,2,4,16,512]{4,3,2,1,0:T(8,128)(2,1)S(1)}, u32[]{:S(2)}, u32[]{:S(2)}) collective-permute-start(bf16[2,2,4,16,512]{4,3,2,1,0:T(8,128)(2,1)S(1)} %get-tuple-element.44), channel_id=1, source_target_pairs={{0,12},{4,8},{8,4},{12,0},{16,28},{20,24},{24,20},{28,16},{1,13},{... | collective-permute-start | bytes 786440 | tf_op jit(solution)/shard_map/ppermute | solution.py:626
  7.7 0.4 collective-permute-start.4
  8.1 3.6 %collective-permute-start.1 = (bf16[2,2,4,16,512]{4,3,2,1,0:T(8,128)(2,1)S(1)}, bf16[2,2,4,16,512]{4,3,2,1,0:T(8,128)(2,1)S(1)}, u32[]{:S(2)}, u32[]{:S(2)}) collective-permute-start(bf16[2,2,4,16,512]{4,3,2,1,0:T(8,128)(2,1)S(1)} %get-tuple-element.42), channel_id=1, source_target_pairs={{0,24},{4,28},{8,16},{12,20},{16,8},{20,12},{24,0},{28,4},{1,25},{... | collective-permute-start | bytes 786440 | tf_op jit(solution)/shard_map/ppermute | solution.py:626
  11.7 0.0 collective-permute-start
  11.8 0.9 collective-permute-start.2
  12.7 2.7 %gather_blocks.4 = (bf16[2,2,4,16,512]{4,3,2,1,0:T(8,128)(2,1)}, bf16[2,2,4,16,512]{4,3,2,1,0:T(8,128)(2,1)}, bf16[2,2,4,16,512]{4,3,2,1,0:T(8,128)(2,1)}) custom-call(s32[16,32]{1,0:T(8,128)} %table_all.5, s32[16]{0:T(128)} %order_all.5, bf16[4,64,16,512]{3,2,1,0:T(8,128)(2,1)} %pool.5, bf16[2,2,4,16,512]{4,3,2,1,0:T(8,128)(2,1)} %get-tuple-element.33.rest_0_), custom_call_target="tpu_custom_call" | custom-call | flops 1 | bytes 1 | tf_op jit(solution)/shard_map/gather_blocks/pallas_call | solution.py:97
  15.4 12.0 %project_qkv.1 = (f32[1024,512]{1,0:T(8,128)}, f32[1024,512]{1,0:T(8,128)}, bf16[1024,512]{1,0:T(8,128)(2,1)}, f32[8,1024]{1,0:T(8,128)S(1)}) custom-call(s32[16]{0:T(128)} %order_all.5, s32[16]{0:T(128)} %lengths.1, f32[1,128]{1,0:T(1,128)S(1)} %copy-done.4, f32[2,512,128]{2,1,0:T(8,128)S(1)} %copy-done.2, bf16[2,512]{1,0:T(2,128)(2,1)S(1)} %copy-done.3, ...), custom_call_target="tpu_custom_call" | custom-call | flops 1 | bytes 1 | tf_op jit(solution)/shard_map/project_qkv/pallas_call | solution.py:262
  27.5 0.0 collective-permute-done.3.refs_2_.refs_3_.rest_3_
  27.5 3.2 %collective-permute-start.5 = (bf16[2,2,4,16,512]{4,3,2,1,0:T(8,128)(2,1)}, bf16[2,2,4,16,512]{4,3,2,1,0:T(8,128)(2,1)}, u32[]{:S(2)}, u32[]{:S(2)}) collective-permute-start(bf16[2,2,4,16,512]{4,3,2,1,0:T(8,128)(2,1)} %hold.3), channel_id=1, source_target_pairs={{0,20},{4,16},{8,28},{12,24},{16,4},{20,0},{24,12},{28,8},{1,21},{... | collective-permute-start | bytes 786440 | tf_op jit(solution)/shard_map/ppermute | solution.py:626
  30.6 0.0 collective-permute-done.4.refs_2_.rest_4_
  30.6 0.4 collective-permute-start.6
  31.1 5.4 %all-gather = f32[32,1024]{1,0:T(8,128)S(1)} all-gather(f32[8,1024]{1,0:T(8,128)S(1)} %get-tuple-element.35.refs_1_), channel_id=2, replica_groups=mesh['req'=8,'tensor'=4] {'tensor'}, dimensions={0}, use_global_device_ids=true | all-gather | bytes 163840 | tf_op jit(solution)/shard_map/all_gather | solution.py:655
  36.5 6.8 %attend_new.1 = (bf16[1024,512]{1,0:T(8,128)(2,1)}, f32[2,512,512]{2,1,0:T(8,128)}, f32[16,1024]{1,0:T(8,128)S(1)}) custom-call(f32[4,8,1024]{2,1,0:T(8,128)S(1)} %bitcast.3, f32[1024,512]{1,0:T(8,128)} %get-tuple-element.36.rest_0_, f32[1024,512]{1,0:T(8,128)} %get-tuple-element.37.rest_1_, bf16[1024,512]{1,0:T(8,128)(2,1)} %get-tuple-element.38.rest_2_), custom_call_target="tpu_custom_call" | custom-call | flops 1 | bytes 1 | tf_op jit(solution)/shard_map/attend_new/pallas_call | solution.py:376
  43.2 3.8 %gather_blocks.5.refs_0_ = bf16[8,2,2,4,16,512]{5,4,3,2,1,0:T(8,128)(2,1)} custom-call(s32[16,32]{1,0:T(8,128)} %table_all.5, s32[16]{0:T(128)} %order_all.5, bf16[4,64,16,512]{3,2,1,0:T(8,128)(2,1)} %pool.5, f32[16,1024]{1,0:T(8,128)S(1)} %get-tuple-element.39.rest_0_.refs_1_.state), custom_call_target="tpu_custom_call" | custom-call | flops 1 | bytes 1 | tf_op jit(solution)/shard_map/gather_blocks/pallas_call | solution.py:97
  47.1 6.1 %all-to-all-start = ((bf16[8,2,2,4,16,512]{5,4,3,2,1,0:T(8,128)(2,1)}), bf16[8,2,2,4,16,512]{5,4,3,2,1,0:T(8,128)(2,1)}, u32[]{:S(2)}, u32[]{:S(2)}) async-start(bf16[8,2,2,4,16,512]{5,4,3,2,1,0:T(8,128)(2,1)} %hold.5.rest_8_.rest_9_), calls=%async_computation | async-start | bytes 4194304 | tf_op jit(solution)/shard_map/all_to_all | solution.py:665
  53.1 0.0 collective-permute-done.2.rest_2_
  53.1 2.9 %collective-permute-done.5.rest_6_ = bf16[2,2,4,16,512]{4,3,2,1,0:T(8,128)(2,1)} collective-permute-done((bf16[2,2,4,16,512]{4,3,2,1,0:T(8,128)(2,1)}, bf16[2,2,4,16,512]{4,3,2,1,0:T(8,128)(2,1)}, u32[]{:S(2)}, u32[]{:S(2)}) %collective-permute-start.5) | collective-permute-done | bytes 262176 | tf_op jit(solution)/shard_map/ppermute | solution.py:626
  56.0 0.0 collective-permute-done.6.rest_7_
  56.0 5.4 %attend_old.2 = (bf16[4,2,4,8,16,512]{5,4,3,2,1,0:T(8,128)(2,1)}, bf16[512,512]{1,0:T(8,128)(2,1)S(1)}, bf16[512,512]{1,0:T(8,128)(2,1)S(1)}, bf16[512,512]{1,0:T(8,128)(2,1)S(1)}) custom-call(f32[16,1024]{1,0:T(8,128)S(1)} %get-tuple-element.39.rest_0_.refs_1_.state, bf16[1024,512]{1,0:T(8,128)(2,1)} %get-tuple-element.40.q_all, ...), custom_call_target="tpu_custom_call" | custom-call | flops 999999995904 | bytes 999999995904 | tf_op jit(solution)/shard_map/attend_old/pallas_call | solution.py:477
  61.5 0.1 collective-permute-start.7
  61.6 1.9 %collective-permute-done.7.second = bf16[512,512]{1,0:T(8,128)(2,1)S(1)} collective-permute-done((bf16[512,512]{1,0:T(8,128)(2,1)S(1)}, bf16[512,512]{1,0:T(8,128)(2,1)S(1)}, u32[]{:S(2)}, u32[]{:S(2)}) %collective-permute-start.7) | collective-permute-done | bytes 524320 | tf_op jit(solution)/shard_map/ppermute | solution.py:626
  63.4 0.1 add_terms.2.rest_10_
  63.6 1.6 %collective-permute-start.10 = (bf16[512,512]{1,0:T(8,128)(2,1)S(1)}, bf16[512,512]{1,0:T(8,128)(2,1)S(1)}, u32[]{:S(2)}, u32[]{:S(2)}) collective-permute-start(bf16[512,512]{1,0:T(8,128)(2,1)S(1)} %add_terms.2.rest_10_), channel_id=1, source_target_pairs={{0,2},{1,3},{2,0},{3,1},{4,6},{5,7},{6,4},{7,5},{8,10},{9,11},{10,... | collective-permute-start | bytes 1572872 | tf_op jit(solution)/shard_map/ppermute | solution.py:626
  65.1 5.4 %attend_old.3 = (bf16[4,2,4,8,16,512]{5,4,3,2,1,0:T(8,128)(2,1)}, bf16[512,512]{1,0:T(8,128)(2,1)S(1)}, bf16[512,512]{1,0:T(8,128)(2,1)S(1)}, bf16[512,512]{1,0:T(8,128)(2,1)S(1)}) custom-call(f32[16,1024]{1,0:T(8,128)S(1)} %get-tuple-element.39.rest_0_.refs_1_.state, bf16[1024,512]{1,0:T(8,128)(2,1)} %get-tuple-element.40.q_all, ...), custom_call_target="tpu_custom_call", output_to_operand_aliasing={{0}: (12, {})} | custom-call | flops 1 | bytes 1 | tf_op jit(solution)/shard_map/attend_old/pallas_call | solution.py:477
  70.6 0.1 collective-permute-start.9
  70.6 2.3 %own_terms.3 = (bf16[512,512]{1,0:T(8,128)(2,1)S(1)}, bf16[512,512]{1,0:T(8,128)(2,1)S(1)}) custom-call(bf16[512,512]{1,0:T(8,128)(2,1)S(1)} %get-tuple-element.56.attended, bf16[512,2048]{1,0:T(8,128)(2,1)} %w.9), custom_call_target="tpu_custom_call" | custom-call | flops 1 | bytes 1 | tf_op jit(solution)/shard_map/own_terms/pallas_call | solution.py:515
  73.0 0.6 collective-permute-start.12
  73.5 2.3 %own_terms.2 = (bf16[512,512]{1,0:T(8,128)(2,1)S(1)}, bf16[512,512]{1,0:T(8,128)(2,1)S(1)}) custom-call(bf16[512,512]{1,0:T(8,128)(2,1)S(1)} %get-tuple-element.51.attended, bf16[512,2048]{1,0:T(8,128)(2,1)} %w.9), custom_call_target="tpu_custom_call" | custom-call | flops 1 | bytes 1 | tf_op jit(solution)/shard_map/own_terms/pallas_call | solution.py:515
  75.9 0.1 collective-permute-start.8
  75.9 1.7 %collective-permute-done.10.rest_0_.third = bf16[512,512]{1,0:T(8,128)(2,1)S(1)} collective-permute-done((bf16[512,512]{1,0:T(8,128)(2,1)S(1)}, bf16[512,512]{1,0:T(8,128)(2,1)S(1)}, u32[]{:S(2)}, u32[]{:S(2)}) %collective-permute-start.10) | collective-permute-done | bytes 524320 | tf_op jit(solution)/shard_map/ppermute | solution.py:626
  77.6 0.0 collective-permute-done.9.second
  77.6 0.1 add_terms.3
  77.7 0.0 copy-start.5
  77.7 1.6 %collective-permute-start.11 = (bf16[512,512]{1,0:T(8,128)(2,1)S(1)}, bf16[512,512]{1,0:T(8,128)(2,1)S(1)}, u32[]{:S(2)}, u32[]{:S(2)}) collective-permute-start(bf16[512,512]{1,0:T(8,128)(2,1)S(1)} %add_terms.3), channel_id=1, source_target_pairs={{0,2},{1,3},{2,0},{3,1},{4,6},{5,7},{6,4},{7,5},{8,10},{9,11},{10,... | collective-permute-start | bytes 1572872 | tf_op jit(solution)/shard_map/ppermute | solution.py:626
  79.3 0.0 collective-permute-done.12.second
  79.3 0.3 total_terms.2
  79.6 11.4 %collective-permute-done.11.third = bf16[512,512]{1,0:T(8,128)(2,1)S(1)} collective-permute-done((bf16[512,512]{1,0:T(8,128)(2,1)S(1)}, bf16[512,512]{1,0:T(8,128)(2,1)S(1)}, u32[]{:S(2)}, u32[]{:S(2)}) %collective-permute-start.11) | collective-permute-done | bytes 524320 | tf_op jit(solution)/shard_map/ppermute | solution.py:626
  91.1 0.3 total_terms.3
  91.4 0.1 collective-permute-start.13
  91.4 1.6 %collective-permute-start.14 = (f32[8,512]{1,0:T(8,128)S(1)}, f32[8,512]{1,0:T(8,128)S(1)}, u32[]{:S(2)}, u32[]{:S(2)}) collective-permute-start(f32[8,512]{1,0:T(8,128)S(1)} %get-tuple-element.60.rest_0_), channel_id=1, source_target_pairs={{0,2},{1,3},{2,0},{3,1},{4,6},{5,7},{6,4},{7,5},{8,10},{9,11},{10,... | collective-permute-start | bytes 49160 | tf_op jit(solution)/shard_map/ppermute | solution.py:626
  93.0 0.3 collective-permute-start.15
  93.3 0.0 collective-permute-done.13.rest_1_
  93.3 1.9 %collective-permute-done.14.rest_2_ = f32[8,512]{1,0:T(8,128)S(1)} collective-permute-done((f32[8,512]{1,0:T(8,128)S(1)}, f32[8,512]{1,0:T(8,128)S(1)}, u32[]{:S(2)}, u32[]{:S(2)}) %collective-permute-start.14) | collective-permute-done | bytes 16416 | tf_op jit(solution)/shard_map/ppermute | solution.py:626
  95.2 0.9 collective-permute-done.15.rest_3_
  96.2 2.4 %finish_layer.1 = bf16[2,512,512]{2,1,0:T(8,128)(2,1)} custom-call(bf16[2,512,2048]{2,1,0:T(8,128)(2,1)} %residual.1, bf16[1,512]{1,0:T(2,128)(2,1)S(1)} %reshape.13.gain, f32[8,512]{1,0:T(8,128)S(1)} %get-tuple-element.60.rest_0_, f32[8,512]{1,0:T(8,128)S(1)} %collective-permute-done.13.rest_1_, f32[8,512]{1,0:T(8,128)S(1)} %collective-permute-done.14.rest_2_, ...), custom_call_target="tpu_custom_call" | custom-call | flops 1 | bytes 1 | tf_op jit(solution)/shard_map/finish_layer/pallas_call | solution.py:607
  98.6 3.4 %all-to-all-done.received = bf16[8,2,2,4,16,512]{5,4,3,2,1,0:T(8,128)(2,1)} async-done(((bf16[8,2,2,4,16,512]{5,4,3,2,1,0:T(8,128)(2,1)}), bf16[8,2,2,4,16,512]{5,4,3,2,1,0:T(8,128)(2,1)}, u32[]{:S(2)}, u32[]{:S(2)}) %all-to-all-start) | async-done | bytes 2097184 | tf_op jit(solution)/shard_map/all_to_all | solution.py:665
  102.0 2.4 %place_blocks.1 = bf16[4,2,4,8,16,512]{5,4,3,2,1,0:T(8,128)(2,1)} custom-call(bf16[4,2,4,8,16,512]{5,4,3,2,1,0:T(8,128)(2,1)} %get-tuple-element.63.filled, bf16[8,2,2,4,16,512]{5,4,3,2,1,0:T(8,128)(2,1)} %all-to-all-done.received), custom_call_target="tpu_custom_call", output_to_operand_aliasing={{}: (0, {})} | custom-call | flops 1 | bytes 1 | tf_op jit(solution)/shard_map/place_blocks/pallas_call | solution.py:132
  (18 shorter events, 0.0 us)
Async XLA Ops:
  3.6 23.8 %collective-permute-start.3 = (bf16[2,2,4,16,512]{4,3,2,1,0:T(8,128)(2,1)S(1)}, bf16[2,2,4,16,512]{4,3,2,1,0:T(8,128)(2,1)S(1)}, u32[]{:S(2)}, u32[]{:S(2)}) collective-permute-start(bf16[2,2,4,16,512]{4,3,2,1,0:T(8,128)(2,1)S(1)} %get-tuple-element.44), channel_id=1, source_target_pairs={{0,12},{4,8},{8,4},{12,0},{16,28},{20,24},{24,20},{28,16},{1,13},{... | collective-permute-start | bytes 786440 | tf_op jit(solution)/shard_map/ppermute | solution.py:626
  7.7 23.0 %collective-permute-start.4 = (bf16[2,2,4,16,512]{4,3,2,1,0:T(8,128)(2,1)S(1)}, bf16[2,2,4,16,512]{4,3,2,1,0:T(8,128)(2,1)S(1)}, u32[]{:S(2)}, u32[]{:S(2)}) collective-permute-start(bf16[2,2,4,16,512]{4,3,2,1,0:T(8,128)(2,1)S(1)} %get-tuple-element.45), channel_id=1, source_target_pairs={{0,8},{4,12},{8,0},{12,4},{16,24},{20,28},{24,16},{28,20},{1,9},{5... | collective-permute-start | bytes 786440 | tf_op jit(solution)/shard_map/ppermute | solution.py:626
  8.1 38.9 %collective-permute-start.1 = (bf16[2,2,4,16,512]{4,3,2,1,0:T(8,128)(2,1)S(1)}, bf16[2,2,4,16,512]{4,3,2,1,0:T(8,128)(2,1)S(1)}, u32[]{:S(2)}, u32[]{:S(2)}) collective-permute-start(bf16[2,2,4,16,512]{4,3,2,1,0:T(8,128)(2,1)S(1)} %get-tuple-element.42), channel_id=1, source_target_pairs={{0,24},{4,28},{8,16},{12,20},{16,8},{20,12},{24,0},{28,4},{1,25},{... | collective-permute-start | bytes 786440 | tf_op jit(solution)/shard_map/ppermute | solution.py:626
  11.7 41.4 %collective-permute-start = (bf16[2,2,4,16,512]{4,3,2,1,0:T(8,128)(2,1)}, bf16[2,2,4,16,512]{4,3,2,1,0:T(8,128)(2,1)S(1)}, u32[]{:S(2)}, u32[]{:S(2)}) collective-permute-start(bf16[2,2,4,16,512]{4,3,2,1,0:T(8,128)(2,1)} %get-tuple-element.33.rest_0_), channel_id=1, source_target_pairs={{0,28},{4,24},{8,20},{12,16},{16,12},{20,8},{24,4},{28,0},{1,29},{... | collective-permute-start | bytes 786440 | tf_op jit(solution)/shard_map/ppermute | solution.py:626
  11.7 3.7 %copy-start.2 = (f32[2,512,128]{2,1,0:T(8,128)S(1)}, f32[2,512,128]{2,1,0:T(8,128)}, u32[]{:S(2)}) copy-start(f32[2,512,128]{2,1,0:T(8,128)} %constant.5.clone.steps) | copy-start | bytes 1572868
  11.7 3.7 %copy-start.3 = (bf16[2,512]{1,0:T(2,128)(2,1)S(1)}, bf16[2,512]{1,0:T(2,128)(2,1)}, u32[]{:S(2)}) copy-start(bf16[2,512]{1,0:T(2,128)(2,1)} %gain.1) | copy-start | bytes 6148
  11.7 3.7 %copy-start.4 = (f32[1,128]{1,0:T(1,128)S(1)}, f32[1,128]{1,0:T(1,128)}, u32[]{:S(2)}) copy-start(f32[1,128]{1,0:T(1,128)} %constant.4.clone.frequency) | copy-start | bytes 1540
  11.8 41.4 %collective-permute-start.2 = (bf16[2,2,4,16,512]{4,3,2,1,0:T(8,128)(2,1)}, bf16[2,2,4,16,512]{4,3,2,1,0:T(8,128)(2,1)}, u32[]{:S(2)}, u32[]{:S(2)}) collective-permute-start(bf16[2,2,4,16,512]{4,3,2,1,0:T(8,128)(2,1)} %get-tuple-element.43), channel_id=1, source_target_pairs={{0,16},{4,20},{8,24},{12,28},{16,0},{20,4},{24,8},{28,12},{1,17},{... | collective-permute-start | bytes 786440 | tf_op jit(solution)/shard_map/ppermute | solution.py:626
  27.5 28.5 %collective-permute-start.5 = (bf16[2,2,4,16,512]{4,3,2,1,0:T(8,128)(2,1)}, bf16[2,2,4,16,512]{4,3,2,1,0:T(8,128)(2,1)}, u32[]{:S(2)}, u32[]{:S(2)}) collective-permute-start(bf16[2,2,4,16,512]{4,3,2,1,0:T(8,128)(2,1)} %hold.3), channel_id=1, source_target_pairs={{0,20},{4,16},{8,28},{12,24},{16,4},{20,0},{24,12},{28,8},{1,21},{... | collective-permute-start | bytes 786440 | tf_op jit(solution)/shard_map/ppermute | solution.py:626
  30.6 25.4 %collective-permute-start.6 = (bf16[2,2,4,16,512]{4,3,2,1,0:T(8,128)(2,1)}, bf16[2,2,4,16,512]{4,3,2,1,0:T(8,128)(2,1)}, u32[]{:S(2)}, u32[]{:S(2)}) collective-permute-start(bf16[2,2,4,16,512]{4,3,2,1,0:T(8,128)(2,1)} %hold.4), channel_id=1, source_target_pairs={{0,4},{4,0},{8,12},{12,8},{16,20},{20,16},{24,28},{28,24},{1,5},{5... | collective-permute-start | bytes 786440 | tf_op jit(solution)/shard_map/ppermute | solution.py:626
  47.0 9.0 %copy-start = (bf16[8,2,2,4,16,512]{5,4,3,2,1,0:T(8,128)(2,1)S(1)}, bf16[8,2,2,4,16,512]{5,4,3,2,1,0:T(8,128)(2,1)}, u32[]{:S(2)}) copy-start(bf16[8,2,2,4,16,512]{5,4,3,2,1,0:T(8,128)(2,1)} %hold.5.rest_8_.rest_9_) | copy-start | bytes 6291460
  47.0 9.0 %copy-start.1 = (bf16[2,2,4,16,512]{4,3,2,1,0:T(8,128)(2,1)S(1)}, bf16[2,2,4,16,512]{4,3,2,1,0:T(8,128)(2,1)}, u32[]{:S(2)}) copy-start(bf16[2,2,4,16,512]{4,3,2,1,0:T(8,128)(2,1)} %get-tuple-element.34.rest_0_.rest_5_) | copy-start | bytes 786436
  47.1 54.9 %all-to-all-start = ((bf16[8,2,2,4,16,512]{5,4,3,2,1,0:T(8,128)(2,1)}), bf16[8,2,2,4,16,512]{5,4,3,2,1,0:T(8,128)(2,1)}, u32[]{:S(2)}, u32[]{:S(2)}) async-start(bf16[8,2,2,4,16,512]{5,4,3,2,1,0:T(8,128)(2,1)} %hold.5.rest_8_.rest_9_), calls=%async_computation | async-start | bytes 4194304 | tf_op jit(solution)/shard_map/all_to_all | solution.py:665
  61.5 2.0 %collective-permute-start.7 = (bf16[512,512]{1,0:T(8,128)(2,1)S(1)}, bf16[512,512]{1,0:T(8,128)(2,1)S(1)}, u32[]{:S(2)}, u32[]{:S(2)}) collective-permute-start(bf16[512,512]{1,0:T(8,128)(2,1)S(1)} %get-tuple-element.50), channel_id=1, source_target_pairs={{0,1},{1,0},{2,3},{3,2},{4,5},{5,4},{6,7},{7,6},{8,9},{9,8},{10,11... | collective-permute-start | bytes 1572872 | tf_op jit(solution)/shard_map/ppermute | solution.py:626
  63.6 14.0 %collective-permute-start.10 = (bf16[512,512]{1,0:T(8,128)(2,1)S(1)}, bf16[512,512]{1,0:T(8,128)(2,1)S(1)}, u32[]{:S(2)}, u32[]{:S(2)}) collective-permute-start(bf16[512,512]{1,0:T(8,128)(2,1)S(1)} %add_terms.2.rest_10_), channel_id=1, source_target_pairs={{0,2},{1,3},{2,0},{3,1},{4,6},{5,7},{6,4},{7,5},{8,10},{9,11},{10,... | collective-permute-start | bytes 1572872 | tf_op jit(solution)/shard_map/ppermute | solution.py:626
  70.6 7.0 %collective-permute-start.9 = (bf16[512,512]{1,0:T(8,128)(2,1)S(1)}, bf16[512,512]{1,0:T(8,128)(2,1)S(1)}, u32[]{:S(2)}, u32[]{:S(2)}) collective-permute-start(bf16[512,512]{1,0:T(8,128)(2,1)S(1)} %get-tuple-element.55), channel_id=1, source_target_pairs={{0,1},{1,0},{2,3},{3,2},{4,5},{5,4},{6,7},{7,6},{8,9},{9,8},{10,11... | collective-permute-start | bytes 1572872 | tf_op jit(solution)/shard_map/ppermute | solution.py:626
  73.0 6.3 %collective-permute-start.12 = (bf16[512,512]{1,0:T(8,128)(2,1)S(1)}, bf16[512,512]{1,0:T(8,128)(2,1)S(1)}, u32[]{:S(2)}, u32[]{:S(2)}) collective-permute-start(bf16[512,512]{1,0:T(8,128)(2,1)S(1)} %get-tuple-element.58), channel_id=1, source_target_pairs={{0,1},{1,0},{2,3},{3,2},{4,5},{5,4},{6,7},{7,6},{8,9},{9,8},{10,11... | collective-permute-start | bytes 1572872 | tf_op jit(solution)/shard_map/ppermute | solution.py:626
  75.9 3.8 %collective-permute-start.8 = (bf16[512,512]{1,0:T(8,128)(2,1)S(1)}, bf16[512,512]{1,0:T(8,128)(2,1)S(1)}, u32[]{:S(2)}, u32[]{:S(2)}) collective-permute-start(bf16[512,512]{1,0:T(8,128)(2,1)S(1)} %get-tuple-element.53), channel_id=1, source_target_pairs={{0,1},{1,0},{2,3},{3,2},{4,5},{5,4},{6,7},{7,6},{8,9},{9,8},{10,11... | collective-permute-start | bytes 1572872 | tf_op jit(solution)/shard_map/ppermute | solution.py:626
  77.7 15.6 %copy-start.5 = (bf16[512]{0:T(512)(128)(2,1)S(1)}, bf16[512]{0:T(512)(128)(2,1)}, u32[]{:S(2)}) copy-start(bf16[512]{0:T(512)(128)(2,1)} %param.15) | copy-start | bytes 3076
  77.7 13.3 %collective-permute-start.11 = (bf16[512,512]{1,0:T(8,128)(2,1)S(1)}, bf16[512,512]{1,0:T(8,128)(2,1)S(1)}, u32[]{:S(2)}, u32[]{:S(2)}) collective-permute-start(bf16[512,512]{1,0:T(8,128)(2,1)S(1)} %add_terms.3), channel_id=1, source_target_pairs={{0,2},{1,3},{2,0},{3,1},{4,6},{5,7},{6,4},{7,5},{8,10},{9,11},{10,... | collective-permute-start | bytes 1572872 | tf_op jit(solution)/shard_map/ppermute | solution.py:626
  91.4 2.0 %collective-permute-start.13 = (f32[8,512]{1,0:T(8,128)S(1)}, f32[8,512]{1,0:T(8,128)S(1)}, u32[]{:S(2)}, u32[]{:S(2)}) collective-permute-start(f32[8,512]{1,0:T(8,128)S(1)} %get-tuple-element.60.rest_0_), channel_id=1, source_target_pairs={{0,1},{1,0},{2,3},{3,2},{4,5},{5,4},{6,7},{7,6},{8,9},{9,8},{10,11... | collective-permute-start | bytes 49160 | tf_op jit(solution)/shard_map/ppermute | solution.py:626
  91.4 3.8 %collective-permute-start.14 = (f32[8,512]{1,0:T(8,128)S(1)}, f32[8,512]{1,0:T(8,128)S(1)}, u32[]{:S(2)}, u32[]{:S(2)}) collective-permute-start(f32[8,512]{1,0:T(8,128)S(1)} %get-tuple-element.60.rest_0_), channel_id=1, source_target_pairs={{0,2},{1,3},{2,0},{3,1},{4,6},{5,7},{6,4},{7,5},{8,10},{9,11},{10,... | collective-permute-start | bytes 49160 | tf_op jit(solution)/shard_map/ppermute | solution.py:626
  93.0 3.2 %collective-permute-start.15 = (f32[8,512]{1,0:T(8,128)S(1)}, f32[8,512]{1,0:T(8,128)S(1)}, u32[]{:S(2)}, u32[]{:S(2)}) collective-permute-start(f32[8,512]{1,0:T(8,128)S(1)} %get-tuple-element.60.rest_0_), channel_id=1, source_target_pairs={{0,3},{1,2},{2,1},{3,0},{4,7},{5,6},{6,5},{7,4},{8,11},{9,10},{10,... | collective-permute-start | bytes 49160 | tf_op jit(solution)/shard_map/ppermute | solution.py:626

commit v7 on v6

--- a/solution.py
+++ b/solution.py
@@ -399,8 +399,8 @@
 
 def attend_old_body(which, span, offsets, q_block, filled, after, state, q_all, mixed_all, w, *rest):
     received, rest = rest[: len(offsets)], rest[len(offsets) + int(filled) + after :]
-    relaid, attended, keep, send = rest[:4]
-    held, q, mixed, w_held, loaded, q_loaded, w_loaded, stored = rest[4:]
+    relaid, attended, keep, *send = rest[:5]
+    held, q, mixed, w_held, loaded, q_loaded, w_loaded, stored = rest[5:]
     me = lax.axis_index("req")
     q_load = pltpu.make_async_copy(q_all.at[pl.ds(which * span, span)], q, q_loaded.at[0])
     mixed_load = pltpu.make_async_copy(mixed_all.at[which], mixed, q_loaded.at[1])
@@ -453,7 +453,10 @@
             sums += jnp.dot(values, scores.astype(jnp.bfloat16), preferred_element_type=jnp.float32)
             attended[low : low + q_block, columns] = jnp.transpose((sums / total)).astype(attended.dtype)
     w_load.wait()
-    group_terms(attended, w_held, ((send, 3), (keep, 2)))
+    rows = send[0].shape[0]
+    for at, out in enumerate(send):
+        group_terms(attended.at[pl.ds(at * rows, rows)], w_held, ((out, 3),))
+    group_terms(attended, w_held, ((keep, 2),))
     for store in stores:
         store.wait()
 
@@ -479,12 +482,13 @@
             attend_old_body, which, span, offsets, q_block, filled is not None, len(after)
         ),
         in_specs=[VMEM] + [ANY] * (3 + len(received) + len(start) + len(after)),
-        out_specs=[ANY] + [VMEM] * 3,
+        out_specs=[ANY] + [VMEM] * 4,
         out_shape=[
             pltpu.HBM(shape, received[0].dtype),
             pltpu.VMEM((span, width), jnp.bfloat16),
             pltpu.VMEM((span, part), jnp.bfloat16),
-            pltpu.VMEM((span, part), jnp.bfloat16),
+            pltpu.VMEM((span // 2, part), jnp.bfloat16),
+            pltpu.VMEM((span // 2, part), jnp.bfloat16),
         ],
         scratch_shapes=[
             pltpu.VMEM((2,) + shape[2:], received[0].dtype),
@@ -524,21 +528,26 @@
     )(*in_vmem(attended), *in_hbm(w))
 
 
-def add_body(first, second, *rest):
+def add_body(first, upper, lower, *rest):
     out = rest[-1]
-    out[...] = (first[...].astype(jnp.float32) + second[...].astype(jnp.float32)).astype(out.dtype)
-
-
-def add(first, second, after=()):
+    rows = upper.shape[0]
+    for at, second in enumerate((upper, lower)):
+        here = slice(at * rows, (at + 1) * rows)
+        out[here] = (first[here].astype(jnp.float32) + second[...].astype(jnp.float32)).astype(
+            out.dtype
+        )
+
+
+def add(first, upper, lower, after=()):
     return pl.pallas_call(
         add_body,
-        in_specs=[VMEM, VMEM] + [ANY] * len(after),
+        in_specs=[VMEM] * 3 + [ANY] * len(after),
         out_specs=VMEM,
         out_shape=pltpu.VMEM(first.shape, first.dtype),
         cost_estimate=cost(1, 1),
         compiler_params=params(4),
         name="add_terms",
-    )(*in_vmem(first, second), *after)
+    )(*in_vmem(first, upper, lower), *after)
 
 
 def total_body(which, first, second, third, *rest):
@@ -574,51 +583,73 @@
     )(*in_vmem(first, second, third), *squares)
 
 
-def finish_body(full_width, count, residual, gain, *rest):
-    squares, totals = rest[:count], rest[count:-5]
-    out, res_held, out_held, loaded, stored = rest[-5:]
-    per_device, span, width = out.shape
+def own_columns_body(residual, after, out, loaded):
+    del after
+    per_device, _, width = out.shape
     start = pl.multiple_of(lax.axis_index("tensor") * width, width)
     loads = [
-        pltpu.make_async_copy(residual.at[p, :, pl.ds(start, width)], res_held.at[p], loaded.at[p])
+        pltpu.make_async_copy(residual.at[p, :, pl.ds(start, width)], out.at[p], loaded.at[p])
         for p in range(per_device)
     ]
     for load in loads:
         load.start()
+    for load in loads:
+        load.wait()
+
+
+def own_columns(residual, width, after):
+    per_device, span, _ = residual.shape
+    return pl.pallas_call(
+        own_columns_body,
+        in_specs=[ANY, ANY],
+        out_specs=VMEM,
+        out_shape=pltpu.VMEM((per_device, span, width), residual.dtype),
+        scratch_shapes=[pltpu.SemaphoreType.DMA((per_device,))],
+        cost_estimate=cost(1, 1),
+        compiler_params=params(2),
+        name="own_columns",
+    )(*in_hbm(residual), after)
+
+
+def finish_body(full_width, count, residual, gain, *rest):
+    squares, totals = rest[:count], rest[count:-3]
+    out, out_held, stored = rest[-3:]
+    per_device, span, width = out.shape
     total = squares[0][...]
     for part in squares[1:]:
         total += part[...]
     scales = as_columns(lax.rsqrt(total / full_width + norm_eps))
+    half = span // 2
     stores = []
     for p in range(per_device):
-        normed = totals[p][...] * scales[:, p : p + 1] * gain[...].astype(jnp.float32)
-        loads[p].wait()
-        out_held[p] = (res_held[p].astype(jnp.float32) + normed).astype(out.dtype)
-        stores.append(pltpu.make_async_copy(out_held.at[p], out.at[p], stored.at[p]))
-        stores[-1].start()
+        for at in range(2):
+            here = slice(at * half, (at + 1) * half)
+            normed = totals[p][here] * scales[here, p : p + 1] * gain[...].astype(jnp.float32)
+            out_held[p, here] = (residual[p, here].astype(jnp.float32) + normed).astype(out.dtype)
+            rows = pl.ds(at * half, half)
+            stores.append(
+                pltpu.make_async_copy(out_held.at[p, rows], out.at[p, rows], stored.at[p, at])
+            )
+            stores[-1].start()
     for store in stores:
         store.wait()
 
 
-def finish(residual, totals, squares, gain):
-    per_device, span, full_width = residual.shape
-    width = totals[0].shape[1]
-    shape = (per_device, span, width)
+def finish(full_width, residual, totals, squares, gain):
+    per_device, span, width = residual.shape
     return pl.pallas_call(
         functools.partial(finish_body, full_width, len(squares)),
-        in_specs=[ANY] + [VMEM] * (1 + len(squares) + per_device),
+        in_specs=[VMEM] * (2 + len(squares) + per_device),
         out_specs=ANY,
-        out_shape=pltpu.HBM(shape, residual.dtype),
+        out_shape=pltpu.HBM(residual.shape, residual.dtype),
         scratch_shapes=[
-            pltpu.VMEM(shape, residual.dtype),
-            pltpu.VMEM(shape, residual.dtype),
-            pltpu.SemaphoreType.DMA((per_device,)),
-            pltpu.SemaphoreType.DMA((per_device,)),
+            pltpu.VMEM(residual.shape, residual.dtype),
+            pltpu.SemaphoreType.DMA((per_device, 2)),
         ],
         cost_estimate=cost(1, 1),
-        compiler_params=params(12),
+        compiler_params=params(8),
         name="finish_layer",
-    )(*in_hbm(residual), gain.reshape(1, width), *squares, *in_vmem(*totals))
+    )(*in_vmem(residual), gain.reshape(1, width), *squares, *in_vmem(*totals))
 
 
 def permuted(value, axis, offset):
@@ -666,7 +697,7 @@
 
     relaid, across, added, totals, row_squares = None, (), (), [], ()
     for p in range(per_device):
-        relaid, attended, keep_far, send_far = attend_old(
+        relaid, attended, keep_far, *send_far = attend_old(
             p,
             span_len,
             queries,
@@ -681,17 +712,20 @@
             after=(sent_rest, *added),
             weight=1 if p else 10**12,
         )
-        added = [add(keep_far, permuted(send_far, "tensor", 1), after=across)]
+        halves = [permuted(rows, "tensor", 1) for rows in send_far]
+        added = [add(keep_far, *halves, after=across)]
         across = [permuted(added[0], "tensor", 2)]
         keep, send = own_terms(attended, w_out, part_width)
         total, *row_squares = total_of(
             p, keep, permuted(send, "tensor", 1), across[0], row_squares
         )
         totals.append(total)
+        if p == 0:
+            residual = own_columns(span_in, part_width, row_squares[0])
     row_squares = row_squares + [
         permuted(row_squares[0], "tensor", at) for at in range(1, tensor_count)
     ]
-    layer_out = finish(span_in, totals, row_squares, post_gain)
+    layer_out = finish(full_width, residual, totals, row_squares, post_gain)
 
     relaid = place(shape, 2, rest, received_rest, relaid)
     return layer_out, relaid.reshape(planes, per_device, -1, part_width)

time: 106 us -> 105 us (level)
  waiting for transfers between devices: 24.1 us -> 22.2 us
    ppermute x16 -> x18, waiting for transfers between devices: 20.7 us -> 18.5 us  [permuted(): return lax.ppermute(value, axis, [(i, i ^ offset) for i in range(size)])]
    pallas_call x2 -> x3, Pallas kernels: 0.24 us -> 1.46 us  [the longest x1 1.22 us: own_columns(): pl.pallas_call(own_columns_body, in_specs=[ANY, ANY], out_specs=VMEM, out...]
    pallas_call x1, Pallas kernels: 2.39 us -> 1.27 us  [finish(): pl.pallas_call(functools.partial(finish_body, full_width, len(squares)),...]
    ppermute x16 -> x18, starting transfers between devices: 18.4 us -> 19.5 us  [permuted(): return lax.ppermute(value, axis, [(i, i ^ offset) for i in range(size)])]
  transfers between devices with their start and end apart: 17 -> 19, of which waited for: 7 -> 8; matrix products, arithmetic and copies ran while one was open for 0% -> 0% of each run, Pallas kernels for 42% -> 43%
where the time goes in v7:
time: 105 us
  Pallas kernels  50.3 us (48%)
  starting transfers between devices  25.5 us (24%)
  waiting for transfers between devices  22.2 us (21%)
  blocking collectives  5.41 us (5%)
    ppermute x18, starting transfers between devices, permuted(): return lax.ppermute(value, axis, [(i, i ^ offset) for i in range(size)])  19.5 us
    ppermute x18, waiting for transfers between devices, permuted(): return lax.ppermute(value, axis, [(i, i ^ offset) for i in range(size)])  18.5 us
    pallas_call x1, Pallas kernels, project(): pl.pallas_call(functools.partial(project_body, per_device, block, len(aft...  12 us
    pallas_call x2, Pallas kernels, attend_old(): pl.pallas_call(functools.partial(attend_old_body, which, span, offsets, q...  11.7 us
    pallas_call x3, Pallas kernels, gather(): pl.pallas_call(functools.partial(gather_body, wanted, staged, count, per_...  9.44 us
    pallas_call x1, Pallas kernels, attend_new(): pl.pallas_call(functools.partial(attend_new_body, full_width, span, q_blo...  6.75 us
    all_to_all x1, starting transfers between devices, on_device(): received_rest = lax.all_to_all(sent_rest, 'req', 0, 0)  6.07 us
    all_gather x1, blocking collectives, on_device(): squares = lax.all_gather(squares, 'tensor')  5.41 us
  transfers between devices with their start and end apart: 19, of which 8 were waited for; matrix products, arithmetic and copies ran while one was open for 0% of the time, Pallas kernels for 43%

profile of v7, /device:TPU:0, one launch (start us, length us, event | category | flops | bytes accessed | tf_op | source)
XLA Modules:
  0.0 104.6 jit_solution(8720160107561381583)
XLA Ops:
  0.6 3.0 %gather_blocks.3 = (bf16[2,2,4,16,512]{4,3,2,1,0:T(8,128)(2,1)}, bf16[2,2,4,16,512]{4,3,2,1,0:T(8,128)(2,1)S(1)}, bf16[2,2,4,16,512]{4,3,2,1,0:T(8,128)(2,1)}, b...) custom-call(s32[16,32]{1,0:T(8,128)} %table_all.5, s32[16]{0:T(128)} %order_all.5, ...), custom_call_target="tpu_custom_call" | custom-call | flops 1 | bytes 1 | tf_op jit(solution)/shard_map/gather_blocks/pallas_call | solution.py:97
  3.6 4.0 %collective-permute-start.3 = (bf16[2,2,4,16,512]{4,3,2,1,0:T(8,128)(2,1)S(1)}, bf16[2,2,4,16,512]{4,3,2,1,0:T(8,128)(2,1)S(1)}, u32[]{:S(2)}, u32[]{:S(2)}) collective-permute-start(bf16[2,2,4,16,512]{4,3,2,1,0:T(8,128)(2,1)S(1)} %get-tuple-element.46), channel_id=1, source_target_pairs={{0,12},{4,8},{8,4},{12,0},{16,28},{20,24},{24,20},{28,16},{1,13},{... | collective-permute-start | bytes 786440 | tf_op jit(solution)/shard_map/ppermute | solution.py:657
  7.7 0.4 collective-permute-start.4
  8.1 3.6 %collective-permute-start.1 = (bf16[2,2,4,16,512]{4,3,2,1,0:T(8,128)(2,1)S(1)}, bf16[2,2,4,16,512]{4,3,2,1,0:T(8,128)(2,1)S(1)}, u32[]{:S(2)}, u32[]{:S(2)}) collective-permute-start(bf16[2,2,4,16,512]{4,3,2,1,0:T(8,128)(2,1)S(1)} %get-tuple-element.44), channel_id=1, source_target_pairs={{0,24},{4,28},{8,16},{12,20},{16,8},{20,12},{24,0},{28,4},{1,25},{... | collective-permute-start | bytes 786440 | tf_op jit(solution)/shard_map/ppermute | solution.py:657
  11.7 0.0 collective-permute-start
  11.8 0.9 collective-permute-start.2
  12.7 2.7 %gather_blocks.4 = (bf16[2,2,4,16,512]{4,3,2,1,0:T(8,128)(2,1)}, bf16[2,2,4,16,512]{4,3,2,1,0:T(8,128)(2,1)}, bf16[2,2,4,16,512]{4,3,2,1,0:T(8,128)(2,1)}) custom-call(s32[16,32]{1,0:T(8,128)} %table_all.5, s32[16]{0:T(128)} %order_all.5, bf16[4,64,16,512]{3,2,1,0:T(8,128)(2,1)} %pool.5, bf16[2,2,4,16,512]{4,3,2,1,0:T(8,128)(2,1)} %get-tuple-element.35.rest_0_), custom_call_target="tpu_custom_call" | custom-call | flops 1 | bytes 1 | tf_op jit(solution)/shard_map/gather_blocks/pallas_call | solution.py:97
  15.4 12.0 %project_qkv.1 = (f32[1024,512]{1,0:T(8,128)}, f32[1024,512]{1,0:T(8,128)}, bf16[1024,512]{1,0:T(8,128)(2,1)}, f32[8,1024]{1,0:T(8,128)S(1)}) custom-call(s32[16]{0:T(128)} %order_all.5, s32[16]{0:T(128)} %lengths.1, f32[1,128]{1,0:T(1,128)S(1)} %copy-done.4, f32[2,512,128]{2,1,0:T(8,128)S(1)} %copy-done.2, bf16[2,512]{1,0:T(2,128)(2,1)S(1)} %copy-done.3, ...), custom_call_target="tpu_custom_call" | custom-call | flops 1 | bytes 1 | tf_op jit(solution)/shard_map/project_qkv/pallas_call | solution.py:262
  27.5 3.2 %collective-permute-start.5 = (bf16[2,2,4,16,512]{4,3,2,1,0:T(8,128)(2,1)}, bf16[2,2,4,16,512]{4,3,2,1,0:T(8,128)(2,1)}, u32[]{:S(2)}, u32[]{:S(2)}) collective-permute-start(bf16[2,2,4,16,512]{4,3,2,1,0:T(8,128)(2,1)} %hold.3), channel_id=1, source_target_pairs={{0,20},{4,16},{8,28},{12,24},{16,4},{20,0},{24,12},{28,8},{1,21},{... | collective-permute-start | bytes 786440 | tf_op jit(solution)/shard_map/ppermute | solution.py:657
  30.6 0.0 collective-permute-done.4.refs_2_.rest_4_
  30.6 0.4 collective-permute-start.6
  31.1 5.4 %all-gather = f32[32,1024]{1,0:T(8,128)S(1)} all-gather(f32[8,1024]{1,0:T(8,128)S(1)} %get-tuple-element.37.refs_1_), channel_id=2, replica_groups=mesh['req'=8,'tensor'=4] {'tensor'}, dimensions={0}, use_global_device_ids=true | all-gather | bytes 163840 | tf_op jit(solution)/shard_map/all_gather | solution.py:686
  36.5 6.8 %attend_new.1 = (bf16[1024,512]{1,0:T(8,128)(2,1)}, f32[2,512,512]{2,1,0:T(8,128)}, f32[16,1024]{1,0:T(8,128)S(1)}) custom-call(f32[4,8,1024]{2,1,0:T(8,128)S(1)} %bitcast.3, f32[1024,512]{1,0:T(8,128)} %get-tuple-element.38.rest_0_, f32[1024,512]{1,0:T(8,128)} %get-tuple-element.39.rest_1_, bf16[1024,512]{1,0:T(8,128)(2,1)} %get-tuple-element.40.rest_2_), custom_call_target="tpu_custom_call" | custom-call | flops 1 | bytes 1 | tf_op jit(solution)/shard_map/attend_new/pallas_call | solution.py:376
  43.2 3.8 %gather_blocks.5.refs_0_ = bf16[8,2,2,4,16,512]{5,4,3,2,1,0:T(8,128)(2,1)} custom-call(s32[16,32]{1,0:T(8,128)} %table_all.5, s32[16]{0:T(128)} %order_all.5, bf16[4,64,16,512]{3,2,1,0:T(8,128)(2,1)} %pool.5, f32[16,1024]{1,0:T(8,128)S(1)} %get-tuple-element.41.rest_0_.refs_1_.state), custom_call_target="tpu_custom_call" | custom-call | flops 1 | bytes 1 | tf_op jit(solution)/shard_map/gather_blocks/pallas_call | solution.py:97
  47.0 0.0 collective-permute-done.1.refs_4_.rest_1_
  47.0 6.1 %all-to-all-start = ((bf16[8,2,2,4,16,512]{5,4,3,2,1,0:T(8,128)(2,1)}), bf16[8,2,2,4,16,512]{5,4,3,2,1,0:T(8,128)(2,1)}, u32[]{:S(2)}, u32[]{:S(2)}) async-start(bf16[8,2,2,4,16,512]{5,4,3,2,1,0:T(8,128)(2,1)} %hold.5.rest_8_.rest_9_), calls=%async_computation | async-start | bytes 4194304 | tf_op jit(solution)/shard_map/all_to_all | solution.py:696
  53.1 0.0 collective-permute-done.2.rest_2_
  53.1 2.9 %collective-permute-done.5.rest_6_ = bf16[2,2,4,16,512]{4,3,2,1,0:T(8,128)(2,1)} collective-permute-done((bf16[2,2,4,16,512]{4,3,2,1,0:T(8,128)(2,1)}, bf16[2,2,4,16,512]{4,3,2,1,0:T(8,128)(2,1)}, u32[]{:S(2)}, u32[]{:S(2)}) %collective-permute-start.5) | collective-permute-done | bytes 262176 | tf_op jit(solution)/shard_map/ppermute | solution.py:657
  56.0 6.3 %attend_old.2 = (bf16[4,2,4,8,16,512]{5,4,3,2,1,0:T(8,128)(2,1)}, bf16[512,512]{1,0:T(8,128)(2,1)S(1)}, bf16[512,512]{1,0:T(8,128)(2,1)S(1)}, bf16[256,512]{1,0:T(8,128)(2,1)S(1)}, bf16[256,512]{1,0:T(8,128)(2,1)S(1)}) custom-call(f32[16,1024]{1,0:T(8,128)S(1)} %get-tuple-element.41.rest_0_.refs_1_.state, bf16[1024,512]{1,0:T(8,128)(2,1)} %get-tuple-element.42.q_all, ...), custom_call_target="tpu_custom_call" | custom-call | flops 999999995904 | bytes 999999995904 | tf_op jit(solution)/shard_map/attend_old/pallas_call | solution.py:480
  62.3 0.1 collective-permute-start.8
  62.4 0.5 collective-permute-start.9
  62.9 1.0 collective-permute-done.8.upper
  63.9 0.4 collective-permute-done.9.lower
  64.3 0.1 add_terms.2.rest_10_
  64.4 1.6 %collective-permute-start.10 = (bf16[512,512]{1,0:T(8,128)(2,1)S(1)}, bf16[512,512]{1,0:T(8,128)(2,1)S(1)}, u32[]{:S(2)}, u32[]{:S(2)}) collective-permute-start(bf16[512,512]{1,0:T(8,128)(2,1)S(1)} %add_terms.2.rest_10_), channel_id=1, source_target_pairs={{0,2},{1,3},{2,0},{3,1},{4,6},{5,7},{6,4},{7,5},{8,10},{9,11},{10,... | collective-permute-start | bytes 1572872 | tf_op jit(solution)/shard_map/ppermute | solution.py:657
  65.9 5.4 %attend_old.3 = (bf16[4,2,4,8,16,512]{5,4,3,2,1,0:T(8,128)(2,1)}, bf16[512,512]{1,0:T(8,128)(2,1)S(1)}, bf16[512,512]{1,0:T(8,128)(2,1)S(1)}, bf16[256,512]{1,0:T(8,128)(2,1)S(1)}, bf16[256,512]{1,0:T(8,128)(2,1)S(1)}) custom-call(f32[16,1024]{1,0:T(8,128)S(1)} %get-tuple-element.41.rest_0_.refs_1_.state, ...), custom_call_target="tpu_custom_call", output_to_operand_aliasing={{0}: (12, {})} | custom-call | flops 1 | bytes 1 | tf_op jit(solution)/shard_map/attend_old/pallas_call | solution.py:480
  71.4 0.1 collective-permute-start.12
  71.5 0.5 collective-permute-start.13
  72.0 2.3 %own_terms.2 = (bf16[512,512]{1,0:T(8,128)(2,1)S(1)}, bf16[512,512]{1,0:T(8,128)(2,1)S(1)}) custom-call(bf16[512,512]{1,0:T(8,128)(2,1)S(1)} %get-tuple-element.50.attended, bf16[512,2048]{1,0:T(8,128)(2,1)} %w.9), custom_call_target="tpu_custom_call" | custom-call | flops 1 | bytes 1 | tf_op jit(solution)/shard_map/own_terms/pallas_call | solution.py:519
  74.3 0.1 collective-permute-start.7
  74.4 2.3 %own_terms.3 = (bf16[512,512]{1,0:T(8,128)(2,1)S(1)}, bf16[512,512]{1,0:T(8,128)(2,1)S(1)}) custom-call(bf16[512,512]{1,0:T(8,128)(2,1)S(1)} %get-tuple-element.58.attended, bf16[512,2048]{1,0:T(8,128)(2,1)} %w.9), custom_call_target="tpu_custom_call" | custom-call | flops 1 | bytes 1 | tf_op jit(solution)/shard_map/own_terms/pallas_call | solution.py:519
  76.7 0.5 collective-permute-start.11
  77.2 1.2 %collective-permute-done.10.third.rest_0_ = bf16[512,512]{1,0:T(8,128)(2,1)S(1)} collective-permute-done((bf16[512,512]{1,0:T(8,128)(2,1)S(1)}, bf16[512,512]{1,0:T(8,128)(2,1)S(1)}, u32[]{:S(2)}, u32[]{:S(2)}) %collective-permute-start.10) | collective-permute-done | bytes 524320 | tf_op jit(solution)/shard_map/ppermute | solution.py:657
  78.4 0.1 add_terms.3
  78.5 0.0 copy-start.5
  78.6 1.6 %collective-permute-start.14 = (bf16[512,512]{1,0:T(8,128)(2,1)S(1)}, bf16[512,512]{1,0:T(8,128)(2,1)S(1)}, u32[]{:S(2)}, u32[]{:S(2)}) collective-permute-start(bf16[512,512]{1,0:T(8,128)(2,1)S(1)} %add_terms.3), channel_id=1, source_target_pairs={{0,2},{1,3},{2,0},{3,1},{4,6},{5,7},{6,4},{7,5},{8,10},{9,11},{10,... | collective-permute-start | bytes 1572872 | tf_op jit(solution)/shard_map/ppermute | solution.py:657
  80.1 0.3 total_terms.2
  80.4 11.4 %collective-permute-done.14.third = bf16[512,512]{1,0:T(8,128)(2,1)S(1)} collective-permute-done((bf16[512,512]{1,0:T(8,128)(2,1)S(1)}, bf16[512,512]{1,0:T(8,128)(2,1)S(1)}, u32[]{:S(2)}, u32[]{:S(2)}) %collective-permute-start.14) | collective-permute-done | bytes 524320 | tf_op jit(solution)/shard_map/ppermute | solution.py:657
  91.9 0.3 total_terms.3
  92.2 0.1 collective-permute-start.15
  92.3 1.6 %collective-permute-start.16 = (f32[8,512]{1,0:T(8,128)S(1)}, f32[8,512]{1,0:T(8,128)S(1)}, u32[]{:S(2)}, u32[]{:S(2)}) collective-permute-start(f32[8,512]{1,0:T(8,128)S(1)} %get-tuple-element.64.rest_0_), channel_id=1, source_target_pairs={{0,2},{1,3},{2,0},{3,1},{4,6},{5,7},{6,4},{7,5},{8,10},{9,11},{10,... | collective-permute-start | bytes 49160 | tf_op jit(solution)/shard_map/ppermute | solution.py:657
  93.8 0.3 collective-permute-start.17
  94.1 1.2 %own_columns.1.residual = bf16[2,512,512]{2,1,0:T(8,128)(2,1)S(1)} custom-call(bf16[2,512,2048]{2,1,0:T(8,128)(2,1)} %residual.1, f32[8,512]{1,0:T(8,128)S(1)} %get-tuple-element.56.after.rest_0_), custom_call_target="tpu_custom_call" | custom-call | flops 1 | bytes 1 | tf_op jit(solution)/shard_map/own_columns/pallas_call | solution.py:602
  95.4 0.7 collective-permute-done.16.rest_2_
  96.1 0.9 collective-permute-done.17.rest_3_
  97.0 1.3 %finish_layer.1 = bf16[2,512,512]{2,1,0:T(8,128)(2,1)} custom-call(bf16[2,512,512]{2,1,0:T(8,128)(2,1)S(1)} %own_columns.1.residual, bf16[1,512]{1,0:T(2,128)(2,1)S(1)} %reshape.14.gain, f32[8,512]{1,0:T(8,128)S(1)} %get-tuple-element.64.rest_0_, f32[8,512]{1,0:T(8,128)S(1)} %collective-permute-done.15.rest_1_, ...), custom_call_target="tpu_custom_call" | custom-call | flops 1 | bytes 1 | tf_op jit(solution)/shard_map/finish_layer/pallas_call | solution.py:640
  98.3 3.7 %all-to-all-done.received = bf16[8,2,2,4,16,512]{5,4,3,2,1,0:T(8,128)(2,1)} async-done(((bf16[8,2,2,4,16,512]{5,4,3,2,1,0:T(8,128)(2,1)}), bf16[8,2,2,4,16,512]{5,4,3,2,1,0:T(8,128)(2,1)}, u32[]{:S(2)}, u32[]{:S(2)}) %all-to-all-start) | async-done | bytes 2097184 | tf_op jit(solution)/shard_map/all_to_all | solution.py:696
  102.0 2.4 %place_blocks.1 = bf16[4,2,4,8,16,512]{5,4,3,2,1,0:T(8,128)(2,1)} custom-call(bf16[4,2,4,8,16,512]{5,4,3,2,1,0:T(8,128)(2,1)} %get-tuple-element.67.filled, bf16[8,2,2,4,16,512]{5,4,3,2,1,0:T(8,128)(2,1)} %all-to-all-done.received), custom_call_target="tpu_custom_call", output_to_operand_aliasing={{}: (0, {})} | custom-call | flops 1 | bytes 1 | tf_op jit(solution)/shard_map/place_blocks/pallas_call | solution.py:132
  (23 shorter events, 0.1 us)
Async XLA Ops:
  3.6 23.8 %collective-permute-start.3 = (bf16[2,2,4,16,512]{4,3,2,1,0:T(8,128)(2,1)S(1)}, bf16[2,2,4,16,512]{4,3,2,1,0:T(8,128)(2,1)S(1)}, u32[]{:S(2)}, u32[]{:S(2)}) collective-permute-start(bf16[2,2,4,16,512]{4,3,2,1,0:T(8,128)(2,1)S(1)} %get-tuple-element.46), channel_id=1, source_target_pairs={{0,12},{4,8},{8,4},{12,0},{16,28},{20,24},{24,20},{28,16},{1,13},{... | collective-permute-start | bytes 786440 | tf_op jit(solution)/shard_map/ppermute | solution.py:657
  7.7 22.9 %collective-permute-start.4 = (bf16[2,2,4,16,512]{4,3,2,1,0:T(8,128)(2,1)S(1)}, bf16[2,2,4,16,512]{4,3,2,1,0:T(8,128)(2,1)S(1)}, u32[]{:S(2)}, u32[]{:S(2)}) collective-permute-start(bf16[2,2,4,16,512]{4,3,2,1,0:T(8,128)(2,1)S(1)} %get-tuple-element.47), channel_id=1, source_target_pairs={{0,8},{4,12},{8,0},{12,4},{16,24},{20,28},{24,16},{28,20},{1,9},{5... | collective-permute-start | bytes 786440 | tf_op jit(solution)/shard_map/ppermute | solution.py:657
  8.1 38.9 %collective-permute-start.1 = (bf16[2,2,4,16,512]{4,3,2,1,0:T(8,128)(2,1)S(1)}, bf16[2,2,4,16,512]{4,3,2,1,0:T(8,128)(2,1)S(1)}, u32[]{:S(2)}, u32[]{:S(2)}) collective-permute-start(bf16[2,2,4,16,512]{4,3,2,1,0:T(8,128)(2,1)S(1)} %get-tuple-element.44), channel_id=1, source_target_pairs={{0,24},{4,28},{8,16},{12,20},{16,8},{20,12},{24,0},{28,4},{1,25},{... | collective-permute-start | bytes 786440 | tf_op jit(solution)/shard_map/ppermute | solution.py:657
  11.7 41.4 %collective-permute-start = (bf16[2,2,4,16,512]{4,3,2,1,0:T(8,128)(2,1)}, bf16[2,2,4,16,512]{4,3,2,1,0:T(8,128)(2,1)S(1)}, u32[]{:S(2)}, u32[]{:S(2)}) collective-permute-start(bf16[2,2,4,16,512]{4,3,2,1,0:T(8,128)(2,1)} %get-tuple-element.35.rest_0_), channel_id=1, source_target_pairs={{0,28},{4,24},{8,20},{12,16},{16,12},{20,8},{24,4},{28,0},{1,29},{... | collective-permute-start | bytes 786440 | tf_op jit(solution)/shard_map/ppermute | solution.py:657
  11.8 3.6 %copy-start.2 = (f32[2,512,128]{2,1,0:T(8,128)S(1)}, f32[2,512,128]{2,1,0:T(8,128)}, u32[]{:S(2)}) copy-start(f32[2,512,128]{2,1,0:T(8,128)} %constant.5.clone.steps) | copy-start | bytes 1572868
  11.8 3.7 %copy-start.3 = (bf16[2,512]{1,0:T(2,128)(2,1)S(1)}, bf16[2,512]{1,0:T(2,128)(2,1)}, u32[]{:S(2)}) copy-start(bf16[2,512]{1,0:T(2,128)(2,1)} %gain.1) | copy-start | bytes 6148
  11.8 3.7 %copy-start.4 = (f32[1,128]{1,0:T(1,128)S(1)}, f32[1,128]{1,0:T(1,128)}, u32[]{:S(2)}) copy-start(f32[1,128]{1,0:T(1,128)} %constant.4.clone.frequency) | copy-start | bytes 1540
  11.8 41.3 %collective-permute-start.2 = (bf16[2,2,4,16,512]{4,3,2,1,0:T(8,128)(2,1)}, bf16[2,2,4,16,512]{4,3,2,1,0:T(8,128)(2,1)}, u32[]{:S(2)}, u32[]{:S(2)}) collective-permute-start(bf16[2,2,4,16,512]{4,3,2,1,0:T(8,128)(2,1)} %get-tuple-element.45), channel_id=1, source_target_pairs={{0,16},{4,20},{8,24},{12,28},{16,0},{20,4},{24,8},{28,12},{1,17},{... | collective-permute-start | bytes 786440 | tf_op jit(solution)/shard_map/ppermute | solution.py:657
  27.5 28.5 %collective-permute-start.5 = (bf16[2,2,4,16,512]{4,3,2,1,0:T(8,128)(2,1)}, bf16[2,2,4,16,512]{4,3,2,1,0:T(8,128)(2,1)}, u32[]{:S(2)}, u32[]{:S(2)}) collective-permute-start(bf16[2,2,4,16,512]{4,3,2,1,0:T(8,128)(2,1)} %hold.3), channel_id=1, source_target_pairs={{0,20},{4,16},{8,28},{12,24},{16,4},{20,0},{24,12},{28,8},{1,21},{... | collective-permute-start | bytes 786440 | tf_op jit(solution)/shard_map/ppermute | solution.py:657
  30.6 25.4 %collective-permute-start.6 = (bf16[2,2,4,16,512]{4,3,2,1,0:T(8,128)(2,1)}, bf16[2,2,4,16,512]{4,3,2,1,0:T(8,128)(2,1)}, u32[]{:S(2)}, u32[]{:S(2)}) collective-permute-start(bf16[2,2,4,16,512]{4,3,2,1,0:T(8,128)(2,1)} %hold.4), channel_id=1, source_target_pairs={{0,4},{4,0},{8,12},{12,8},{16,20},{20,16},{24,28},{28,24},{1,5},{5... | collective-permute-start | bytes 786440 | tf_op jit(solution)/shard_map/ppermute | solution.py:657
  47.0 9.0 %copy-start = (bf16[8,2,2,4,16,512]{5,4,3,2,1,0:T(8,128)(2,1)S(1)}, bf16[8,2,2,4,16,512]{5,4,3,2,1,0:T(8,128)(2,1)}, u32[]{:S(2)}) copy-start(bf16[8,2,2,4,16,512]{5,4,3,2,1,0:T(8,128)(2,1)} %hold.5.rest_8_.rest_9_) | copy-start | bytes 6291460
  47.0 9.0 %copy-start.1 = (bf16[2,2,4,16,512]{4,3,2,1,0:T(8,128)(2,1)S(1)}, bf16[2,2,4,16,512]{4,3,2,1,0:T(8,128)(2,1)}, u32[]{:S(2)}) copy-start(bf16[2,2,4,16,512]{4,3,2,1,0:T(8,128)(2,1)} %get-tuple-element.36.rest_0_.rest_5_) | copy-start | bytes 786436
  47.0 54.9 %all-to-all-start = ((bf16[8,2,2,4,16,512]{5,4,3,2,1,0:T(8,128)(2,1)}), bf16[8,2,2,4,16,512]{5,4,3,2,1,0:T(8,128)(2,1)}, u32[]{:S(2)}, u32[]{:S(2)}) async-start(bf16[8,2,2,4,16,512]{5,4,3,2,1,0:T(8,128)(2,1)} %hold.5.rest_8_.rest_9_), calls=%async_computation | async-start | bytes 4194304 | tf_op jit(solution)/shard_map/all_to_all | solution.py:696
  62.3 1.6 %collective-permute-start.8 = (bf16[256,512]{1,0:T(8,128)(2,1)S(1)}, bf16[256,512]{1,0:T(8,128)(2,1)S(1)}, u32[]{:S(2)}, u32[]{:S(2)}) collective-permute-start(bf16[256,512]{1,0:T(8,128)(2,1)S(1)} %get-tuple-element.54), channel_id=1, source_target_pairs={{0,1},{1,0},{2,3},{3,2},{4,5},{5,4},{6,7},{7,6},{8,9},{9,8},{10,11... | collective-permute-start | bytes 786440 | tf_op jit(solution)/shard_map/ppermute | solution.py:657
  62.4 1.9 %collective-permute-start.9 = (bf16[256,512]{1,0:T(8,128)(2,1)S(1)}, bf16[256,512]{1,0:T(8,128)(2,1)S(1)}, u32[]{:S(2)}, u32[]{:S(2)}) collective-permute-start(bf16[256,512]{1,0:T(8,128)(2,1)S(1)} %get-tuple-element.55), channel_id=1, source_target_pairs={{0,1},{1,0},{2,3},{3,2},{4,5},{5,4},{6,7},{7,6},{8,9},{9,8},{10,11... | collective-permute-start | bytes 786440 | tf_op jit(solution)/shard_map/ppermute | solution.py:657
  64.4 14.0 %collective-permute-start.10 = (bf16[512,512]{1,0:T(8,128)(2,1)S(1)}, bf16[512,512]{1,0:T(8,128)(2,1)S(1)}, u32[]{:S(2)}, u32[]{:S(2)}) collective-permute-start(bf16[512,512]{1,0:T(8,128)(2,1)S(1)} %add_terms.2.rest_10_), channel_id=1, source_target_pairs={{0,2},{1,3},{2,0},{3,1},{4,6},{5,7},{6,4},{7,5},{8,10},{9,11},{10,... | collective-permute-start | bytes 1572872 | tf_op jit(solution)/shard_map/ppermute | solution.py:657
  71.4 5.9 %collective-permute-start.12 = (bf16[256,512]{1,0:T(8,128)(2,1)S(1)}, bf16[256,512]{1,0:T(8,128)(2,1)S(1)}, u32[]{:S(2)}, u32[]{:S(2)}) collective-permute-start(bf16[256,512]{1,0:T(8,128)(2,1)S(1)} %get-tuple-element.62), channel_id=1, source_target_pairs={{0,1},{1,0},{2,3},{3,2},{4,5},{5,4},{6,7},{7,6},{8,9},{9,8},{10,11... | collective-permute-start | bytes 786440 | tf_op jit(solution)/shard_map/ppermute | solution.py:657
  71.5 5.8 %collective-permute-start.13 = (bf16[256,512]{1,0:T(8,128)(2,1)S(1)}, bf16[256,512]{1,0:T(8,128)(2,1)S(1)}, u32[]{:S(2)}, u32[]{:S(2)}) collective-permute-start(bf16[256,512]{1,0:T(8,128)(2,1)S(1)} %get-tuple-element.63), channel_id=1, source_target_pairs={{0,1},{1,0},{2,3},{3,2},{4,5},{5,4},{6,7},{7,6},{8,9},{9,8},{10,11... | collective-permute-start | bytes 786440 | tf_op jit(solution)/shard_map/ppermute | solution.py:657
  74.3 5.8 %collective-permute-start.7 = (bf16[512,512]{1,0:T(8,128)(2,1)S(1)}, bf16[512,512]{1,0:T(8,128)(2,1)S(1)}, u32[]{:S(2)}, u32[]{:S(2)}) collective-permute-start(bf16[512,512]{1,0:T(8,128)(2,1)S(1)} %get-tuple-element.52), channel_id=1, source_target_pairs={{0,1},{1,0},{2,3},{3,2},{4,5},{5,4},{6,7},{7,6},{8,9},{9,8},{10,11... | collective-permute-start | bytes 1572872 | tf_op jit(solution)/shard_map/ppermute | solution.py:657
  76.7 3.7 %collective-permute-start.11 = (bf16[512,512]{1,0:T(8,128)(2,1)S(1)}, bf16[512,512]{1,0:T(8,128)(2,1)S(1)}, u32[]{:S(2)}, u32[]{:S(2)}) collective-permute-start(bf16[512,512]{1,0:T(8,128)(2,1)S(1)} %get-tuple-element.60), channel_id=1, source_target_pairs={{0,1},{1,0},{2,3},{3,2},{4,5},{5,4},{6,7},{7,6},{8,9},{9,8},{10,11... | collective-permute-start | bytes 1572872 | tf_op jit(solution)/shard_map/ppermute | solution.py:657
  78.5 15.6 %copy-start.5 = (bf16[512]{0:T(512)(128)(2,1)S(1)}, bf16[512]{0:T(512)(128)(2,1)}, u32[]{:S(2)}) copy-start(bf16[512]{0:T(512)(128)(2,1)} %param.15) | copy-start | bytes 3076
  78.6 13.3 %collective-permute-start.14 = (bf16[512,512]{1,0:T(8,128)(2,1)S(1)}, bf16[512,512]{1,0:T(8,128)(2,1)S(1)}, u32[]{:S(2)}, u32[]{:S(2)}) collective-permute-start(bf16[512,512]{1,0:T(8,128)(2,1)S(1)} %add_terms.3), channel_id=1, source_target_pairs={{0,2},{1,3},{2,0},{3,1},{4,6},{5,7},{6,4},{7,5},{8,10},{9,11},{10,... | collective-permute-start | bytes 1572872 | tf_op jit(solution)/shard_map/ppermute | solution.py:657
  92.2 3.2 %collective-permute-start.15 = (f32[8,512]{1,0:T(8,128)S(1)}, f32[8,512]{1,0:T(8,128)S(1)}, u32[]{:S(2)}, u32[]{:S(2)}) collective-permute-start(f32[8,512]{1,0:T(8,128)S(1)} %get-tuple-element.64.rest_0_), channel_id=1, source_target_pairs={{0,1},{1,0},{2,3},{3,2},{4,5},{5,4},{6,7},{7,6},{8,9},{9,8},{10,11... | collective-permute-start | bytes 49160 | tf_op jit(solution)/shard_map/ppermute | solution.py:657
  92.3 3.8 %collective-permute-start.16 = (f32[8,512]{1,0:T(8,128)S(1)}, f32[8,512]{1,0:T(8,128)S(1)}, u32[]{:S(2)}, u32[]{:S(2)}) collective-permute-start(f32[8,512]{1,0:T(8,128)S(1)} %get-tuple-element.64.rest_0_), channel_id=1, source_target_pairs={{0,2},{1,3},{2,0},{3,1},{4,6},{5,7},{6,4},{7,5},{8,10},{9,11},{10,... | collective-permute-start | bytes 49160 | tf_op jit(solution)/shard_map/ppermute | solution.py:657
  93.8 3.2 %collective-permute-start.17 = (f32[8,512]{1,0:T(8,128)S(1)}, f32[8,512]{1,0:T(8,128)S(1)}, u32[]{:S(2)}, u32[]{:S(2)}) collective-permute-start(f32[8,512]{1,0:T(8,128)S(1)} %get-tuple-element.64.rest_0_), channel_id=1, source_target_pairs={{0,3},{1,2},{2,1},{3,0},{4,7},{5,6},{6,5},{7,4},{8,11},{9,10},{10,... | collective-permute-start | bytes 49160 | tf_op jit(solution)/shard_map/ppermute | solution.py:657

commit v8 on v7

--- a/solution.py
+++ b/solution.py
@@ -723,7 +723,7 @@
         if p == 0:
             residual = own_columns(span_in, part_width, row_squares[0])
     row_squares = row_squares + [
-        permuted(row_squares[0], "tensor", at) for at in range(1, tensor_count)
+        permuted(row_squares[0], "tensor", at) for at in range(tensor_count - 1, 0, -1)
     ]
     layer_out = finish(full_width, residual, totals, row_squares, post_gain)
 

time: 105 us -> 105 us (level)
  no operation moved by 1% of the time
where the time goes in v8:
time: 105 us
  Pallas kernels  50.3 us (48%)
  starting transfers between devices  25.5 us (24%)
  waiting for transfers between devices  22.2 us (21%)
  blocking collectives  5.41 us (5%)
    ppermute x18, starting transfers between devices, permuted(): return lax.ppermute(value, axis, [(i, i ^ offset) for i in range(size)])  19.4 us
    ppermute x18, waiting for transfers between devices, permuted(): return lax.ppermute(value, axis, [(i, i ^ offset) for i in range(size)])  17.6 us
    pallas_call x1, Pallas kernels, project(): pl.pallas_call(functools.partial(project_body, per_device, block, len(aft...  12 us
    pallas_call x2, Pallas kernels, attend_old(): pl.pallas_call(functools.partial(attend_old_body, which, span, offsets, q...  11.7 us
    pallas_call x3, Pallas kernels, gather(): pl.pallas_call(functools.partial(gather_body, wanted, staged, count, per_...  9.44 us
    pallas_call x1, Pallas kernels, attend_new(): pl.pallas_call(functools.partial(attend_new_body, full_width, span, q_blo...  6.76 us
    all_to_all x1, starting transfers between devices, on_device(): received_rest = lax.all_to_all(sent_rest, 'req', 0, 0)  6.06 us
    all_gather x1, blocking collectives, on_device(): squares = lax.all_gather(squares, 'tensor')  5.41 us
  transfers between devices with their start and end apart: 19, of which 8 were waited for; matrix products, arithmetic and copies ran while one was open for 0% of the time, Pallas kernels for 43%

profile of v8, /device:TPU:0, one launch (start us, length us, event | category | flops | bytes accessed | tf_op | source)
XLA Modules:
  0.0 104.5 jit_solution(13216270713692747573)
XLA Ops:
  0.6 3.0 %gather_blocks.3 = (bf16[2,2,4,16,512]{4,3,2,1,0:T(8,128)(2,1)}, bf16[2,2,4,16,512]{4,3,2,1,0:T(8,128)(2,1)S(1)}, bf16[2,2,4,16,512]{4,3,2,1,0:T(8,128)(2,1)}, b...) custom-call(s32[16,32]{1,0:T(8,128)} %table_all.5, s32[16]{0:T(128)} %order_all.5, ...), custom_call_target="tpu_custom_call" | custom-call | flops 1 | bytes 1 | tf_op jit(solution)/shard_map/gather_blocks/pallas_call | solution.py:97
  3.6 4.0 %collective-permute-start.3 = (bf16[2,2,4,16,512]{4,3,2,1,0:T(8,128)(2,1)S(1)}, bf16[2,2,4,16,512]{4,3,2,1,0:T(8,128)(2,1)S(1)}, u32[]{:S(2)}, u32[]{:S(2)}) collective-permute-start(bf16[2,2,4,16,512]{4,3,2,1,0:T(8,128)(2,1)S(1)} %get-tuple-element.46), channel_id=1, source_target_pairs={{0,12},{4,8},{8,4},{12,0},{16,28},{20,24},{24,20},{28,16},{1,13},{... | collective-permute-start | bytes 786440 | tf_op jit(solution)/shard_map/ppermute | solution.py:657
  7.7 0.4 collective-permute-start.4
  8.1 3.6 %collective-permute-start.1 = (bf16[2,2,4,16,512]{4,3,2,1,0:T(8,128)(2,1)S(1)}, bf16[2,2,4,16,512]{4,3,2,1,0:T(8,128)(2,1)S(1)}, u32[]{:S(2)}, u32[]{:S(2)}) collective-permute-start(bf16[2,2,4,16,512]{4,3,2,1,0:T(8,128)(2,1)S(1)} %get-tuple-element.44), channel_id=1, source_target_pairs={{0,24},{4,28},{8,16},{12,20},{16,8},{20,12},{24,0},{28,4},{1,25},{... | collective-permute-start | bytes 786440 | tf_op jit(solution)/shard_map/ppermute | solution.py:657
  11.7 0.0 collective-permute-start
  11.7 0.9 collective-permute-start.2
  12.7 2.7 %gather_blocks.4 = (bf16[2,2,4,16,512]{4,3,2,1,0:T(8,128)(2,1)}, bf16[2,2,4,16,512]{4,3,2,1,0:T(8,128)(2,1)}, bf16[2,2,4,16,512]{4,3,2,1,0:T(8,128)(2,1)}) custom-call(s32[16,32]{1,0:T(8,128)} %table_all.5, s32[16]{0:T(128)} %order_all.5, bf16[4,64,16,512]{3,2,1,0:T(8,128)(2,1)} %pool.5, bf16[2,2,4,16,512]{4,3,2,1,0:T(8,128)(2,1)} %get-tuple-element.35.rest_0_), custom_call_target="tpu_custom_call" | custom-call | flops 1 | bytes 1 | tf_op jit(solution)/shard_map/gather_blocks/pallas_call | solution.py:97
  15.4 12.0 %project_qkv.1 = (f32[1024,512]{1,0:T(8,128)}, f32[1024,512]{1,0:T(8,128)}, bf16[1024,512]{1,0:T(8,128)(2,1)}, f32[8,1024]{1,0:T(8,128)S(1)}) custom-call(s32[16]{0:T(128)} %order_all.5, s32[16]{0:T(128)} %lengths.1, f32[1,128]{1,0:T(1,128)S(1)} %copy-done.4, f32[2,512,128]{2,1,0:T(8,128)S(1)} %copy-done.2, bf16[2,512]{1,0:T(2,128)(2,1)S(1)} %copy-done.3, ...), custom_call_target="tpu_custom_call" | custom-call | flops 1 | bytes 1 | tf_op jit(solution)/shard_map/project_qkv/pallas_call | solution.py:262
  27.4 0.0 collective-permute-done.3.refs_2_.refs_3_.rest_3_
  27.5 3.2 %collective-permute-start.5 = (bf16[2,2,4,16,512]{4,3,2,1,0:T(8,128)(2,1)}, bf16[2,2,4,16,512]{4,3,2,1,0:T(8,128)(2,1)}, u32[]{:S(2)}, u32[]{:S(2)}) collective-permute-start(bf16[2,2,4,16,512]{4,3,2,1,0:T(8,128)(2,1)} %hold.3), channel_id=1, source_target_pairs={{0,20},{4,16},{8,28},{12,24},{16,4},{20,0},{24,12},{28,8},{1,21},{... | collective-permute-start | bytes 786440 | tf_op jit(solution)/shard_map/ppermute | solution.py:657
  30.6 0.4 collective-permute-start.6
  31.0 5.4 %all-gather = f32[32,1024]{1,0:T(8,128)S(1)} all-gather(f32[8,1024]{1,0:T(8,128)S(1)} %get-tuple-element.37.refs_1_), channel_id=2, replica_groups=mesh['req'=8,'tensor'=4] {'tensor'}, dimensions={0}, use_global_device_ids=true | all-gather | bytes 163840 | tf_op jit(solution)/shard_map/all_gather | solution.py:686
  36.5 6.8 %attend_new.1 = (bf16[1024,512]{1,0:T(8,128)(2,1)}, f32[2,512,512]{2,1,0:T(8,128)}, f32[16,1024]{1,0:T(8,128)S(1)}) custom-call(f32[4,8,1024]{2,1,0:T(8,128)S(1)} %bitcast.3, f32[1024,512]{1,0:T(8,128)} %get-tuple-element.38.rest_0_, f32[1024,512]{1,0:T(8,128)} %get-tuple-element.39.rest_1_, bf16[1024,512]{1,0:T(8,128)(2,1)} %get-tuple-element.40.rest_2_), custom_call_target="tpu_custom_call" | custom-call | flops 1 | bytes 1 | tf_op jit(solution)/shard_map/attend_new/pallas_call | solution.py:376
  43.2 3.8 %gather_blocks.5.refs_0_ = bf16[8,2,2,4,16,512]{5,4,3,2,1,0:T(8,128)(2,1)} custom-call(s32[16,32]{1,0:T(8,128)} %table_all.5, s32[16]{0:T(128)} %order_all.5, bf16[4,64,16,512]{3,2,1,0:T(8,128)(2,1)} %pool.5, f32[16,1024]{1,0:T(8,128)S(1)} %get-tuple-element.41.rest_0_.refs_1_.state), custom_call_target="tpu_custom_call" | custom-call | flops 1 | bytes 1 | tf_op jit(solution)/shard_map/gather_blocks/pallas_call | solution.py:97
  47.0 6.1 %all-to-all-start = ((bf16[8,2,2,4,16,512]{5,4,3,2,1,0:T(8,128)(2,1)}), bf16[8,2,2,4,16,512]{5,4,3,2,1,0:T(8,128)(2,1)}, u32[]{:S(2)}, u32[]{:S(2)}) async-start(bf16[8,2,2,4,16,512]{5,4,3,2,1,0:T(8,128)(2,1)} %hold.5.rest_8_.rest_9_), calls=%async_computation | async-start | bytes 4194304 | tf_op jit(solution)/shard_map/all_to_all | solution.py:696
  53.1 0.0 collective-permute-done.rest_0_
  53.1 2.9 %collective-permute-done.5.rest_6_ = bf16[2,2,4,16,512]{4,3,2,1,0:T(8,128)(2,1)} collective-permute-done((bf16[2,2,4,16,512]{4,3,2,1,0:T(8,128)(2,1)}, bf16[2,2,4,16,512]{4,3,2,1,0:T(8,128)(2,1)}, u32[]{:S(2)}, u32[]{:S(2)}) %collective-permute-start.5) | collective-permute-done | bytes 262176 | tf_op jit(solution)/shard_map/ppermute | solution.py:657
  56.0 6.3 %attend_old.2 = (bf16[4,2,4,8,16,512]{5,4,3,2,1,0:T(8,128)(2,1)}, bf16[512,512]{1,0:T(8,128)(2,1)S(1)}, bf16[512,512]{1,0:T(8,128)(2,1)S(1)}, bf16[256,512]{1,0:T(8,128)(2,1)S(1)}, bf16[256,512]{1,0:T(8,128)(2,1)S(1)}) custom-call(f32[16,1024]{1,0:T(8,128)S(1)} %get-tuple-element.41.rest_0_.refs_1_.state, bf16[1024,512]{1,0:T(8,128)(2,1)} %get-tuple-element.42.q_all, ...), custom_call_target="tpu_custom_call" | custom-call | flops 999999995904 | bytes 999999995904 | tf_op jit(solution)/shard_map/attend_old/pallas_call | solution.py:480
  62.3 0.1 collective-permute-start.8
  62.4 0.5 collective-permute-start.9
  62.9 1.0 collective-permute-done.8.upper
  63.9 0.4 collective-permute-done.9.lower
  64.3 0.1 add_terms.2.rest_10_
  64.4 1.6 %collective-permute-start.10 = (bf16[512,512]{1,0:T(8,128)(2,1)S(1)}, bf16[512,512]{1,0:T(8,128)(2,1)S(1)}, u32[]{:S(2)}, u32[]{:S(2)}) collective-permute-start(bf16[512,512]{1,0:T(8,128)(2,1)S(1)} %add_terms.2.rest_10_), channel_id=1, source_target_pairs={{0,2},{1,3},{2,0},{3,1},{4,6},{5,7},{6,4},{7,5},{8,10},{9,11},{10,... | collective-permute-start | bytes 1572872 | tf_op jit(solution)/shard_map/ppermute | solution.py:657
  65.9 5.4 %attend_old.3 = (bf16[4,2,4,8,16,512]{5,4,3,2,1,0:T(8,128)(2,1)}, bf16[512,512]{1,0:T(8,128)(2,1)S(1)}, bf16[512,512]{1,0:T(8,128)(2,1)S(1)}, bf16[256,512]{1,0:T(8,128)(2,1)S(1)}, bf16[256,512]{1,0:T(8,128)(2,1)S(1)}) custom-call(f32[16,1024]{1,0:T(8,128)S(1)} %get-tuple-element.41.rest_0_.refs_1_.state, ...), custom_call_target="tpu_custom_call", output_to_operand_aliasing={{0}: (12, {})} | custom-call | flops 1 | bytes 1 | tf_op jit(solution)/shard_map/attend_old/pallas_call | solution.py:480
  71.4 0.1 collective-permute-start.12
  71.5 0.5 collective-permute-start.13
  72.0 2.3 %own_terms.2 = (bf16[512,512]{1,0:T(8,128)(2,1)S(1)}, bf16[512,512]{1,0:T(8,128)(2,1)S(1)}) custom-call(bf16[512,512]{1,0:T(8,128)(2,1)S(1)} %get-tuple-element.50.attended, bf16[512,2048]{1,0:T(8,128)(2,1)} %w.9), custom_call_target="tpu_custom_call" | custom-call | flops 1 | bytes 1 | tf_op jit(solution)/shard_map/own_terms/pallas_call | solution.py:519
  74.3 0.1 collective-permute-start.7
  74.4 2.3 %own_terms.3 = (bf16[512,512]{1,0:T(8,128)(2,1)S(1)}, bf16[512,512]{1,0:T(8,128)(2,1)S(1)}) custom-call(bf16[512,512]{1,0:T(8,128)(2,1)S(1)} %get-tuple-element.58.attended, bf16[512,2048]{1,0:T(8,128)(2,1)} %w.9), custom_call_target="tpu_custom_call" | custom-call | flops 1 | bytes 1 | tf_op jit(solution)/shard_map/own_terms/pallas_call | solution.py:519
  76.7 0.5 collective-permute-start.11
  77.2 0.0 collective-permute-done.12.upper
  77.2 1.2 %collective-permute-done.10.third.rest_0_ = bf16[512,512]{1,0:T(8,128)(2,1)S(1)} collective-permute-done((bf16[512,512]{1,0:T(8,128)(2,1)S(1)}, bf16[512,512]{1,0:T(8,128)(2,1)S(1)}, u32[]{:S(2)}, u32[]{:S(2)}) %collective-permute-start.10) | collective-permute-done | bytes 524320 | tf_op jit(solution)/shard_map/ppermute | solution.py:657
  78.4 0.1 add_terms.3
  78.5 0.0 copy-start.5
  78.6 1.6 %collective-permute-start.14 = (bf16[512,512]{1,0:T(8,128)(2,1)S(1)}, bf16[512,512]{1,0:T(8,128)(2,1)S(1)}, u32[]{:S(2)}, u32[]{:S(2)}) collective-permute-start(bf16[512,512]{1,0:T(8,128)(2,1)S(1)} %add_terms.3), channel_id=1, source_target_pairs={{0,2},{1,3},{2,0},{3,1},{4,6},{5,7},{6,4},{7,5},{8,10},{9,11},{10,... | collective-permute-start | bytes 1572872 | tf_op jit(solution)/shard_map/ppermute | solution.py:657
  80.1 0.3 total_terms.2
  80.4 11.4 %collective-permute-done.14.third = bf16[512,512]{1,0:T(8,128)(2,1)S(1)} collective-permute-done((bf16[512,512]{1,0:T(8,128)(2,1)S(1)}, bf16[512,512]{1,0:T(8,128)(2,1)S(1)}, u32[]{:S(2)}, u32[]{:S(2)}) %collective-permute-start.14) | collective-permute-done | bytes 524320 | tf_op jit(solution)/shard_map/ppermute | solution.py:657
  91.9 0.3 total_terms.3
  92.2 0.1 collective-permute-start.15
  92.3 1.6 %collective-permute-start.16 = (f32[8,512]{1,0:T(8,128)S(1)}, f32[8,512]{1,0:T(8,128)S(1)}, u32[]{:S(2)}, u32[]{:S(2)}) collective-permute-start(f32[8,512]{1,0:T(8,128)S(1)} %get-tuple-element.64.rest_0_), channel_id=1, source_target_pairs={{0,2},{1,3},{2,0},{3,1},{4,6},{5,7},{6,4},{7,5},{8,10},{9,11},{10,... | collective-permute-start | bytes 49160 | tf_op jit(solution)/shard_map/ppermute | solution.py:657
  93.8 0.3 collective-permute-start.17
  94.1 1.2 %own_columns.1.residual = bf16[2,512,512]{2,1,0:T(8,128)(2,1)S(1)} custom-call(bf16[2,512,2048]{2,1,0:T(8,128)(2,1)} %residual.1, f32[8,512]{1,0:T(8,128)S(1)} %get-tuple-element.56.after.rest_0_), custom_call_target="tpu_custom_call" | custom-call | flops 1 | bytes 1 | tf_op jit(solution)/shard_map/own_columns/pallas_call | solution.py:602
  95.3 0.2 collective-permute-done.15.rest_1_
  95.5 0.5 collective-permute-done.16.rest_2_
  96.1 1.3 %finish_layer.1 = bf16[2,512,512]{2,1,0:T(8,128)(2,1)} custom-call(bf16[2,512,512]{2,1,0:T(8,128)(2,1)S(1)} %own_columns.1.residual, bf16[1,512]{1,0:T(2,128)(2,1)S(1)} %reshape.14.gain, f32[8,512]{1,0:T(8,128)S(1)} %get-tuple-element.64.rest_0_, f32[8,512]{1,0:T(8,128)S(1)} %collective-permute-done.15.rest_1_, ...), custom_call_target="tpu_custom_call" | custom-call | flops 1 | bytes 1 | tf_op jit(solution)/shard_map/finish_layer/pallas_call | solution.py:640
  97.3 4.6 %all-to-all-done.received = bf16[8,2,2,4,16,512]{5,4,3,2,1,0:T(8,128)(2,1)} async-done(((bf16[8,2,2,4,16,512]{5,4,3,2,1,0:T(8,128)(2,1)}), bf16[8,2,2,4,16,512]{5,4,3,2,1,0:T(8,128)(2,1)}, u32[]{:S(2)}, u32[]{:S(2)}) %all-to-all-start) | async-done | bytes 2097184 | tf_op jit(solution)/shard_map/all_to_all | solution.py:696
  101.9 2.4 %place_blocks.1 = bf16[4,2,4,8,16,512]{5,4,3,2,1,0:T(8,128)(2,1)} custom-call(bf16[4,2,4,8,16,512]{5,4,3,2,1,0:T(8,128)(2,1)} %get-tuple-element.67.filled, bf16[8,2,2,4,16,512]{5,4,3,2,1,0:T(8,128)(2,1)} %all-to-all-done.received), custom_call_target="tpu_custom_call", output_to_operand_aliasing={{}: (0, {})} | custom-call | flops 1 | bytes 1 | tf_op jit(solution)/shard_map/place_blocks/pallas_call | solution.py:132
  (23 shorter events, 0.1 us)
Async XLA Ops:
  3.6 23.8 %collective-permute-start.3 = (bf16[2,2,4,16,512]{4,3,2,1,0:T(8,128)(2,1)S(1)}, bf16[2,2,4,16,512]{4,3,2,1,0:T(8,128)(2,1)S(1)}, u32[]{:S(2)}, u32[]{:S(2)}) collective-permute-start(bf16[2,2,4,16,512]{4,3,2,1,0:T(8,128)(2,1)S(1)} %get-tuple-element.46), channel_id=1, source_target_pairs={{0,12},{4,8},{8,4},{12,0},{16,28},{20,24},{24,20},{28,16},{1,13},{... | collective-permute-start | bytes 786440 | tf_op jit(solution)/shard_map/ppermute | solution.py:657
  7.7 22.9 %collective-permute-start.4 = (bf16[2,2,4,16,512]{4,3,2,1,0:T(8,128)(2,1)S(1)}, bf16[2,2,4,16,512]{4,3,2,1,0:T(8,128)(2,1)S(1)}, u32[]{:S(2)}, u32[]{:S(2)}) collective-permute-start(bf16[2,2,4,16,512]{4,3,2,1,0:T(8,128)(2,1)S(1)} %get-tuple-element.47), channel_id=1, source_target_pairs={{0,8},{4,12},{8,0},{12,4},{16,24},{20,28},{24,16},{28,20},{1,9},{5... | collective-permute-start | bytes 786440 | tf_op jit(solution)/shard_map/ppermute | solution.py:657
  8.1 38.8 %collective-permute-start.1 = (bf16[2,2,4,16,512]{4,3,2,1,0:T(8,128)(2,1)S(1)}, bf16[2,2,4,16,512]{4,3,2,1,0:T(8,128)(2,1)S(1)}, u32[]{:S(2)}, u32[]{:S(2)}) collective-permute-start(bf16[2,2,4,16,512]{4,3,2,1,0:T(8,128)(2,1)S(1)} %get-tuple-element.44), channel_id=1, source_target_pairs={{0,24},{4,28},{8,16},{12,20},{16,8},{20,12},{24,0},{28,4},{1,25},{... | collective-permute-start | bytes 786440 | tf_op jit(solution)/shard_map/ppermute | solution.py:657
  11.7 41.4 %collective-permute-start = (bf16[2,2,4,16,512]{4,3,2,1,0:T(8,128)(2,1)}, bf16[2,2,4,16,512]{4,3,2,1,0:T(8,128)(2,1)S(1)}, u32[]{:S(2)}, u32[]{:S(2)}) collective-permute-start(bf16[2,2,4,16,512]{4,3,2,1,0:T(8,128)(2,1)} %get-tuple-element.35.rest_0_), channel_id=1, source_target_pairs={{0,28},{4,24},{8,20},{12,16},{16,12},{20,8},{24,4},{28,0},{1,29},{... | collective-permute-start | bytes 786440 | tf_op jit(solution)/shard_map/ppermute | solution.py:657
  11.7 3.7 %copy-start.2 = (f32[2,512,128]{2,1,0:T(8,128)S(1)}, f32[2,512,128]{2,1,0:T(8,128)}, u32[]{:S(2)}) copy-start(f32[2,512,128]{2,1,0:T(8,128)} %constant.5.clone.steps) | copy-start | bytes 1572868
  11.7 3.7 %copy-start.3 = (bf16[2,512]{1,0:T(2,128)(2,1)S(1)}, bf16[2,512]{1,0:T(2,128)(2,1)}, u32[]{:S(2)}) copy-start(bf16[2,512]{1,0:T(2,128)(2,1)} %gain.1) | copy-start | bytes 6148
  11.7 3.7 %copy-start.4 = (f32[1,128]{1,0:T(1,128)S(1)}, f32[1,128]{1,0:T(1,128)}, u32[]{:S(2)}) copy-start(f32[1,128]{1,0:T(1,128)} %constant.4.clone.frequency) | copy-start | bytes 1540
  11.7 41.3 %collective-permute-start.2 = (bf16[2,2,4,16,512]{4,3,2,1,0:T(8,128)(2,1)}, bf16[2,2,4,16,512]{4,3,2,1,0:T(8,128)(2,1)}, u32[]{:S(2)}, u32[]{:S(2)}) collective-permute-start(bf16[2,2,4,16,512]{4,3,2,1,0:T(8,128)(2,1)} %get-tuple-element.45), channel_id=1, source_target_pairs={{0,16},{4,20},{8,24},{12,28},{16,0},{20,4},{24,8},{28,12},{1,17},{... | collective-permute-start | bytes 786440 | tf_op jit(solution)/shard_map/ppermute | solution.py:657
  27.5 28.5 %collective-permute-start.5 = (bf16[2,2,4,16,512]{4,3,2,1,0:T(8,128)(2,1)}, bf16[2,2,4,16,512]{4,3,2,1,0:T(8,128)(2,1)}, u32[]{:S(2)}, u32[]{:S(2)}) collective-permute-start(bf16[2,2,4,16,512]{4,3,2,1,0:T(8,128)(2,1)} %hold.3), channel_id=1, source_target_pairs={{0,20},{4,16},{8,28},{12,24},{16,4},{20,0},{24,12},{28,8},{1,21},{... | collective-permute-start | bytes 786440 | tf_op jit(solution)/shard_map/ppermute | solution.py:657
  30.6 25.4 %collective-permute-start.6 = (bf16[2,2,4,16,512]{4,3,2,1,0:T(8,128)(2,1)}, bf16[2,2,4,16,512]{4,3,2,1,0:T(8,128)(2,1)}, u32[]{:S(2)}, u32[]{:S(2)}) collective-permute-start(bf16[2,2,4,16,512]{4,3,2,1,0:T(8,128)(2,1)} %hold.4), channel_id=1, source_target_pairs={{0,4},{4,0},{8,12},{12,8},{16,20},{20,16},{24,28},{28,24},{1,5},{5... | collective-permute-start | bytes 786440 | tf_op jit(solution)/shard_map/ppermute | solution.py:657
  47.0 9.0 %copy-start = (bf16[8,2,2,4,16,512]{5,4,3,2,1,0:T(8,128)(2,1)S(1)}, bf16[8,2,2,4,16,512]{5,4,3,2,1,0:T(8,128)(2,1)}, u32[]{:S(2)}) copy-start(bf16[8,2,2,4,16,512]{5,4,3,2,1,0:T(8,128)(2,1)} %hold.5.rest_8_.rest_9_) | copy-start | bytes 6291460
  47.0 9.0 %copy-start.1 = (bf16[2,2,4,16,512]{4,3,2,1,0:T(8,128)(2,1)S(1)}, bf16[2,2,4,16,512]{4,3,2,1,0:T(8,128)(2,1)}, u32[]{:S(2)}) copy-start(bf16[2,2,4,16,512]{4,3,2,1,0:T(8,128)(2,1)} %get-tuple-element.36.rest_0_.rest_5_) | copy-start | bytes 786436
  47.0 54.9 %all-to-all-start = ((bf16[8,2,2,4,16,512]{5,4,3,2,1,0:T(8,128)(2,1)}), bf16[8,2,2,4,16,512]{5,4,3,2,1,0:T(8,128)(2,1)}, u32[]{:S(2)}, u32[]{:S(2)}) async-start(bf16[8,2,2,4,16,512]{5,4,3,2,1,0:T(8,128)(2,1)} %hold.5.rest_8_.rest_9_), calls=%async_computation | async-start | bytes 4194304 | tf_op jit(solution)/shard_map/all_to_all | solution.py:696
  62.3 1.6 %collective-permute-start.8 = (bf16[256,512]{1,0:T(8,128)(2,1)S(1)}, bf16[256,512]{1,0:T(8,128)(2,1)S(1)}, u32[]{:S(2)}, u32[]{:S(2)}) collective-permute-start(bf16[256,512]{1,0:T(8,128)(2,1)S(1)} %get-tuple-element.54), channel_id=1, source_target_pairs={{0,1},{1,0},{2,3},{3,2},{4,5},{5,4},{6,7},{7,6},{8,9},{9,8},{10,11... | collective-permute-start | bytes 786440 | tf_op jit(solution)/shard_map/ppermute | solution.py:657
  62.4 1.9 %collective-permute-start.9 = (bf16[256,512]{1,0:T(8,128)(2,1)S(1)}, bf16[256,512]{1,0:T(8,128)(2,1)S(1)}, u32[]{:S(2)}, u32[]{:S(2)}) collective-permute-start(bf16[256,512]{1,0:T(8,128)(2,1)S(1)} %get-tuple-element.55), channel_id=1, source_target_pairs={{0,1},{1,0},{2,3},{3,2},{4,5},{5,4},{6,7},{7,6},{8,9},{9,8},{10,11... | collective-permute-start | bytes 786440 | tf_op jit(solution)/shard_map/ppermute | solution.py:657
  64.4 14.0 %collective-permute-start.10 = (bf16[512,512]{1,0:T(8,128)(2,1)S(1)}, bf16[512,512]{1,0:T(8,128)(2,1)S(1)}, u32[]{:S(2)}, u32[]{:S(2)}) collective-permute-start(bf16[512,512]{1,0:T(8,128)(2,1)S(1)} %add_terms.2.rest_10_), channel_id=1, source_target_pairs={{0,2},{1,3},{2,0},{3,1},{4,6},{5,7},{6,4},{7,5},{8,10},{9,11},{10,... | collective-permute-start | bytes 1572872 | tf_op jit(solution)/shard_map/ppermute | solution.py:657
  71.4 5.9 %collective-permute-start.12 = (bf16[256,512]{1,0:T(8,128)(2,1)S(1)}, bf16[256,512]{1,0:T(8,128)(2,1)S(1)}, u32[]{:S(2)}, u32[]{:S(2)}) collective-permute-start(bf16[256,512]{1,0:T(8,128)(2,1)S(1)} %get-tuple-element.62), channel_id=1, source_target_pairs={{0,1},{1,0},{2,3},{3,2},{4,5},{5,4},{6,7},{7,6},{8,9},{9,8},{10,11... | collective-permute-start | bytes 786440 | tf_op jit(solution)/shard_map/ppermute | solution.py:657
  71.5 5.8 %collective-permute-start.13 = (bf16[256,512]{1,0:T(8,128)(2,1)S(1)}, bf16[256,512]{1,0:T(8,128)(2,1)S(1)}, u32[]{:S(2)}, u32[]{:S(2)}) collective-permute-start(bf16[256,512]{1,0:T(8,128)(2,1)S(1)} %get-tuple-element.63), channel_id=1, source_target_pairs={{0,1},{1,0},{2,3},{3,2},{4,5},{5,4},{6,7},{7,6},{8,9},{9,8},{10,11... | collective-permute-start | bytes 786440 | tf_op jit(solution)/shard_map/ppermute | solution.py:657
  74.3 5.8 %collective-permute-start.7 = (bf16[512,512]{1,0:T(8,128)(2,1)S(1)}, bf16[512,512]{1,0:T(8,128)(2,1)S(1)}, u32[]{:S(2)}, u32[]{:S(2)}) collective-permute-start(bf16[512,512]{1,0:T(8,128)(2,1)S(1)} %get-tuple-element.52), channel_id=1, source_target_pairs={{0,1},{1,0},{2,3},{3,2},{4,5},{5,4},{6,7},{7,6},{8,9},{9,8},{10,11... | collective-permute-start | bytes 1572872 | tf_op jit(solution)/shard_map/ppermute | solution.py:657
  76.7 3.7 %collective-permute-start.11 = (bf16[512,512]{1,0:T(8,128)(2,1)S(1)}, bf16[512,512]{1,0:T(8,128)(2,1)S(1)}, u32[]{:S(2)}, u32[]{:S(2)}) collective-permute-start(bf16[512,512]{1,0:T(8,128)(2,1)S(1)} %get-tuple-element.60), channel_id=1, source_target_pairs={{0,1},{1,0},{2,3},{3,2},{4,5},{5,4},{6,7},{7,6},{8,9},{9,8},{10,11... | collective-permute-start | bytes 1572872 | tf_op jit(solution)/shard_map/ppermute | solution.py:657
  78.5 15.6 %copy-start.5 = (bf16[512]{0:T(512)(128)(2,1)S(1)}, bf16[512]{0:T(512)(128)(2,1)}, u32[]{:S(2)}) copy-start(bf16[512]{0:T(512)(128)(2,1)} %param.15) | copy-start | bytes 3076
  78.6 13.3 %collective-permute-start.14 = (bf16[512,512]{1,0:T(8,128)(2,1)S(1)}, bf16[512,512]{1,0:T(8,128)(2,1)S(1)}, u32[]{:S(2)}, u32[]{:S(2)}) collective-permute-start(bf16[512,512]{1,0:T(8,128)(2,1)S(1)} %add_terms.3), channel_id=1, source_target_pairs={{0,2},{1,3},{2,0},{3,1},{4,6},{5,7},{6,4},{7,5},{8,10},{9,11},{10,... | collective-permute-start | bytes 1572872 | tf_op jit(solution)/shard_map/ppermute | solution.py:657
  92.2 3.4 %collective-permute-start.15 = (f32[8,512]{1,0:T(8,128)S(1)}, f32[8,512]{1,0:T(8,128)S(1)}, u32[]{:S(2)}, u32[]{:S(2)}) collective-permute-start(f32[8,512]{1,0:T(8,128)S(1)} %get-tuple-element.64.rest_0_), channel_id=1, source_target_pairs={{0,3},{1,2},{2,1},{3,0},{4,7},{5,6},{6,5},{7,4},{8,11},{9,10},{10,... | collective-permute-start | bytes 49160 | tf_op jit(solution)/shard_map/ppermute | solution.py:657
  92.3 3.8 %collective-permute-start.16 = (f32[8,512]{1,0:T(8,128)S(1)}, f32[8,512]{1,0:T(8,128)S(1)}, u32[]{:S(2)}, u32[]{:S(2)}) collective-permute-start(f32[8,512]{1,0:T(8,128)S(1)} %get-tuple-element.64.rest_0_), channel_id=1, source_target_pairs={{0,2},{1,3},{2,0},{3,1},{4,6},{5,7},{6,4},{7,5},{8,10},{9,11},{10,... | collective-permute-start | bytes 49160 | tf_op jit(solution)/shard_map/ppermute | solution.py:657
  93.8 2.2 %collective-permute-start.17 = (f32[8,512]{1,0:T(8,128)S(1)}, f32[8,512]{1,0:T(8,128)S(1)}, u32[]{:S(2)}, u32[]{:S(2)}) collective-permute-start(f32[8,512]{1,0:T(8,128)S(1)} %get-tuple-element.64.rest_0_), channel_id=1, source_target_pairs={{0,1},{1,0},{2,3},{3,2},{4,5},{5,4},{6,7},{7,6},{8,9},{9,8},{10,11... | collective-permute-start | bytes 49160 | tf_op jit(solution)/shard_map/ppermute | solution.py:657
